TPU v7x, 256 devices: a whole 4x4x8 slice. The times are simulated.
256 devices in a mesh: gx: 16 (over x, y), gz: 8 (over z), gy: 2 (over core).
Axes of the slice: x: 4, y: 4, z: 8, core: 2. Of those that a mesh axis runs over, the one named last changes fastest.
Arguments:
- source: float32 [2, 384, 192, 256], P(None, 'gx', 'gz', 'gy'), may hold values from -12 to 20
- iterate: float32 [2, 384, 192, 256], P(None, 'gx', 'gz', 'gy'), may hold values from -3 to 5
- wave_sq: float32 [384, 192, 256], P('gx', 'gz', 'gy'), may hold values from 0.3 to 1.2
- front: int32 [1], replicated, may hold values from 8 to 14
- pml_flags: int32 [16, 8], P('gx', 'gz'), may hold values from 0 to 3
Outputs:
- solution: float32 [2, 384, 192, 256], P(None, 'gx', 'gz', 'gy')
- residual: float32 [2, 384, 192, 256], P(None, 'gx', 'gz', 'gy')
- norm: float32 [1], replicated
Inputs may be any that keep to these rules, and one draw needn't show every extreme that they name: Subdomains whose column and row indices sum to front[0] plus a multiple of 8 relax. `pml_flags`: bit 0 puts an absorbing layer on the subdomain's upper x side, bit 1 on its upper z side.
All inputs are finite; a program needn't handle non-finite values.
Results may differ from a plain program's by a relative error of at most 0.0001.
Values sent between devices are 32-bit elements; how exact they have to be, the bound alone decides.
No kernel may reach another device: no remote copies, remote signals or barrier semaphores. Data moves between devices by JAX's collectives and lax.ppermute only.
A program may use at most 64 MiB of HBM per device.

v0:
```python
import functools

import jax
import jax.numpy as jnp
from jax import lax
from jax.experimental import pallas as pl
from jax.experimental.pallas import tpu as pltpu
from jax.sharding import PartitionSpec as P

BAND = 4
PML = 8
SWEEPS = 10
OMEGA = 0.6
SIGMA = 6.0

CX = 24
CZ = 24
LANES = 128
EXT = CX + BAND
GROUP = 16
HALO = 10
STRIDE = 4
BATCH = 4
PER = EXT // STRIDE

VMEM_LIMIT = 40 * 1024 * 1024

SMEM = pl.BlockSpec(memory_space=pltpu.SMEM)
VMEM = pl.BlockSpec(memory_space=pltpu.VMEM)


def lane_ids():
    return lax.broadcasted_iota(jnp.int32, (8, LANES), 1)


def row_ids():
    return lax.broadcasted_iota(jnp.int32, (8, LANES), 0)


def roll(value, shift):
    if isinstance(shift, int):
        shift = shift % LANES
        if shift == 0:
            return value
    return pltpu.roll(value, shift, 1)


def pair_sum(value):
    return roll(value, 1) + roll(value, -1)


def stencil_parts(centre, across, z_centre, z_across):
    both = across + z_centre
    part = 0.25 * z_across
    near = both + part
    return centre + 0.25 * (near + part), near


def tile_of(fields, bands, corner_tiles, field, plane, tile):
    if tile == 0:
        return corner_tiles[field, plane]
    rows = pl.ds(8 * (tile - 1), 8)
    if plane < BAND:
        return bands[field, plane, rows, :]
    ref, index = fields[field]
    x = plane - BAND
    return ref[x, rows, :] if index is None else ref[index, x, rows, :]


def fill_low_tiles(low, z_band, corner, keep_x, keep_z):
    keep_both = keep_x * keep_z
    low[...] = jnp.zeros_like(low)
    for field in range(5):
        for plane in range(EXT):
            if plane < BAND:
                low[field, plane, pl.ds(4, 4), :] = corner[field, plane] * keep_both
            else:
                low[field, plane, pl.ds(4, 4), :] = z_band[field, plane - BAND] * keep_z


def halo_kernel(info, keep, iterate, source, wave, x_band, z_band, corner, out, low):
    half = info[0]
    active = info[1]

    @pl.when(active == 1)
    def _():
        keep_x = keep[0]
        fill_low_tiles(low, z_band, corner, keep_x, keep[1])
        fields = [(iterate, 0), (iterate, 1), (source, 0), (source, 1), (wave, None)]
        lanes = lane_ids()
        place = lanes % GROUP
        least = (GROUP - HALO) * (1 - half)
        wanted = (place >= least) & (place < least + HALO)
        masks = [wanted & (lanes // GROUP == j) for j in range(PER)]
        for field in range(5):
            for start in range(STRIDE):
                for tile in range(4):
                    packed = jnp.zeros((8, LANES), jnp.float32)
                    for j in range(PER):
                        plane = STRIDE * j + start
                        value = tile_of(fields, x_band, low, field, plane, tile)
                        if plane < BAND and tile > 0:
                            value = value * keep_x
                        turned = pltpu.roll(value, GROUP * (j + 1 - half), 1)
                        packed = jnp.where(masks[j], turned, packed)
                    out[field, start, pl.ds(8 * tile, 8), :] = packed

    @pl.when(active == 0)
    def _():
        out[...] = jnp.zeros_like(out)


def relax_kernel(
    info, keep, iterate, source, wave, x_band, z_band, corner, halo, out,
    low, w, w_next, e_re, e_im, f_re, f_im, h, h_next, he_re, he_im, hf_re, hf_im, hq, hr, hs, mq, mr,
):
    half = info[0]
    active = info[1]

    @pl.when(active == 0)
    def _():
        out[...] = iterate[...]

    @pl.when(active == 1)
    def _():
        keep_x = keep[0]
        flag_x = keep[2]
        flag_z = keep[3]
        fill_low_tiles(low, z_band, corner, keep_x, keep[1])
        fields = [(iterate, 0), (iterate, 1), (source, 0), (source, 1), (wave, None)]
        lanes = lane_ids()
        rows = row_ids()
        place = lanes % GROUP
        group = lanes // GROUP
        least = (GROUP - HALO) * half
        zeros = jnp.zeros((8, LANES), jnp.float32)

        for scratch in (w, w_next, h, h_next):
            scratch[...] = jnp.zeros_like(scratch)

        def coefficients(wave_sq, s_re, s_im, sigma):
            diag = 5.0 - wave_sq
            scale = (0.5 * OMEGA) / (diag * diag + sigma * sigma)
            er = diag * scale
            ei = -sigma * scale
            return er, ei, 2.0 * (er * s_re - ei * s_im), 2.0 * (er * s_im + ei * s_re)

        def sigma_z(tile):
            if tile == 0:
                return zeros
            z = (rows + 8 * (tile - 1)).astype(jnp.float32)
            ramp = jnp.maximum(z - (CZ - PML) + 1.0, 0.0) / PML
            return SIGMA * ramp * ramp * flag_z

        for tile in range(4):
            along_z = sigma_z(tile)
            kept_rows = rows < 5
            for plane in range(EXT):
                values = [tile_of(fields, x_band, low, f, plane, tile) for f in range(5)]
                if plane < BAND and tile > 0:
                    values = [value * keep_x for value in values]
                w_re, w_im, s_re, s_im, wave_sq = values
                at = pl.ds(8 * tile, 8)
                w[0, plane + 1, pl.ds(8 + 8 * tile, 8), :] = w_re
                w[1, plane + 1, pl.ds(8 + 8 * tile, 8), :] = w_im
                if plane == 0:
                    er, ei, fr, fi = zeros, zeros, OMEGA * w_re, OMEGA * w_im
                else:
                    ramp = max(plane - BAND - (CX - PML) + 1.0, 0.0) / PML
                    sigma = along_z + SIGMA * ramp * ramp * flag_x
                    er, ei, fr, fi = coefficients(wave_sq, s_re, s_im, sigma)
                    if tile == 0:
                        er = jnp.where(kept_rows, 0.0, er)
                        ei = jnp.where(kept_rows, 0.0, ei)
                        fr = jnp.where(kept_rows, OMEGA * w_re, fr)
                        fi = jnp.where(kept_rows, OMEGA * w_im, fi)
                e_re[plane, at, :] = er
                e_im[plane, at, :] = ei
                f_re[plane, at, :] = fr
                f_im[plane, at, :] = fi

            for start in range(STRIDE):
                at = pl.ds(8 * tile, 8)
                w_re, w_im, s_re, s_im, wave_sq = [halo[f, start, at, :] for f in range(5)]
                h[0, start, pl.ds(8 + 8 * tile, 8), :] = w_re
                h[1, start, pl.ds(8 + 8 * tile, 8), :] = w_im
                x = (STRIDE * group + start - BAND).astype(jnp.float32)
                ramp = jnp.maximum(x - (CX - PML) + 1.0, 0.0) / PML
                sigma = along_z + SIGMA * ramp * ramp * flag_x
                er, ei, fr, fi = coefficients(wave_sq, s_re, s_im, sigma)
                kept = (place < least) | (place >= least + HALO) | (group == PER)
                if start == 0:
                    kept = kept | (group == 0)
                if tile == 0:
                    kept = kept | kept_rows
                he_re[start, at, :] = jnp.where(kept, 0.0, er)
                he_im[start, at, :] = jnp.where(kept, 0.0, ei)
                hf_re[start, at, :] = jnp.where(kept, OMEGA * w_re, fr)
                hf_im[start, at, :] = jnp.where(kept, OMEGA * w_im, fi)

        first_lane = lanes == 0
        last_lane = lanes == LANES - 1
        turns = [GROUP * (j + half) for j in range(PER)]
        joined = place == (GROUP - 1) * half
        to_edge = jnp.where(half == 0, LANES - 1, 1)
        back_turns = [lax.rem(LANES - turn + to_edge, LANES) for turn in turns]
        taken = [
            lanes == lax.rem(turn + jnp.where(half == 0, LANES - 1, 0), LANES) for turn in turns
        ]

        def updated(w_re, w_im, t_re, t_im, er, ei, fr, fi):
            new_re = (1.0 - OMEGA) * w_re + fr + (er * t_re - ei * t_im)
            new_im = (1.0 - OMEGA) * w_im + fi + (er * t_im + ei * t_re)
            return new_re, new_im

        def sweep(w, h, w_out, h_out):
            def centre_and_z(ref, part, plane, tile):
                base = 8 + 8 * tile
                return ref[part, plane, pl.ds(base, 8), :], (
                    ref[part, plane, pl.ds(base - 1, 8), :]
                    + ref[part, plane, pl.ds(base + 1, 8), :]
                )

            for tile in range(4):
                at = pl.ds(8 * tile, 8)
                for part in range(2):
                    both = [centre_and_z(h, part, s, tile) for s in range(STRIDE)]
                    below = [roll(value, GROUP) for value in both[-1]]
                    above = [roll(value, -GROUP) for value in both[0]]
                    both = [below] + both + [above]
                    for s in range(STRIDE):
                        q, near = stencil_parts(
                            both[s + 1][0], both[s][0] + both[s + 2][0],
                            both[s + 1][1], both[s][1] + both[s + 2][1],
                        )
                        hq[part, s, at, :] = q
                        hs[part, s, at, :] = jnp.where(joined, q, 0.0)
                        hr[part, s, at, :] = near

            for tile in range(4):
                at = pl.ds(8 * tile, 8)
                for part in range(2):
                    before, here = (zeros, zeros), centre_and_z(w, part, 1, tile)
                    for plane in range(EXT):
                        after = (zeros, zeros)
                        if plane + 1 < EXT:
                            after = centre_and_z(w, part, plane + 2, tile)
                        q, near = stencil_parts(
                            here[0], before[0] + after[0], here[1], before[1] + after[1]
                        )
                        mq[part, plane, at, :] = q
                        mr[part, plane, at, :] = near
                        before, here = here, after

            for tile in range(4):
                at = pl.ds(8 * tile, 8)
                base = 8 + 8 * tile
                for first in range(0, EXT, BATCH):
                    planes = range(first, first + BATCH)
                    q = [[mq[part, plane, at, :] for part in range(2)] for plane in planes]
                    up = [[roll(value, -1) for value in pair] for pair in q]
                    down = [[roll(value, 1) for value in pair] for pair in q]
                    side = [
                        [
                            pltpu.roll(hs[part, plane % STRIDE, at, :], back_turns[plane // STRIDE], 1)
                            for part in range(2)
                        ]
                        for plane in planes
                    ]
                    for n, plane in enumerate(planes):
                        total = [
                            jnp.where(last_lane, side[n][part], up[n][part])
                            + jnp.where(first_lane, side[n][part], down[n][part])
                            + mr[part, plane, at, :]
                            for part in range(2)
                        ]
                        new_re, new_im = updated(
                            w[0, plane + 1, pl.ds(base, 8), :], w[1, plane + 1, pl.ds(base, 8), :],
                            total[0], total[1],
                            e_re[plane, at, :], e_im[plane, at, :],
                            f_re[plane, at, :], f_im[plane, at, :],
                        )
                        w_out[0, plane + 1, pl.ds(base, 8), :] = new_re
                        w_out[1, plane + 1, pl.ds(base, 8), :] = new_im

            for tile in range(4):
                at = pl.ds(8 * tile, 8)
                base = 8 + 8 * tile
                for start in range(STRIDE):
                    total = []
                    for part in range(2):
                        turned = [
                            pltpu.roll(mq[part, STRIDE * j + start, at, :], turns[j], 1)
                            for j in range(PER)
                        ]
                        q = hq[part, start, at, :]
                        for j in range(PER):
                            q = jnp.where(taken[j], turned[j], q)
                        total.append(pair_sum(q) + hr[part, start, at, :])
                    new_re, new_im = updated(
                        h[0, start, pl.ds(base, 8), :], h[1, start, pl.ds(base, 8), :],
                        total[0], total[1],
                        he_re[start, at, :], he_im[start, at, :],
                        hf_re[start, at, :], hf_im[start, at, :],
                    )
                    h_out[0, start, pl.ds(base, 8), :] = new_re
                    h_out[1, start, pl.ds(base, 8), :] = new_im

        def two_sweeps(turn, carry):
            sweep(w, h, w_next, h_next)
            sweep(w_next, h_next, w, h)
            return carry

        lax.fori_loop(0, SWEEPS // 2, two_sweeps, 0)
        for part in range(2):
            for x in range(CX):
                out[part, x] = w[part, x + BAND + 1, pl.ds(16, CZ), :]


def fill_box(box, field, x_low, x_high, z_low, z_high, keep):
    for part in range(2):
        box[part, 0, pl.ds(8, CZ), :] = x_low[part] * keep[0]
        box[part, CX + 1, pl.ds(8, CZ), :] = x_high[part] * keep[1]
        for x in range(CX):
            box[part, x + 1, pl.ds(8, CZ), :] = field[part, x]
        for x in range(CX + 2):
            box[part, x, pl.ds(0, 8), :] = jnp.zeros((8, LANES), jnp.float32)
            box[part, x, pl.ds(8 + CZ, 8), :] = jnp.zeros((8, LANES), jnp.float32)
            side = 1.0 if 0 < x <= CX else keep[0 if x == 0 else 1]
            low_scale, high_scale = keep[2] * side, keep[3] * side
            box[part, x, pl.ds(7, 1), :] = z_low[part, pl.ds(x, 1), :] * low_scale
            box[part, x, pl.ds(8 + CZ, 1), :] = z_high[part, pl.ds(x, 1), :] * high_scale


def side_kernel(info, keep, field, x_low, x_high, z_low, z_high, out, box):
    half = info[0]
    fill_box(box, field, x_low, x_high, z_low, z_high, keep)
    lanes = lane_ids()
    edge = jnp.where(half == 0, LANES - 1, 0)
    for part in range(2):
        for tile in range(5):
            packed = jnp.zeros((8, LANES), jnp.float32)
            for x in range(CX + 2):
                value = box[part, x, pl.ds(8 * tile, 8), :]
                turned = pltpu.roll(value, lax.rem(x + LANES - edge, LANES), 1)
                packed = jnp.where(lanes == x, turned, packed)
            out[part, pl.ds(8 * tile, 8), :] = packed


def residual_kernel(
    info, keep, field, source, wave, x_low, x_high, z_low, z_high, side, out, total, box, sides
):
    half = info[0]
    fill_box(box, field, x_low, x_high, z_low, z_high, keep)
    lanes = lane_ids()
    zeros = jnp.zeros((8, LANES), jnp.float32)
    first_lane = lanes == 0
    last_lane = lanes == LANES - 1
    open_lane = lanes == jnp.where(half == 0, 0, LANES - 1)
    squares = zeros
    for part in range(2):
        for tile in range(1, 4):
            base = 8 * tile
            c = side[part, pl.ds(base, 8), :]
            zc = side[part, pl.ds(base - 1, 8), :] + side[part, pl.ds(base + 1, 8), :]
            side_q, _ = stencil_parts(c, pair_sum(c), zc, pair_sum(zc))

            def load(plane):
                c = box[part, plane, pl.ds(base, 8), :]
                zc = (
                    box[part, plane, pl.ds(base - 1, 8), :]
                    + box[part, plane, pl.ds(base + 1, 8), :]
                )
                return c, zc

            before, here = load(0), load(1)
            at = pl.ds(base - 8, 8)
            for x in range(CX):
                after = load(x + 2)
                q, near = stencil_parts(
                    here[0], before[0] + after[0], here[1], before[1] + after[1]
                )
                shift = lax.rem(2 * LANES - (x + 1) - half, LANES)
                beyond = jnp.where(open_lane, pltpu.roll(side_q, shift, 1), 0.0)
                up = roll(jnp.where(first_lane, beyond, q), -1)
                down = roll(jnp.where(last_lane, beyond, q), 1)
                gap = (
                    source[part, x, at, :]
                    - (5.0 - wave[x, at, :]) * here[0]
                    + 0.5 * (up + down + near)
                )
                out[part, x, at, :] = gap
                squares = squares + gap * gap
                before, here = here, after
    total[...] = jnp.broadcast_to(jnp.sum(squares), total.shape)


def params():
    return pltpu.CompilerParams(vmem_limit_bytes=VMEM_LIMIT)


def f32(*shape):
    return jax.ShapeDtypeStruct(shape, jnp.float32)


def ring(value, axis, by):
    size = lax.axis_size(axis)
    return lax.ppermute(value, axis, [(i, (i + by) % size) for i in range(size)])


def diagonal(value, by_x, by_z):
    size_x, size_z = lax.axis_size("gx"), lax.axis_size("gz")
    pairs = [
        (x * size_z + z, ((x + by_x) % size_x) * size_z + (z + by_z) % size_z)
        for x in range(size_x)
        for z in range(size_z)
    ]
    return lax.ppermute(value, ("gx", "gz"), pairs)


def swap(value):
    return lax.ppermute(value, "gy", [(0, 1), (1, 0)])


def on_device(source, iterate, wave_sq, front, pml_flags):
    size_x, size_z, size_y = lax.axis_size("gx"), lax.axis_size("gz"), lax.axis_size("gy")
    at_x, at_z, half = lax.axis_index("gx"), lax.axis_index("gz"), lax.axis_index("gy")
    active = (jnp.mod(at_x + at_z - front[0], size_z) == 0).astype(jnp.int32)
    info = jnp.stack([half.astype(jnp.int32), active])
    flag_bits = pml_flags[0, 0]
    as_float = lambda test: test.astype(jnp.float32)
    band_keep = jnp.stack(
        [
            as_float(at_x > 0),
            as_float(at_z > 0),
            as_float(flag_bits % 2),
            as_float(flag_bits // 2 % 2),
        ]
    )
    box_keep = jnp.stack(
        [
            as_float(at_x > 0),
            as_float(at_x < size_x - 1),
            as_float(at_z > 0),
            as_float(at_z < size_z - 1),
        ]
    )

    def bands(index):
        return jnp.concatenate([iterate[index], source[index], wave_sq[index[1:]][None]], 0)

    every, last = slice(None), slice(CX - BAND, CX)
    corner = diagonal(bands((every, last, last)), 1, 1)
    x_band = ring(bands((every, last, every)), "gx", 1)
    z_band = ring(bands((every, every, last)), "gz", 1)

    halo = pl.pallas_call(
        halo_kernel,
        out_shape=f32(5, STRIDE, 32, LANES),
        in_specs=[SMEM] * 2 + [VMEM] * 6,
        out_specs=VMEM,
        scratch_shapes=[pltpu.VMEM((5, EXT, 8, LANES), jnp.float32)],
        compiler_params=params(),
        name="pack_halo",
    )(info, band_keep, iterate, source, wave_sq, x_band, z_band, corner)
    halo = swap(halo)
    box_like = pltpu.VMEM((EXT, 32, LANES), jnp.float32)
    halo_like = pltpu.VMEM((STRIDE, 32, LANES), jnp.float32)
    pair_like = pltpu.VMEM((2, STRIDE, 32, LANES), jnp.float32)
    plane_pair = pltpu.VMEM((2, EXT, 32, LANES), jnp.float32)
    new = pl.pallas_call(
        relax_kernel,
        out_shape=f32(2, CX, CZ, LANES),
        in_specs=[SMEM] * 2 + [VMEM] * 7,
        out_specs=VMEM,
        scratch_shapes=[
            pltpu.VMEM((5, EXT, 8, LANES), jnp.float32),
            pltpu.VMEM((2, EXT + 2, 48, LANES), jnp.float32),
            pltpu.VMEM((2, EXT + 2, 48, LANES), jnp.float32),
            box_like, box_like, box_like, box_like,
            pltpu.VMEM((2, STRIDE, 48, LANES), jnp.float32),
            pltpu.VMEM((2, STRIDE, 48, LANES), jnp.float32),
            halo_like, halo_like, halo_like, halo_like,
            pair_like, pair_like, pair_like, plane_pair, plane_pair,
        ],
        compiler_params=params(),
        name="relax",
    )(info, band_keep, iterate, source, wave_sq, x_band, z_band, corner, halo)

    x_low = ring(new[:, CX - 1], "gx", 1)
    x_high = ring(new[:, 0], "gx", -1)

    def face(z):
        return jnp.concatenate([x_low[:, z][:, None], new[:, :, z], x_high[:, z][:, None]], 1)

    z_low = ring(face(CZ - 1), "gz", 1)
    z_high = ring(face(0), "gz", -1)
    box_scratch = pltpu.VMEM((2, CX + 2, 48, LANES), jnp.float32)
    side = pl.pallas_call(
        side_kernel,
        out_shape=f32(2, 40, LANES),
        in_specs=[SMEM] * 2 + [VMEM] * 5,
        out_specs=VMEM,
        scratch_shapes=[box_scratch],
        compiler_params=params(),
        name="y_side",
    )(info, box_keep, new, x_low, x_high, z_low, z_high)
    side = swap(side)
    count = size_x * size_z * size_y
    residual, total = pl.pallas_call(
        residual_kernel,
        out_shape=(f32(2, CX, CZ, LANES), f32(count, LANES)),
        in_specs=[SMEM] * 2 + [VMEM] * 8,
        out_specs=(VMEM, VMEM),
        scratch_shapes=[box_scratch, pltpu.VMEM((2, 40, LANES), jnp.float32)],
        compiler_params=params(),
        name="residual",
    )(info, box_keep, new, source, wave_sq, x_low, x_high, z_low, z_high, side)
    parts = lax.all_to_all(total, ("gx", "gz", "gy"), 0, 0, tiled=True)
    cells = 2 * CX * CZ * LANES * count
    norm = jnp.sqrt(jnp.sum(parts, axis=0)[:1] / cells)
    return new, residual, norm


def solution(mesh):
    in_specs = (
        P(None, "gx", "gz", "gy"),
        P(None, "gx", "gz", "gy"),
        P("gx", "gz", "gy"),
        P(),
        P("gx", "gz"),
    )
    out_specs = (P(None, "gx", "gz", "gy"), P(None, "gx", "gz", "gy"), P())
    return jax.shard_map(
        on_device, mesh=mesh, in_specs=in_specs, out_specs=out_specs, check_vma=False
    )
```

profile of v0, /device:TPU:1, one launch (start us, length us, event | category | flops | bytes accessed | tf_op | source)
XLA Modules:
  0.0 101.5 jit_solution(5216355693147483813)
XLA Ops:
  0.6 0.9 slice_bitcast_fusion.1
  1.5 0.9 slice.54
  2.4 0.9 slice-done
  3.3 2.2 %collective-permute-start = (f32[5,4,24,128]{3,2,1,0:T(8,128)S(1)}, f32[5,4,24,128]{3,2,1,0:T(8,128)S(1)}, u32[]{:S(2)}, u32[]{:S(2)}) collective-permute-start(f32[5,4,24,128]{3,2,1,0:T(8,128)S(1)} %pad_maximum_fusion), channel_id=1, source_target_pairs={{0,16},{16,32},{32,48},{48,64},{64,80},{80,96},{96,112},{112,128},... | collective-permute-start | bytes 737288 | tf_op jit(solution)/shard_map/ppermute | solution.py:408
  5.6 1.0 slice.57
  6.6 1.7 %collective-permute-start.1 = (f32[5,24,4,128]{3,2,1,0:T(4,128)S(1)}, f32[5,24,4,128]{3,2,1,0:T(4,128)S(1)}, u32[]{:S(2)}, u32[]{:S(2)}) collective-permute-start(f32[5,24,4,128]{3,2,1,0:T(4,128)S(1)} %pad_maximum_fusion.1), channel_id=1, source_target_pairs={{0,2},{2,4},{4,6},{6,8},{8,10},{10,12},{12,14},{14,0},{1,3},{3,5},... | collective-permute-start | bytes 737288 | tf_op jit(solution)/shard_map/ppermute | solution.py:408
  8.4 2.7 %collective-permute-start.2 = (f32[5,4,4,128]{3,2,1,0:T(4,128)S(1)}, f32[5,4,4,128]{3,2,1,0:T(4,128)S(1)}, u32[]{:S(2)}, u32[]{:S(2)}) collective-permute-start(f32[5,4,4,128]{3,2,1,0:T(4,128)S(1)} %pad_maximum_fusion.2), channel_id=1, source_target_pairs={{0,18},{2,20},{4,22},{6,24},{8,26},{10,28},{12,30},{14,16},{16,34}... | collective-permute-start | bytes 122888 | tf_op jit(solution)/shard_map/ppermute | solution.py:418
  12.6 9.2 %collective-permute-done.2.corner = f32[5,4,4,128]{3,2,1,0:T(4,128)S(1)} collective-permute-done((f32[5,4,4,128]{3,2,1,0:T(4,128)S(1)}, f32[5,4,4,128]{3,2,1,0:T(4,128)S(1)}, u32[]{:S(2)}, u32[]{:S(2)}) %collective-permute-start.2) | collective-permute-done | bytes 40992 | tf_op jit(solution)/shard_map/ppermute | solution.py:418
  21.9 1.2 %pack_halo.1 = f32[5,4,32,128]{3,2,1,0:T(8,128)S(1)} custom-call(s32[2]{0:T(128)S(1)} %pad_add_fusion.info, f32[4]{0:T(128)S(1)} %pad_maximum_fusion.5.keep, f32[2,24,24,128]{3,2,1,0:T(8,128)S(1)} %copy-done.3, f32[2,24,24,128]{3,2,1,0:T(8,128)S(1)} %copy-done, f32[24,24,128]{2,1,0:T(8,128)S(1)} %copy-done.2, ...), custom_call_target="tpu_custom_call" | custom-call | tf_op jit(solution)/shard_map/pack_halo/pallas_call | solution.py:457
  23.1 1.7 %collective-permute-start.3 = (f32[5,4,32,128]{3,2,1,0:T(8,128)S(1)}, f32[5,4,32,128]{3,2,1,0:T(8,128)S(1)}, u32[]{:S(2)}, u32[]{:S(2)}) collective-permute-start(f32[5,4,32,128]{3,2,1,0:T(8,128)S(1)} %pack_halo.1), channel_id=1, source_target_pairs={{0,1},{1,0},{2,3},{3,2},{4,5},{5,4},{6,7},{7,6},{8,9},{9,8},{10,11... | collective-permute-start | bytes 983048 | tf_op jit(solution)/shard_map/ppermute | solution.py:422
  24.8 1.3 %collective-permute-done.3.halo = f32[5,4,32,128]{3,2,1,0:T(8,128)S(1)} collective-permute-done((f32[5,4,32,128]{3,2,1,0:T(8,128)S(1)}, f32[5,4,32,128]{3,2,1,0:T(8,128)S(1)}, u32[]{:S(2)}, u32[]{:S(2)}) %collective-permute-start.3) | collective-permute-done | bytes 327712 | tf_op jit(solution)/shard_map/ppermute | solution.py:422
  26.1 32.3 %relax.1.field = f32[2,24,24,128]{3,2,1,0:T(8,128)} custom-call(s32[2]{0:T(128)S(1)} %pad_add_fusion.info, f32[4]{0:T(128)S(1)} %pad_maximum_fusion.5.keep, f32[2,24,24,128]{3,2,1,0:T(8,128)S(1)} %copy-done.3, f32[2,24,24,128]{3,2,1,0:T(8,128)S(1)} %copy-done, f32[24,24,128]{2,1,0:T(8,128)S(1)} %copy-done.2, ...), custom_call_target="tpu_custom_call" | custom-call | tf_op jit(solution)/shard_map/relax/pallas_call | solution.py:471
  58.4 0.8 slice_bitcast_fusion.2
  59.1 1.1 %fusion = (f32[2,24,1,128]{3,2,1,0:T(1,128)S(1)}, f32[2,24,1,128]{3,2,1,0:T(1,128)S(1)}) fusion(f32[2,24,24,128]{3,2,1,0:T(8,128)} %relax.1.field), kind=kLoop, calls=%fused_computation.13 | loop fusion | bytes 98304 | tf_op jit(solution)/shard_map/slice | solution.py:494
  60.2 1.5 %collective-permute-start.4 = (f32[2,24,128]{2,1,0:T(8,128)S(1)}, f32[2,24,128]{2,1,0:T(8,128)S(1)}, u32[]{:S(2)}, u32[]{:S(2)}) collective-permute-start(f32[2,24,128]{2,1,0:T(8,128)S(1)} %get-tuple-element.10), channel_id=1, source_target_pairs={{0,16},{16,32},{32,48},{48,64},{64,80},{80,96},{96,112},{112,128},... | collective-permute-start | bytes 73736 | tf_op jit(solution)/shard_map/ppermute | solution.py:408
  61.8 4.5 %collective-permute-done.4.x_low = f32[2,24,128]{2,1,0:T(8,128)S(1)} collective-permute-done((f32[2,24,128]{2,1,0:T(8,128)S(1)}, f32[2,24,128]{2,1,0:T(8,128)S(1)}, u32[]{:S(2)}, u32[]{:S(2)}) %collective-permute-start.4) | collective-permute-done | bytes 24608 | tf_op jit(solution)/shard_map/ppermute | solution.py:408
  66.4 2.7 %collective-permute-start.7 = (f32[2,26,128]{2,1,0:T(8,128)S(1)}, f32[2,26,128]{2,1,0:T(8,128)S(1)}, u32[]{:S(2)}, u32[]{:S(2)}) collective-permute-start(f32[2,26,128]{2,1,0:T(8,128)S(1)} %pad_maximum_fusion.4), channel_id=1, source_target_pairs={{0,14},{2,0},{4,2},{6,4},{8,6},{10,8},{12,10},{14,12},{1,15},{3,1}... | collective-permute-start | bytes 79880 | tf_op jit(solution)/shard_map/ppermute | solution.py:408
  69.2 1.1 %collective-permute-done.6.z_low = f32[2,26,128]{2,1,0:T(8,128)S(1)} collective-permute-done((f32[2,26,128]{2,1,0:T(8,128)S(1)}, f32[2,26,128]{2,1,0:T(8,128)S(1)}, u32[]{:S(2)}, u32[]{:S(2)}) %collective-permute-start.6) | collective-permute-done | bytes 26656 | tf_op jit(solution)/shard_map/ppermute | solution.py:408
  70.4 1.1 %copy-done.1 = f32[2,24,24,128]{3,2,1,0:T(8,128)S(1)} copy-done((f32[2,24,24,128]{3,2,1,0:T(8,128)S(1)}, f32[2,24,24,128]{3,2,1,0:T(8,128)}, u32[]{:S(2)}) %copy-start.1) | copy-done | bytes 589848
  71.4 0.9 y_side.1
  72.4 2.8 %collective-permute-start.8 = (f32[2,40,128]{2,1,0:T(8,128)S(1)}, f32[2,40,128]{2,1,0:T(8,128)S(1)}, u32[]{:S(2)}, u32[]{:S(2)}) collective-permute-start(f32[2,40,128]{2,1,0:T(8,128)S(1)} %y_side.1), channel_id=1, source_target_pairs={{0,1},{1,0},{2,3},{3,2},{4,5},{5,4},{6,7},{7,6},{8,9},{9,8},{10,11... | collective-permute-start | bytes 122888 | tf_op jit(solution)/shard_map/ppermute | solution.py:422
  75.1 0.9 collective-permute-done.8.side
  76.0 4.6 %residual.1 = (f32[2,24,24,128]{3,2,1,0:T(8,128)}, f32[256,128]{1,0:T(8,128)S(1)}) custom-call(s32[2]{0:T(128)S(1)} %pad_add_fusion.info, f32[4]{0:T(128)S(1)} %pad_maximum_fusion.6.keep, f32[2,24,24,128]{3,2,1,0:T(8,128)S(1)} %copy-done.1, f32[2,24,24,128]{3,2,1,0:T(8,128)S(1)} %copy-done, f32[24,24,128]{2,1,0:T(8,128)S(1)} %copy-done.2, ...), custom_call_target="tpu_custom_call" | custom-call | tf_op jit(solution)/shard_map/residual/pallas_call | solution.py:510
  80.6 19.5 %all_to_all.9 = f32[256,1,128]{2,1,0:T(1,128)S(1)} all-to-all(f32[256,1,128]{2,1,0:T(1,128)S(1)} %bitcast.39), channel_id=1, replica_groups=mesh['gx'=16,'gz'=8,'gy'=2] {'gx','gz','gy'}, dimensions={0} | all-to-all | bytes 262144 | tf_op jit(solution)/shard_map/all_to_all | solution.py:519
  (30 shorter events, 0.9 us)
Async XLA Ops:
  0.6 4.9 %copy-start.2 = (f32[24,24,128]{2,1,0:T(8,128)S(1)}, f32[24,24,128]{2,1,0:T(8,128)}, u32[]{:S(2)}) copy-start(f32[24,24,128]{2,1,0:T(8,128)} %wave.5) | copy-start | bytes 884740
  2.4 0.9 slice-start
  2.4 4.1 %copy-start = (f32[2,24,24,128]{3,2,1,0:T(8,128)S(1)}, f32[2,24,24,128]{3,2,1,0:T(8,128)}, u32[]{:S(2)}) copy-start(f32[2,24,24,128]{3,2,1,0:T(8,128)} %source.5) | copy-start | bytes 1769476
  3.3 5.0 %copy-start.3 = (f32[2,24,24,128]{3,2,1,0:T(8,128)S(1)}, f32[2,24,24,128]{3,2,1,0:T(8,128)}, u32[]{:S(2)}) copy-start(f32[2,24,24,128]{3,2,1,0:T(8,128)} %iterate.3) | copy-start | bytes 1769476
  3.3 18.5 %collective-permute-start = (f32[5,4,24,128]{3,2,1,0:T(8,128)S(1)}, f32[5,4,24,128]{3,2,1,0:T(8,128)S(1)}, u32[]{:S(2)}, u32[]{:S(2)}) collective-permute-start(f32[5,4,24,128]{3,2,1,0:T(8,128)S(1)} %pad_maximum_fusion), channel_id=1, source_target_pairs={{0,16},{16,32},{32,48},{48,64},{64,80},{80,96},{96,112},{112,128},... | collective-permute-start | bytes 737288 | tf_op jit(solution)/shard_map/ppermute | solution.py:408
  6.6 15.3 %collective-permute-start.1 = (f32[5,24,4,128]{3,2,1,0:T(4,128)S(1)}, f32[5,24,4,128]{3,2,1,0:T(4,128)S(1)}, u32[]{:S(2)}, u32[]{:S(2)}) collective-permute-start(f32[5,24,4,128]{3,2,1,0:T(4,128)S(1)} %pad_maximum_fusion.1), channel_id=1, source_target_pairs={{0,2},{2,4},{4,6},{6,8},{8,10},{10,12},{12,14},{14,0},{1,3},{3,5},... | collective-permute-start | bytes 737288 | tf_op jit(solution)/shard_map/ppermute | solution.py:408
  8.4 13.5 %collective-permute-start.2 = (f32[5,4,4,128]{3,2,1,0:T(4,128)S(1)}, f32[5,4,4,128]{3,2,1,0:T(4,128)S(1)}, u32[]{:S(2)}, u32[]{:S(2)}) collective-permute-start(f32[5,4,4,128]{3,2,1,0:T(4,128)S(1)} %pad_maximum_fusion.2), channel_id=1, source_target_pairs={{0,18},{2,20},{4,22},{6,24},{8,26},{10,28},{12,30},{14,16},{16,34}... | collective-permute-start | bytes 122888 | tf_op jit(solution)/shard_map/ppermute | solution.py:418
  23.1 2.9 %collective-permute-start.3 = (f32[5,4,32,128]{3,2,1,0:T(8,128)S(1)}, f32[5,4,32,128]{3,2,1,0:T(8,128)S(1)}, u32[]{:S(2)}, u32[]{:S(2)}) collective-permute-start(f32[5,4,32,128]{3,2,1,0:T(8,128)S(1)} %pack_halo.1), channel_id=1, source_target_pairs={{0,1},{1,0},{2,3},{3,2},{4,5},{5,4},{6,7},{7,6},{8,9},{9,8},{10,11... | collective-permute-start | bytes 983048 | tf_op jit(solution)/shard_map/ppermute | solution.py:422
  59.1 2.7 %collective-permute-start.5 = (f32[2,24,128]{2,1,0:T(8,128)S(1)}, f32[2,24,128]{2,1,0:T(8,128)S(1)}, u32[]{:S(2)}, u32[]{:S(2)}) collective-permute-start(f32[2,24,128]{2,1,0:T(8,128)S(1)} %get-tuple-element.9), channel_id=1, source_target_pairs={{0,240},{16,0},{32,16},{48,32},{64,48},{80,64},{96,80},{112,96},{1... | collective-permute-start | bytes 73736 | tf_op jit(solution)/shard_map/ppermute | solution.py:408
  60.2 6.1 %collective-permute-start.4 = (f32[2,24,128]{2,1,0:T(8,128)S(1)}, f32[2,24,128]{2,1,0:T(8,128)S(1)}, u32[]{:S(2)}, u32[]{:S(2)}) collective-permute-start(f32[2,24,128]{2,1,0:T(8,128)S(1)} %get-tuple-element.10), channel_id=1, source_target_pairs={{0,16},{16,32},{32,48},{48,64},{64,80},{80,96},{96,112},{112,128},... | collective-permute-start | bytes 73736 | tf_op jit(solution)/shard_map/ppermute | solution.py:408
  66.3 4.1 %collective-permute-start.6 = (f32[2,26,128]{2,1,0:T(8,128)S(1)}, f32[2,26,128]{2,1,0:T(8,128)S(1)}, u32[]{:S(2)}, u32[]{:S(2)}) collective-permute-start(f32[2,26,128]{2,1,0:T(8,128)S(1)} %pad_maximum_fusion.3), channel_id=1, source_target_pairs={{0,2},{2,4},{4,6},{6,8},{8,10},{10,12},{12,14},{14,0},{1,3},{3,5},... | collective-permute-start | bytes 79880 | tf_op jit(solution)/shard_map/ppermute | solution.py:408
  66.4 3.9 %collective-permute-start.7 = (f32[2,26,128]{2,1,0:T(8,128)S(1)}, f32[2,26,128]{2,1,0:T(8,128)S(1)}, u32[]{:S(2)}, u32[]{:S(2)}) collective-permute-start(f32[2,26,128]{2,1,0:T(8,128)S(1)} %pad_maximum_fusion.4), channel_id=1, source_target_pairs={{0,14},{2,0},{4,2},{6,4},{8,6},{10,8},{12,10},{14,12},{1,15},{3,1}... | collective-permute-start | bytes 79880 | tf_op jit(solution)/shard_map/ppermute | solution.py:408
  70.4 1.1 %copy-start.1 = (f32[2,24,24,128]{3,2,1,0:T(8,128)S(1)}, f32[2,24,24,128]{3,2,1,0:T(8,128)}, u32[]{:S(2)}) copy-start(f32[2,24,24,128]{3,2,1,0:T(8,128)} %relax.1.field) | copy-start | bytes 1769476
  72.4 3.6 %collective-permute-start.8 = (f32[2,40,128]{2,1,0:T(8,128)S(1)}, f32[2,40,128]{2,1,0:T(8,128)S(1)}, u32[]{:S(2)}, u32[]{:S(2)}) collective-permute-start(f32[2,40,128]{2,1,0:T(8,128)S(1)} %y_side.1), channel_id=1, source_target_pairs={{0,1},{1,0},{2,3},{3,2},{4,5},{5,4},{6,7},{7,6},{8,9},{9,8},{10,11... | collective-permute-start | bytes 122888 | tf_op jit(solution)/shard_map/ppermute | solution.py:422
where the time goes:
time: 102 us
  Pallas kernels  39.1 us (38%)
  blocking collectives  19.5 us (19%)
  waiting for transfers between devices  17 us (17%)
  starting transfers between devices  15.5 us (15%)
  local copies, waits for them, and re-layouts  6.56 us (6%)
  between operations  3.33 us (3%)
    pallas_call x1, Pallas kernels, on_device(): pl.pallas_call(relax_kernel, out_shape=f32(2, CX, CZ, LANES), in_specs=[S...  32.3 us
    all_to_all x1, blocking collectives, on_device(): parts = lax.all_to_all(total, ('gx', 'gz', 'gy'), 0, 0, tiled=True)  19.5 us
    ppermute x1, waiting for transfers between devices, diagonal(): return lax.ppermute(value, ('gx', 'gz'), pairs)  9.25 us
    ppermute x6, starting transfers between devices, ring(): lax.ppermute(value, axis, [(i, (i + by) % size) for i in range(size)])  8.28 us
    ppermute x6, waiting for transfers between devices, ring(): lax.ppermute(value, axis, [(i, (i + by) % size) for i in range(size)])  5.67 us
    pallas_call x1, Pallas kernels, on_device(): pl.pallas_call(residual_kernel, out_shape=(f32(2, CX, CZ, LANES), f32(cou...  4.6 us
    ppermute x2, starting transfers between devices, swap(): return lax.ppermute(value, 'gy', [(0, 1), (1, 0)])  4.45 us
    ppermute x1, starting transfers between devices, diagonal(): return lax.ppermute(value, ('gx', 'gz'), pairs)  2.73 us
  transfers between devices with their start and end apart: 9, of which 6 were waited for; matrix products, arithmetic and copies ran while one was open for 2% of the time, Pallas kernels for 0%

commit v1 on v0

v1 whole, which is shorter than its diff:
```python
import jax
import jax.numpy as jnp
from jax import lax
from jax.experimental import pallas as pl
from jax.experimental.pallas import tpu as pltpu
from jax.sharding import PartitionSpec as P

BAND = 4
PML = 8
SWEEPS = 10
OMEGA = 0.6
SIGMA = 6.0

CX = 24
CZ = 24
LANES = 128
EXT = CX + BAND
GROUP = 16
HALO = 11
STRIDE = 4
LAYERS = 2 * BAND + 3 * (BAND - 1)
PER = EXT // STRIDE

SIDE_ROW = 26

MIB = 1024 * 1024

SMEM = pl.BlockSpec(memory_space=pltpu.SMEM)
VMEM = pl.BlockSpec(memory_space=pltpu.VMEM)
HBM = pl.BlockSpec(memory_space=pltpu.HBM)


def lane_ids():
    return lax.broadcasted_iota(jnp.int32, (8, LANES), 1)


def row_ids():
    return lax.broadcasted_iota(jnp.int32, (8, LANES), 0)


def roll(value, shift):
    if isinstance(shift, int):
        shift = shift % LANES
        if shift == 0:
            return value
    return pltpu.roll(value, shift, 1)


def pair_sum(value):
    return roll(value, 1) + roll(value, -1)


def stencil_parts(centre, across, z_centre, z_across):
    both = across + z_centre
    part = 0.25 * z_across
    near = both + part
    return centre + 0.25 * (near + part), near


def layers(field):
    return 0 if field < 2 else 1


def layer_row(field, layer):
    return 4 * field + layer if field < 2 else 8 + 3 * (field - 2) + layer - 1


def bands_kernel(iterate, source, wave, x_out, z_out, corner_out, x_part, z_part, sems):
    fields = [iterate.at[0], iterate.at[1], source.at[0], source.at[1], wave]
    copies = [
        pltpu.make_async_copy(ref.at[pl.ds(CX - BAND, BAND)], x_part.at[f], sems.at[f])
        for f, ref in enumerate(fields)
    ]
    for f, ref in enumerate(fields):
        for piece in range(2):
            some = pl.ds(CX // 2 * piece, CX // 2)
            copies.append(
                pltpu.make_async_copy(
                    ref.at[some, pl.ds(CZ - 8, 8)], z_part.at[f, some], sems.at[5 + 2 * f + piece]
                )
            )
    for copy in copies:
        copy.start()
    for copy in copies:
        copy.wait()
    corner_out[...] = jnp.zeros_like(corner_out)
    for field in range(5):
        first = layers(field)
        depth = BAND - first
        for layer in range(first, BAND):
            row = layer_row(field, layer)
            x_out[row] = x_part[field, layer]
            corner_out[pl.ds(BAND * row, BAND), :] = x_part[field, layer, pl.ds(CZ - BAND, BAND), :]
        for x in range(CX):
            rows = pl.ds(LAYERS * x + layer_row(field, first), depth)
            z_out[rows, :] = z_part[field, x, pl.ds(8 - depth, depth), :]


def tile_of(fields, bands, corner_tiles, field, plane, tile, keep_x):
    if tile == 0:
        return corner_tiles[field, plane]
    rows = pl.ds(8 * (tile - 1), 8)
    if plane < BAND:
        if plane < layers(field):
            return jnp.zeros((8, LANES), jnp.float32)
        return bands[layer_row(field, plane), rows, :] * keep_x
    ref, index = fields[field]
    x = plane - BAND
    return ref[x, rows, :] if index is None else ref[index, x, rows, :]


def fill_low_tiles(low, z_band, corner, keep_x, keep_z):
    keep_both = keep_x * keep_z
    low[...] = jnp.zeros_like(low)
    for field in range(5):
        first = layers(field)
        depth = BAND - first
        for plane in range(EXT):
            to = pl.ds(8 - depth, depth)
            if plane >= BAND:
                rows = pl.ds(LAYERS * (plane - BAND) + layer_row(field, first), depth)
                low[field, plane, to, :] = z_band[rows, :] * keep_z
            elif plane >= first:
                rows = pl.ds(BAND * layer_row(field, plane) + first, depth)
                low[field, plane, to, :] = corner[rows, :] * keep_both


def halo_kernel(info, keep, iterate, source, wave, x_band, z_band, corner, out, low):
    half = info[0]
    keep_x = keep[0]
    fill_low_tiles(low, z_band, corner, keep_x, keep[1])
    fields = [(iterate, 0), (iterate, 1), (source, 0), (source, 1), (wave, None)]
    lanes = lane_ids()
    place = lanes % GROUP
    least = (GROUP - HALO) * (1 - half)
    wanted = (place >= least) & (place < least + HALO)
    masks = [wanted & (lanes // GROUP == j) for j in range(PER)]
    for field in range(5):
        for start in range(STRIDE):
            for tile in range(4):
                packed = jnp.zeros((8, LANES), jnp.float32)
                for j in range(PER):
                    value = tile_of(fields, x_band, low, field, STRIDE * j + start, tile, keep_x)
                    turned = pltpu.roll(value, GROUP * (j + 1 - half), 1)
                    packed = jnp.where(masks[j], turned, packed)
                out[field, start, pl.ds(8 * tile, 8), :] = packed


def relax_kernel(
    info, keep, iterate, source, wave, x_band, z_band, corner, halo,
    out, own, beside, x_first, x_last, z_first, z_last,
    low, w, w_next, e_re, e_im, f_re, f_im, h, h_next, he_re, he_im, hf_re, hf_im, hq, hr, hs, mq, mr,
):
    half = info[0]
    active = info[1]

    @pl.when(active == 0)
    def _():
        own[...] = iterate[...]
        beside[...] = halo[pl.ds(0, 2)]

    @pl.when(active == 1)
    def _():
        keep_x = keep[0]
        flag_x = keep[2]
        flag_z = keep[3]
        fill_low_tiles(low, z_band, corner, keep_x, keep[1])
        fields = [(iterate, 0), (iterate, 1), (source, 0), (source, 1), (wave, None)]
        lanes = lane_ids()
        rows = row_ids()
        place = lanes % GROUP
        group = lanes // GROUP
        least = (GROUP - HALO) * half
        zeros = jnp.zeros((8, LANES), jnp.float32)

        for scratch in (w, w_next, h, h_next):
            scratch[...] = jnp.zeros_like(scratch)

        def coefficients(wave_sq, s_re, s_im, sigma):
            diag = 5.0 - wave_sq
            scale = (0.5 * OMEGA) / (diag * diag + sigma * sigma)
            er = diag * scale
            ei = -sigma * scale
            return er, ei, 2.0 * (er * s_re - ei * s_im), 2.0 * (er * s_im + ei * s_re)

        def sigma_z(tile):
            if tile == 0:
                return zeros
            z = (rows + 8 * (tile - 1)).astype(jnp.float32)
            ramp = jnp.maximum(z - (CZ - PML) + 1.0, 0.0) / PML
            return SIGMA * ramp * ramp * flag_z

        for tile in range(4):
            along_z = sigma_z(tile)
            kept_rows = rows < 5
            for plane in range(EXT):
                values = [tile_of(fields, x_band, low, f, plane, tile, keep_x) for f in range(5)]
                w_re, w_im, s_re, s_im, wave_sq = values
                at = pl.ds(8 * tile, 8)
                w[0, plane + 1, pl.ds(8 + 8 * tile, 8), :] = w_re
                w[1, plane + 1, pl.ds(8 + 8 * tile, 8), :] = w_im
                if plane == 0:
                    er, ei, fr, fi = zeros, zeros, OMEGA * w_re, OMEGA * w_im
                else:
                    ramp = max(plane - BAND - (CX - PML) + 1.0, 0.0) / PML
                    sigma = along_z + SIGMA * ramp * ramp * flag_x
                    er, ei, fr, fi = coefficients(wave_sq, s_re, s_im, sigma)
                    if tile == 0:
                        er = jnp.where(kept_rows, 0.0, er)
                        ei = jnp.where(kept_rows, 0.0, ei)
                        fr = jnp.where(kept_rows, OMEGA * w_re, fr)
                        fi = jnp.where(kept_rows, OMEGA * w_im, fi)
                e_re[plane, at, :] = er
                e_im[plane, at, :] = ei
                f_re[plane, at, :] = fr
                f_im[plane, at, :] = fi

            for start in range(STRIDE):
                at = pl.ds(8 * tile, 8)
                w_re, w_im, s_re, s_im, wave_sq = [halo[f, start, at, :] for f in range(5)]
                h[0, start, pl.ds(8 + 8 * tile, 8), :] = w_re
                h[1, start, pl.ds(8 + 8 * tile, 8), :] = w_im
                x = (STRIDE * group + start - BAND).astype(jnp.float32)
                ramp = jnp.maximum(x - (CX - PML) + 1.0, 0.0) / PML
                sigma = along_z + SIGMA * ramp * ramp * flag_x
                er, ei, fr, fi = coefficients(wave_sq, s_re, s_im, sigma)
                kept = (place < least) | (place >= least + HALO) | (group == PER)
                if start == 0:
                    kept = kept | (group == 0)
                if tile == 0:
                    kept = kept | kept_rows
                he_re[start, at, :] = jnp.where(kept, 0.0, er)
                he_im[start, at, :] = jnp.where(kept, 0.0, ei)
                hf_re[start, at, :] = jnp.where(kept, OMEGA * w_re, fr)
                hf_im[start, at, :] = jnp.where(kept, OMEGA * w_im, fi)

        first_lane = lanes == 0
        last_lane = lanes == LANES - 1
        turns = [GROUP * (j + half) for j in range(PER)]
        joined = place == (GROUP - 1) * half
        to_edge = jnp.where(half == 0, LANES - 1, 1)
        back_turns = [lax.rem(LANES - turn + to_edge, LANES) for turn in turns]
        taken = [
            lanes == lax.rem(turn + jnp.where(half == 0, LANES - 1, 0), LANES) for turn in turns
        ]

        def undamped(plane, tile):
            return plane < BAND + CX - PML and tile < 3

        def updated(w_re, w_im, t_re, t_im, er, ei, fr, fi):
            new_re = (1.0 - OMEGA) * w_re + fr
            new_im = (1.0 - OMEGA) * w_im + fi
            if ei is None:
                return new_re + er * t_re, new_im + er * t_im
            return new_re + (er * t_re - ei * t_im), new_im + (er * t_im + ei * t_re)

        def sweep(w, h, w_out, h_out):
            def centre_and_z(ref, part, plane, tile):
                base = 8 + 8 * tile
                return ref[part, plane, pl.ds(base, 8), :], (
                    ref[part, plane, pl.ds(base - 1, 8), :]
                    + ref[part, plane, pl.ds(base + 1, 8), :]
                )

            for tile in range(4):
                at = pl.ds(8 * tile, 8)
                for part in range(2):
                    both = [centre_and_z(h, part, s, tile) for s in range(STRIDE)]
                    below = [roll(value, GROUP) for value in both[-1]]
                    above = [roll(value, -GROUP) for value in both[0]]
                    both = [below] + both + [above]
                    for s in range(STRIDE):
                        q, near = stencil_parts(
                            both[s + 1][0], both[s][0] + both[s + 2][0],
                            both[s + 1][1], both[s][1] + both[s + 2][1],
                        )
                        hq[part, s, at, :] = q
                        hs[part, s, at, :] = jnp.where(joined, q, 0.0)
                        hr[part, s, at, :] = near

            for tile in range(4):
                at = pl.ds(8 * tile, 8)
                for part in range(2):
                    before, here = (zeros, zeros), centre_and_z(w, part, 1, tile)
                    for plane in range(EXT):
                        after = (zeros, zeros)
                        if plane + 1 < EXT:
                            after = centre_and_z(w, part, plane + 2, tile)
                        q, near = stencil_parts(
                            here[0], before[0] + after[0], here[1], before[1] + after[1]
                        )
                        mq[part, plane, at, :] = q
                        mr[part, plane, at, :] = near
                        before, here = here, after

            for tile in range(4):
                at = pl.ds(8 * tile, 8)
                base = 8 + 8 * tile
                joint = [[hq[part, s, at, :] for s in range(STRIDE)] for part in range(2)]
                for j in range(PER):
                    planes = range(STRIDE * j, STRIDE * (j + 1))
                    q = [[mq[part, plane, at, :] for part in range(2)] for plane in planes]
                    up = [[roll(value, -1) for value in pair] for pair in q]
                    down = [[roll(value, 1) for value in pair] for pair in q]
                    side = [
                        [
                            pltpu.roll(hs[part, s, at, :], back_turns[j], 1)
                            for part in range(2)
                        ]
                        for s in range(STRIDE)
                    ]
                    turned = [[pltpu.roll(value, turns[j], 1) for value in pair] for pair in q]
                    for n, plane in enumerate(planes):
                        total = [
                            jnp.where(last_lane, side[n][part], up[n][part])
                            + jnp.where(first_lane, side[n][part], down[n][part])
                            + mr[part, plane, at, :]
                            for part in range(2)
                        ]
                        for part in range(2):
                            joint[part][n] = jnp.where(taken[j], turned[n][part], joint[part][n])
                        new_re, new_im = updated(
                            w[0, plane + 1, pl.ds(base, 8), :], w[1, plane + 1, pl.ds(base, 8), :],
                            total[0], total[1],
                            e_re[plane, at, :], None if undamped(plane, tile) else e_im[plane, at, :],
                            f_re[plane, at, :], f_im[plane, at, :],
                        )
                        w_out[0, plane + 1, pl.ds(base, 8), :] = new_re
                        w_out[1, plane + 1, pl.ds(base, 8), :] = new_im

                for part in range(2):
                    for s in range(STRIDE):
                        hq[part, s, at, :] = joint[part][s]

            for tile in range(4):
                at = pl.ds(8 * tile, 8)
                base = 8 + 8 * tile
                total = [
                    [pair_sum(hq[part, s, at, :]) + hr[part, s, at, :] for part in range(2)]
                    for s in range(STRIDE)
                ]
                for s in range(STRIDE):
                    new_re, new_im = updated(
                        h[0, s, pl.ds(base, 8), :], h[1, s, pl.ds(base, 8), :],
                        total[s][0], total[s][1],
                        he_re[s, at, :], he_im[s, at, :],
                        hf_re[s, at, :], hf_im[s, at, :],
                    )
                    h_out[0, s, pl.ds(base, 8), :] = new_re
                    h_out[1, s, pl.ds(base, 8), :] = new_im

        def two_sweeps(turn, carry):
            sweep(w, h, w_next, h_next)
            sweep(w_next, h_next, w, h)
            return carry

        lax.fori_loop(0, SWEEPS // 2, two_sweeps, 0)
        for part in range(2):
            for x in range(CX):
                own[part, x] = w[part, x + BAND + 1, pl.ds(16, CZ), :]
            for s in range(STRIDE):
                beside[part, s] = h[part, s, pl.ds(8, 32), :]

    out[...] = own[...]
    for part in range(2):
        x_first[part, 0] = own[part, 0]
        x_first[part, 1] = beside[part, 0, pl.ds(8, CZ), :]
        x_last[part, 0] = own[part, CX - 1]
        x_last[part, 1] = beside[part, (CX - 1) % STRIDE, pl.ds(8, CZ), :]
        for face, z in ((z_first, 0), (z_last, CZ - 1)):
            face[part, pl.ds(24, 8), :] = jnp.zeros((8, LANES), jnp.float32)
            for x in range(CX):
                face[part, pl.ds(x + 1, 1), :] = own[part, x, pl.ds(z, 1), :]
            for s in range(STRIDE):
                face[part, pl.ds(SIDE_ROW + s, 1), :] = beside[part, s, pl.ds(8 + z, 1), :]


def face_kernel(keep, z_first, z_last, x_low, x_high, first_out, last_out):
    group = lax.broadcasted_iota(jnp.int32, (1, LANES), 1) // GROUP
    for face, out, z in ((z_first, first_out, 0), (z_last, last_out, CZ - 1)):
        out[...] = face[...]
        for part in range(2):
            row = pl.ds(z, 1)
            out[part, pl.ds(0, 1), :] = x_low[part, 0, row, :] * keep[0]
            out[part, pl.ds(CX + 1, 1), :] = x_high[part, 0, row, :] * keep[1]
            for s, ref, scale in ((STRIDE - 1, x_low, keep[0]), (0, x_high, keep[1])):
                at = pl.ds(SIDE_ROW + s, 1)
                to, turn = (0, -6 * GROUP) if s else (7, 6 * GROUP)
                out[part, at, :] = jnp.where(
                    group == to, roll(ref[part, 1, row, :] * scale, turn), face[part, at, :]
                )


def residual_kernel(
    info, keep, field, source, wave, beside, x_low, x_high, z_low, z_high,
    out, total, box, sides, mq, mr, hs,
):
    half = info[0]
    lanes = lane_ids()
    group = lanes // GROUP
    zeros = jnp.zeros((8, LANES), jnp.float32)
    for part in range(2):
        box[part, 0, pl.ds(8, CZ), :] = x_low[part, 0] * keep[0]
        box[part, CX + 1, pl.ds(8, CZ), :] = x_high[part, 0] * keep[1]
        for x in range(CX):
            box[part, x + 1, pl.ds(8, CZ), :] = field[part, x]
        for x in range(CX + 2):
            box[part, x, pl.ds(7, 1), :] = z_low[part, pl.ds(x, 1), :] * keep[2]
            box[part, x, pl.ds(8 + CZ, 1), :] = z_high[part, pl.ds(x, 1), :] * keep[3]
        for s in range(STRIDE):
            row = pl.ds(SIDE_ROW + s, 1)
            sides[part, s, pl.ds(7, 1), :] = z_low[part, row, :] * keep[2]
            sides[part, s, pl.ds(8 + CZ, 1), :] = z_high[part, row, :] * keep[3]
            for tile in range(3):
                value = beside[part, s, pl.ds(8 + 8 * tile, 8), :]
                rows = pl.ds(8 * tile, 8)
                if s == STRIDE - 1:
                    value = jnp.where(
                        group == 0, roll(x_low[part, 1, rows, :] * keep[0], -6 * GROUP), value
                    )
                if s == 0:
                    value = jnp.where(
                        group == 7, roll(x_high[part, 1, rows, :] * keep[1], 6 * GROUP), value
                    )
                sides[part, s, pl.ds(8 + 8 * tile, 8), :] = value

    def centre_and_z(ref, part, plane, tile):
        base = 8 + 8 * tile
        return ref[part, plane, pl.ds(base, 8), :], (
            ref[part, plane, pl.ds(base - 1, 8), :] + ref[part, plane, pl.ds(base + 1, 8), :]
        )

    joined = lanes % GROUP == (GROUP - 1) * half
    for part in range(2):
        for tile in range(3):
            at = pl.ds(8 * tile, 8)
            both = [centre_and_z(sides, part, s, tile) for s in range(STRIDE)]
            below = [roll(value, GROUP) for value in both[-1]]
            above = [roll(value, -GROUP) for value in both[0]]
            both = [below] + both + [above]
            for s in range(STRIDE):
                q, _ = stencil_parts(
                    both[s + 1][0], both[s][0] + both[s + 2][0],
                    both[s + 1][1], both[s][1] + both[s + 2][1],
                )
                hs[part, s, at, :] = jnp.where(joined, q, 0.0)

    for part in range(2):
        for tile in range(3):
            at = pl.ds(8 * tile, 8)
            before, here = centre_and_z(box, part, 0, tile), centre_and_z(box, part, 1, tile)
            for x in range(CX):
                after = centre_and_z(box, part, x + 2, tile)
                q, near = stencil_parts(
                    here[0], before[0] + after[0], here[1], before[1] + after[1]
                )
                mq[part, x, at, :] = q
                mr[part, x, at, :] = near
                before, here = here, after

    first_lane = lanes == 0
    last_lane = lanes == LANES - 1
    to_edge = jnp.where(half == 0, LANES - 1, 1)
    squares = [zeros] * 4
    for part in range(2):
        for tile in range(3):
            at = pl.ds(8 * tile, 8)
            for j in range(1, PER):
                turn = lax.rem(LANES - GROUP * (j + half) + to_edge, LANES)
                planes = range(STRIDE * (j - 1), STRIDE * j)
                q = [mq[part, x, at, :] for x in planes]
                up = [roll(value, -1) for value in q]
                down = [roll(value, 1) for value in q]
                side = [pltpu.roll(hs[part, s, at, :], turn, 1) for s in range(STRIDE)]
                for n, x in enumerate(planes):
                    y = jnp.where(last_lane, side[n], up[n]) + jnp.where(
                        first_lane, side[n], down[n]
                    )
                    gap = (
                        source[part, x, at, :]
                        - (5.0 - wave[x, at, :]) * field[part, x, at, :]
                        + 0.5 * (y + mr[part, x, at, :])
                    )
                    out[part, x, at, :] = gap
                    squares[n] = squares[n] + gap * gap
    total[...] = jnp.broadcast_to(jnp.sum(sum(squares[1:], squares[0])), total.shape)


def f32(*shape):
    return jax.ShapeDtypeStruct(shape, jnp.float32)


def ring(value, axis, by):
    size = lax.axis_size(axis)
    return lax.ppermute(value, axis, [(i, (i + by) % size) for i in range(size)])


def diagonal(value, by_x, by_z):
    size_x, size_z = lax.axis_size("gx"), lax.axis_size("gz")
    pairs = [
        (x * size_z + z, ((x + by_x) % size_x) * size_z + (z + by_z) % size_z)
        for x in range(size_x)
        for z in range(size_z)
    ]
    return lax.ppermute(value, ("gx", "gz"), pairs)


def swap(value):
    return lax.ppermute(value, "gy", [(0, 1), (1, 0)])


def on_device(source, iterate, wave_sq, front, pml_flags):
    size_x, size_z, size_y = lax.axis_size("gx"), lax.axis_size("gz"), lax.axis_size("gy")
    at_x, at_z, half = lax.axis_index("gx"), lax.axis_index("gz"), lax.axis_index("gy")
    active = (jnp.mod(at_x + at_z - front[0], size_z) == 0).astype(jnp.int32)
    info = jnp.stack([half.astype(jnp.int32), active])
    flag_bits = pml_flags[0, 0]
    as_float = lambda test: test.astype(jnp.float32)
    band_keep = jnp.stack(
        [
            as_float(at_x > 0),
            as_float(at_z > 0),
            as_float(flag_bits % 2),
            as_float(flag_bits // 2 % 2),
        ]
    )
    box_keep = jnp.stack(
        [
            as_float(at_x > 0),
            as_float(at_x < size_x - 1),
            as_float(at_z > 0),
            as_float(at_z < size_z - 1),
        ]
    )

    def call(kernel, outs, ins, name, scratch=(), place=VMEM, sems=0, limit=20 * MIB):
        scalars = sum(value.ndim == 1 for value in ins)
        return pl.pallas_call(
            kernel,
            out_shape=outs,
            in_specs=[SMEM] * scalars + [place] * (len(ins) - scalars),
            out_specs=jax.tree.map(lambda _: VMEM, outs),
            scratch_shapes=[pltpu.VMEM(shape, jnp.float32) for shape in scratch]
            + [pltpu.SemaphoreType.DMA((sems,))] * (sems > 0),
            compiler_params=pltpu.CompilerParams(vmem_limit_bytes=limit),
            name=name,
        )(*ins)

    x_band, z_band, corner = call(
        bands_kernel,
        (f32(LAYERS, CZ, LANES), f32(LAYERS * CX, LANES), f32(72, LANES)),
        (iterate, source, wave_sq),
        "bands",
        [(5, BAND, CZ, LANES), (5, CX, 8, LANES)],
        place=HBM,
        sems=15,
        limit=60 * MIB,
    )
    corner = diagonal(corner, 1, 1)
    x_band = ring(x_band, "gx", 1)
    z_band = ring(z_band, "gz", 1)
    low_tiles = (5, EXT, 8, LANES)
    halo = call(
        halo_kernel,
        f32(5, STRIDE, 32, LANES),
        (info, band_keep, iterate, source, wave_sq, x_band, z_band, corner),
        "pack_halo",
        [low_tiles],
    )
    halo = swap(halo)
    planes, packs = (EXT, 32, LANES), (STRIDE, 32, LANES)
    own = (2, CX, CZ, LANES)
    box_like, pack_like = (2, EXT + 2, 48, LANES), (2, STRIDE, 48, LANES)
    x_face, z_face = f32(2, 2, CZ, LANES), f32(2, 32, LANES)
    new, field, beside, x_first, x_last, z_first, z_last = call(
        relax_kernel,
        (f32(*own), f32(*own), f32(2, STRIDE, 32, LANES), x_face, x_face, z_face, z_face),
        (info, band_keep, iterate, source, wave_sq, x_band, z_band, corner, halo),
        "relax",
        [low_tiles, box_like, box_like]
        + [planes] * 4
        + [pack_like] * 2
        + [packs] * 4
        + [(2,) + packs] * 3
        + [(2,) + planes] * 2,
    )
    x_low = ring(x_last, "gx", 1)
    x_high = ring(x_first, "gx", -1)
    z_first, z_last = call(
        face_kernel, (z_face, z_face), (box_keep, z_first, z_last, x_low, x_high), "faces"
    )
    z_low = ring(z_last, "gz", 1)
    z_high = ring(z_first, "gz", -1)
    count = size_x * size_z * size_y
    residual, total = call(
        residual_kernel,
        (f32(*own), f32(count, LANES)),
        (info, box_keep, field, source, wave_sq, beside, x_low, x_high, z_low, z_high),
        "residual",
        [(2, CX + 2, 48, LANES), (2, STRIDE, 48, LANES), own, own, (2, STRIDE, CZ, LANES)],
    )
    parts = lax.all_to_all(total, ("gx", "gz", "gy"), 0, 0, tiled=True)
    cells = 2 * CX * CZ * LANES * count
    norm = jnp.sqrt(jnp.sum(parts, axis=0)[:1] / cells)
    return new, residual, norm


def solution(mesh):
    in_specs = (
        P(None, "gx", "gz", "gy"),
        P(None, "gx", "gz", "gy"),
        P("gx", "gz", "gy"),
        P(),
        P("gx", "gz"),
    )
    out_specs = (P(None, "gx", "gz", "gy"), P(None, "gx", "gz", "gy"), P())
    return jax.shard_map(
        on_device, mesh=mesh, in_specs=in_specs, out_specs=out_specs, check_vma=False
    )
```

time: 102 us -> 76.9 us (0.75); the launches traced: 102 us -> 77.6 us
  Pallas kernels: 39.1 us -> 7.51 us
  blocking collectives: 19.5 us -> 33.3 us
  local copies, waits for them, and re-layouts: 6.56 us -> 0.01 us
  starting transfers between devices: 15.5 us -> 16.9 us
    pallas_call x4 -> x5, Pallas kernels: 39.1 us -> 7.51 us  [call(): pl.pallas_call(kernel, out_shape=outs, in_specs=[SMEM] * scalars + [place...]
    all_to_all x1, blocking collectives: 19.5 us -> 33.3 us  [on_device(): parts = lax.all_to_all(total, ('gx', 'gz', 'gy'), 0, 0, tiled=True)]
    ppermute x1, waiting for transfers between devices: 9.25 us -> 4.78 us  [diagonal(): return lax.ppermute(value, ('gx', 'gz'), pairs)]
    ppermute x6, waiting for transfers between devices: 5.67 us -> 10 us  [ring(): lax.ppermute(value, axis, [(i, (i + by) % size) for i in range(size)])]
    slice x10 -> x0, local copies, waits for them, and re-layouts: 3.84 us -> none  [the longest x3 1.86 us: bands(): iterate[index]]
    ppermute x6, starting transfers between devices: 8.28 us -> 11 us  [ring(): lax.ppermute(value, axis, [(i, (i + by) % size) for i in range(size)])]
    ppermute x2 -> x1, starting transfers between devices: 4.45 us -> 2.35 us  [swap(): return lax.ppermute(value, 'gy', [(0, 1), (1, 0)])]
    unnamed x8 -> x6, local copies, waits for them, and re-layouts: 1.08 us -> 0.01 us
  transfers between devices with their start and end apart: 9 -> 8, of which waited for: 6 -> 6; matrix products, arithmetic and copies ran while one was open for 2% -> 0% of each run, Pallas kernels for 0% -> 0%
where the time goes in v1:
time: 76.9 us; the launch traced here: 77.6 us
  blocking collectives  33.3 us (43%)
  starting transfers between devices  16.9 us (22%)
  waiting for transfers between devices  16.1 us (21%)
  Pallas kernels  7.51 us (10%)
  between operations  3.27 us (4%)
    all_to_all x1, blocking collectives, on_device(): parts = lax.all_to_all(total, ('gx', 'gz', 'gy'), 0, 0, tiled=True)  33.3 us
    ppermute x6, starting transfers between devices, ring(): lax.ppermute(value, axis, [(i, (i + by) % size) for i in range(size)])  11 us
    ppermute x6, waiting for transfers between devices, ring(): lax.ppermute(value, axis, [(i, (i + by) % size) for i in range(size)])  10 us
    pallas_call x5, Pallas kernels, call(): pl.pallas_call(kernel, out_shape=outs, in_specs=[SMEM] * scalars + [place...  7.51 us
    ppermute x1, waiting for transfers between devices, diagonal(): return lax.ppermute(value, ('gx', 'gz'), pairs)  4.78 us
    ppermute x1, starting transfers between devices, diagonal(): return lax.ppermute(value, ('gx', 'gz'), pairs)  3.56 us
    ppermute x1, starting transfers between devices, swap(): return lax.ppermute(value, 'gy', [(0, 1), (1, 0)])  2.35 us
  transfers between devices with their start and end apart: 8, of which 6 were waited for; matrix products, arithmetic and copies ran while one was open for 0% of the time, Pallas kernels for 0%

profile of v1, /device:TPU:1, one launch (start us, length us, event | category | flops | bytes accessed | tf_op | source)
XLA Modules:
  0.0 77.6 jit_solution(4093518684454789330)
XLA Ops:
  0.7 2.1 %bands.1 = (f32[17,24,128]{2,1,0:T(8,128)}, f32[408,128]{1,0:T(8,128)}, f32[72,128]{1,0:T(8,128)}) custom-call(f32[2,24,24,128]{3,2,1,0:T(8,128)} %iterate.5, f32[2,24,24,128]{3,2,1,0:T(8,128)} %source.7, f32[24,24,128]{2,1,0:T(8,128)} %wave.7), custom_call_target="tpu_custom_call" | custom-call | tf_op jit(solution)/shard_map/bands/pallas_call | solution.py:538
  2.8 3.6 %collective-permute-start.2 = (f32[72,128]{1,0:T(8,128)}, f32[72,128]{1,0:T(8,128)S(1)}, u32[]{:S(2)}, u32[]{:S(2)}) collective-permute-start(f32[72,128]{1,0:T(8,128)} %get-tuple-element.19), channel_id=1, source_target_pairs={{0,18},{2,20},{4,22},{6,24},{8,26},{10,28},{12,30},{14,16},{16,34}... | collective-permute-start | bytes 110600 | tf_op jit(solution)/shard_map/ppermute | solution.py:505
  6.4 1.3 %collective-permute-start = (f32[17,24,128]{2,1,0:T(8,128)}, f32[17,24,128]{2,1,0:T(8,128)S(1)}, u32[]{:S(2)}, u32[]{:S(2)}) collective-permute-start(f32[17,24,128]{2,1,0:T(8,128)} %get-tuple-element.17), channel_id=1, source_target_pairs={{0,16},{16,32},{32,48},{48,64},{64,80},{80,96},{96,112},{112,128},... | collective-permute-start | bytes 626696 | tf_op jit(solution)/shard_map/ppermute | solution.py:495
  7.7 1.6 %collective-permute-start.1 = (f32[408,128]{1,0:T(8,128)}, f32[408,128]{1,0:T(8,128)S(1)}, u32[]{:S(2)}, u32[]{:S(2)}) collective-permute-start(f32[408,128]{1,0:T(8,128)} %get-tuple-element.18), channel_id=1, source_target_pairs={{0,2},{2,4},{4,6},{6,8},{8,10},{10,12},{12,14},{14,0},{1,3},{3,5},... | collective-permute-start | bytes 626696 | tf_op jit(solution)/shard_map/ppermute | solution.py:495
  10.7 0.1 pad_add_fusion.info
  10.7 0.1 pad_maximum_fusion.keep
  10.8 4.8 %collective-permute-done.2.corner = f32[72,128]{1,0:T(8,128)S(1)} collective-permute-done((f32[72,128]{1,0:T(8,128)}, f32[72,128]{1,0:T(8,128)S(1)}, u32[]{:S(2)}, u32[]{:S(2)}) %collective-permute-start.2) | collective-permute-done | bytes 36896 | tf_op jit(solution)/shard_map/ppermute | solution.py:505
  15.6 0.4 collective-permute-done.x_band
  16.0 1.2 %pack_halo.1 = f32[5,4,32,128]{3,2,1,0:T(8,128)S(1)} custom-call(s32[2]{0:T(128)S(1)} %pad_add_fusion.info, f32[4]{0:T(128)S(1)} %pad_maximum_fusion.keep, f32[2,24,24,128]{3,2,1,0:T(8,128)S(1)} %copy-done.1, f32[2,24,24,128]{3,2,1,0:T(8,128)S(1)} %copy-done, f32[24,24,128]{2,1,0:T(8,128)S(1)} %copy-done.2, f32[17,24,128]{2,1,0:T(8,128)S(1)} %collective-permute-done.x_band, ...), custom_call_target="tpu_custom_call" | custom-call | tf_op jit(solution)/shard_map/pack_halo/pallas_call | solution.py:538
  17.3 2.3 %collective-permute-start.3 = (f32[5,4,32,128]{3,2,1,0:T(8,128)S(1)}, f32[5,4,32,128]{3,2,1,0:T(8,128)S(1)}, u32[]{:S(2)}, u32[]{:S(2)}) collective-permute-start(f32[5,4,32,128]{3,2,1,0:T(8,128)S(1)} %pack_halo.1), channel_id=1, source_target_pairs={{0,1},{1,0},{2,3},{3,2},{4,5},{5,4},{6,7},{7,6},{8,9},{9,8},{10,11... | collective-permute-start | bytes 983048 | tf_op jit(solution)/shard_map/ppermute | solution.py:509
  19.6 1.3 %collective-permute-done.3.halo = f32[5,4,32,128]{3,2,1,0:T(8,128)S(1)} collective-permute-done((f32[5,4,32,128]{3,2,1,0:T(8,128)S(1)}, f32[5,4,32,128]{3,2,1,0:T(8,128)S(1)}, u32[]{:S(2)}, u32[]{:S(2)}) %collective-permute-start.3) | collective-permute-done | bytes 327712 | tf_op jit(solution)/shard_map/ppermute | solution.py:509
  20.9 1.5 %relax.1 = (f32[2,24,24,128]{3,2,1,0:T(8,128)}, f32[2,24,24,128]{3,2,1,0:T(8,128)S(1)}, f32[2,4,32,128]{3,2,1,0:T(8,128)S(1)}, f32[2,2,24,128]{3,2,1,0:T(8,128)S...) custom-call(s32[2]{0:T(128)S(1)} %pad_add_fusion.info, ...), custom_call_target="tpu_custom_call" | custom-call | tf_op jit(solution)/shard_map/relax/pallas_call | solution.py:538
  22.4 0.0 collective-permute-start.4
  22.4 4.8 %collective-permute-start.5 = (f32[2,2,24,128]{3,2,1,0:T(8,128)S(1)}, f32[2,2,24,128]{3,2,1,0:T(8,128)S(1)}, u32[]{:S(2)}, u32[]{:S(2)}) collective-permute-start(f32[2,2,24,128]{3,2,1,0:T(8,128)S(1)} %get-tuple-element.24), channel_id=1, source_target_pairs={{0,240},{16,0},{32,16},{48,32},{64,48},{80,64},{96,80},{112,96},{1... | collective-permute-start | bytes 147464 | tf_op jit(solution)/shard_map/ppermute | solution.py:495
  27.2 0.1 pad_maximum_fusion.1.keep
  27.2 1.4 %collective-permute-done.4.x_low = f32[2,2,24,128]{3,2,1,0:T(8,128)S(1)} collective-permute-done((f32[2,2,24,128]{3,2,1,0:T(8,128)S(1)}, f32[2,2,24,128]{3,2,1,0:T(8,128)S(1)}, u32[]{:S(2)}, u32[]{:S(2)}) %collective-permute-start.4) | collective-permute-done | bytes 49184 | tf_op jit(solution)/shard_map/ppermute | solution.py:495
  28.6 0.6 faces.1
  29.3 0.9 %collective-permute-start.6 = (f32[2,32,128]{2,1,0:T(8,128)S(1)}, f32[2,32,128]{2,1,0:T(8,128)S(1)}, u32[]{:S(2)}, u32[]{:S(2)}) collective-permute-start(f32[2,32,128]{2,1,0:T(8,128)S(1)} %get-tuple-element.27), channel_id=1, source_target_pairs={{0,2},{2,4},{4,6},{6,8},{8,10},{10,12},{12,14},{14,0},{1,3},{3,5},... | collective-permute-start | bytes 98312 | tf_op jit(solution)/shard_map/ppermute | solution.py:495
  30.1 2.4 %collective-permute-start.7 = (f32[2,32,128]{2,1,0:T(8,128)S(1)}, f32[2,32,128]{2,1,0:T(8,128)S(1)}, u32[]{:S(2)}, u32[]{:S(2)}) collective-permute-start(f32[2,32,128]{2,1,0:T(8,128)S(1)} %get-tuple-element.28), channel_id=1, source_target_pairs={{0,14},{2,0},{4,2},{6,4},{8,6},{10,8},{12,10},{14,12},{1,15},{3,1}... | collective-permute-start | bytes 98312 | tf_op jit(solution)/shard_map/ppermute | solution.py:495
  32.5 1.2 %collective-permute-done.6.z_low = f32[2,32,128]{2,1,0:T(8,128)S(1)} collective-permute-done((f32[2,32,128]{2,1,0:T(8,128)S(1)}, f32[2,32,128]{2,1,0:T(8,128)S(1)}, u32[]{:S(2)}, u32[]{:S(2)}) %collective-permute-start.6) | collective-permute-done | bytes 32800 | tf_op jit(solution)/shard_map/ppermute | solution.py:495
  33.8 7.0 %collective-permute-done.7.z_high = f32[2,32,128]{2,1,0:T(8,128)S(1)} collective-permute-done((f32[2,32,128]{2,1,0:T(8,128)S(1)}, f32[2,32,128]{2,1,0:T(8,128)S(1)}, u32[]{:S(2)}, u32[]{:S(2)}) %collective-permute-start.7) | collective-permute-done | bytes 32800 | tf_op jit(solution)/shard_map/ppermute | solution.py:495
  40.8 2.0 %residual.1 = (f32[2,24,24,128]{3,2,1,0:T(8,128)}, f32[256,128]{1,0:T(8,128)S(1)}) custom-call(s32[2]{0:T(128)S(1)} %pad_add_fusion.info, f32[4]{0:T(128)S(1)} %pad_maximum_fusion.1.keep, f32[2,24,24,128]{3,2,1,0:T(8,128)S(1)} %get-tuple-element.21.field, f32[2,24,24,128]{3,2,1,0:T(8,128)S(1)} %copy-done, f32[24,24,128]{2,1,0:T(8,128)S(1)} %copy-done.2, ...), custom_call_target="tpu_custom_call" | custom-call | tf_op jit(solution)/shard_map/residual/pallas_call | solution.py:538
  42.8 33.3 %all_to_all.9 = f32[256,1,128]{2,1,0:T(1,128)S(1)} all-to-all(f32[256,1,128]{2,1,0:T(1,128)S(1)} %bitcast.19), channel_id=1, replica_groups=mesh['gx'=16,'gz'=8,'gy'=2] {'gx','gz','gy'}, dimensions={0} | all-to-all | bytes 262144 | tf_op jit(solution)/shard_map/all_to_all | solution.py:602
  76.1 0.3 reduce_sum.9
  (8 shorter events, 0.0 us)
Async XLA Ops:
  0.6 15.4 %copy-start = (f32[2,24,24,128]{3,2,1,0:T(8,128)S(1)}, f32[2,24,24,128]{3,2,1,0:T(8,128)}, u32[]{:S(2)}) copy-start(f32[2,24,24,128]{3,2,1,0:T(8,128)} %source.7) | copy-start | bytes 1769476
  0.6 15.4 %copy-start.1 = (f32[2,24,24,128]{3,2,1,0:T(8,128)S(1)}, f32[2,24,24,128]{3,2,1,0:T(8,128)}, u32[]{:S(2)}) copy-start(f32[2,24,24,128]{3,2,1,0:T(8,128)} %iterate.5) | copy-start | bytes 1769476
  0.6 15.4 %copy-start.2 = (f32[24,24,128]{2,1,0:T(8,128)S(1)}, f32[24,24,128]{2,1,0:T(8,128)}, u32[]{:S(2)}) copy-start(f32[24,24,128]{2,1,0:T(8,128)} %wave.7) | copy-start | bytes 884740
  2.8 12.8 %collective-permute-start.2 = (f32[72,128]{1,0:T(8,128)}, f32[72,128]{1,0:T(8,128)S(1)}, u32[]{:S(2)}, u32[]{:S(2)}) collective-permute-start(f32[72,128]{1,0:T(8,128)} %get-tuple-element.19), channel_id=1, source_target_pairs={{0,18},{2,20},{4,22},{6,24},{8,26},{10,28},{12,30},{14,16},{16,34}... | collective-permute-start | bytes 110600 | tf_op jit(solution)/shard_map/ppermute | solution.py:505
  6.4 9.6 %collective-permute-start = (f32[17,24,128]{2,1,0:T(8,128)}, f32[17,24,128]{2,1,0:T(8,128)S(1)}, u32[]{:S(2)}, u32[]{:S(2)}) collective-permute-start(f32[17,24,128]{2,1,0:T(8,128)} %get-tuple-element.17), channel_id=1, source_target_pairs={{0,16},{16,32},{32,48},{48,64},{64,80},{80,96},{96,112},{112,128},... | collective-permute-start | bytes 626696 | tf_op jit(solution)/shard_map/ppermute | solution.py:495
  7.7 8.3 %collective-permute-start.1 = (f32[408,128]{1,0:T(8,128)}, f32[408,128]{1,0:T(8,128)S(1)}, u32[]{:S(2)}, u32[]{:S(2)}) collective-permute-start(f32[408,128]{1,0:T(8,128)} %get-tuple-element.18), channel_id=1, source_target_pairs={{0,2},{2,4},{4,6},{6,8},{8,10},{10,12},{12,14},{14,0},{1,3},{3,5},... | collective-permute-start | bytes 626696 | tf_op jit(solution)/shard_map/ppermute | solution.py:495
  17.3 3.6 %collective-permute-start.3 = (f32[5,4,32,128]{3,2,1,0:T(8,128)S(1)}, f32[5,4,32,128]{3,2,1,0:T(8,128)S(1)}, u32[]{:S(2)}, u32[]{:S(2)}) collective-permute-start(f32[5,4,32,128]{3,2,1,0:T(8,128)S(1)} %pack_halo.1), channel_id=1, source_target_pairs={{0,1},{1,0},{2,3},{3,2},{4,5},{5,4},{6,7},{7,6},{8,9},{9,8},{10,11... | collective-permute-start | bytes 983048 | tf_op jit(solution)/shard_map/ppermute | solution.py:509
  22.4 6.3 %collective-permute-start.4 = (f32[2,2,24,128]{3,2,1,0:T(8,128)S(1)}, f32[2,2,24,128]{3,2,1,0:T(8,128)S(1)}, u32[]{:S(2)}, u32[]{:S(2)}) collective-permute-start(f32[2,2,24,128]{3,2,1,0:T(8,128)S(1)} %get-tuple-element.23), channel_id=1, source_target_pairs={{0,16},{16,32},{32,48},{48,64},{64,80},{80,96},{96,112},{112,128},... | collective-permute-start | bytes 147464 | tf_op jit(solution)/shard_map/ppermute | solution.py:495
  22.4 6.2 %collective-permute-start.5 = (f32[2,2,24,128]{3,2,1,0:T(8,128)S(1)}, f32[2,2,24,128]{3,2,1,0:T(8,128)S(1)}, u32[]{:S(2)}, u32[]{:S(2)}) collective-permute-start(f32[2,2,24,128]{3,2,1,0:T(8,128)S(1)} %get-tuple-element.24), channel_id=1, source_target_pairs={{0,240},{16,0},{32,16},{48,32},{64,48},{80,64},{96,80},{112,96},{1... | collective-permute-start | bytes 147464 | tf_op jit(solution)/shard_map/ppermute | solution.py:495
  29.3 4.5 %collective-permute-start.6 = (f32[2,32,128]{2,1,0:T(8,128)S(1)}, f32[2,32,128]{2,1,0:T(8,128)S(1)}, u32[]{:S(2)}, u32[]{:S(2)}) collective-permute-start(f32[2,32,128]{2,1,0:T(8,128)S(1)} %get-tuple-element.27), channel_id=1, source_target_pairs={{0,2},{2,4},{4,6},{6,8},{8,10},{10,12},{12,14},{14,0},{1,3},{3,5},... | collective-permute-start | bytes 98312 | tf_op jit(solution)/shard_map/ppermute | solution.py:495
  30.1 10.6 %collective-permute-start.7 = (f32[2,32,128]{2,1,0:T(8,128)S(1)}, f32[2,32,128]{2,1,0:T(8,128)S(1)}, u32[]{:S(2)}, u32[]{:S(2)}) collective-permute-start(f32[2,32,128]{2,1,0:T(8,128)S(1)} %get-tuple-element.28), channel_id=1, source_target_pairs={{0,14},{2,0},{4,2},{6,4},{8,6},{10,8},{12,10},{14,12},{1,15},{3,1}... | collective-permute-start | bytes 98312 | tf_op jit(solution)/shard_map/ppermute | solution.py:495

commit v2 on v1

--- a/solution.py
+++ b/solution.py
@@ -18,6 +18,7 @@
 GROUP = 16
 HALO = 11
 STRIDE = 4
+MOVERS = (EXT // STRIDE + 1) // 2
 LAYERS = 2 * BAND + 3 * (BAND - 1)
 PER = EXT // STRIDE
 
@@ -109,10 +110,10 @@
     return ref[x, rows, :] if index is None else ref[index, x, rows, :]
 
 
-def fill_low_tiles(low, z_band, corner, keep_x, keep_z):
+def fill_low_tiles(low, z_band, corner, keep_x, keep_z, count=5):
     keep_both = keep_x * keep_z
     low[...] = jnp.zeros_like(low)
-    for field in range(5):
+    for field in range(count):
         first = layers(field)
         depth = BAND - first
         for plane in range(EXT):
@@ -146,13 +147,71 @@
                 out[field, start, pl.ds(8 * tile, 8), :] = packed
 
 
+def coefficients(wave_sq, s_re, s_im, sigma):
+    diag = 5.0 - wave_sq
+    scale = (0.5 * OMEGA) / (diag * diag + sigma * sigma)
+    er = diag * scale
+    ei = -sigma * scale
+    return er, ei, 2.0 * (er * s_re - ei * s_im), 2.0 * (er * s_im + ei * s_re)
+
+
+def sigma_z(tile, flag):
+    if tile == 0:
+        return jnp.zeros((8, LANES), jnp.float32)
+    z = (row_ids() + 8 * (tile - 1)).astype(jnp.float32)
+    ramp = jnp.maximum(z - (CZ - PML) + 1.0, 0.0) / PML
+    return SIGMA * ramp * ramp * flag
+
+
+def weights_kernel(
+    info, keep, iterate, source, wave, x_band, z_band, corner,
+    e_re, e_im, f_re, f_im, movers, low,
+):
+    half = info[0]
+    keep_x = keep[0]
+    lane = lax.broadcasted_iota(jnp.int32, (16, 2 * LANES), 1)
+    row = lax.broadcasted_iota(jnp.int32, (16, 2 * LANES), 0)
+    ends = lane % LANES == (LANES - 1) * (1 - half)
+    for m in range(MOVERS):
+        start = GROUP * (2 * m + lane // LANES) + (GROUP - 1) * half
+        for first in range(0, 2 * LANES, 16):
+            hit = ends & ((row + first) % LANES == start)
+            movers[m, pl.ds(first, 16), :] = hit.astype(jnp.float32).astype(jnp.bfloat16)
+    fill_low_tiles(low, z_band, corner, keep_x, keep[1])
+    fields = [(iterate, 0), (iterate, 1), (source, 0), (source, 1), (wave, None)]
+    zeros = jnp.zeros((8, LANES), jnp.float32)
+    kept_rows = row_ids() < 5
+    for tile in range(4):
+        along_z = sigma_z(tile, keep[3])
+        at = pl.ds(8 * tile, 8)
+        for plane in range(EXT):
+            values = [tile_of(fields, x_band, low, f, plane, tile, keep_x) for f in range(5)]
+            w_re, w_im, s_re, s_im, wave_sq = values
+            if plane == 0:
+                er, ei, fr, fi = zeros, zeros, OMEGA * w_re, OMEGA * w_im
+            else:
+                ramp = max(plane - BAND - (CX - PML) + 1.0, 0.0) / PML
+                sigma = along_z + SIGMA * ramp * ramp * keep[2]
+                er, ei, fr, fi = coefficients(wave_sq, s_re, s_im, sigma)
+                if tile == 0:
+                    er = jnp.where(kept_rows, 0.0, er)
+                    ei = jnp.where(kept_rows, 0.0, ei)
+                    fr = jnp.where(kept_rows, OMEGA * w_re, fr)
+                    fi = jnp.where(kept_rows, OMEGA * w_im, fi)
+            e_re[plane, at, :] = er
+            e_im[plane, at, :] = ei
+            f_re[plane, at, :] = fr
+            f_im[plane, at, :] = fi
+
+
 def relax_kernel(
-    info, keep, iterate, source, wave, x_band, z_band, corner, halo,
-    out, own, beside, x_first, x_last, z_first, z_last,
-    low, w, w_next, e_re, e_im, f_re, f_im, h, h_next, he_re, he_im, hf_re, hf_im, hq, hr, hs, mq, mr,
+    info, keep, iterate, x_band, z_band, corner, e_re, e_im, f_re, f_im, movers, halo,
+    own, beside, x_a, x_b, z_first, z_last,
+    low, w, w_next, h, h_next, he_re, he_im, hf_re, hf_im, hq, hr, hs, mq, mr, sides,
 ):
     half = info[0]
     active = info[1]
+    odd = info[2]
 
     @pl.when(active == 0)
     def _():
@@ -162,67 +221,33 @@
     @pl.when(active == 1)
     def _():
         keep_x = keep[0]
-        flag_x = keep[2]
-        flag_z = keep[3]
-        fill_low_tiles(low, z_band, corner, keep_x, keep[1])
-        fields = [(iterate, 0), (iterate, 1), (source, 0), (source, 1), (wave, None)]
+        fill_low_tiles(low, z_band, corner, keep_x, keep[1], 2)
+        fields = [(iterate, 0), (iterate, 1)]
         lanes = lane_ids()
         rows = row_ids()
         place = lanes % GROUP
         group = lanes // GROUP
         least = (GROUP - HALO) * half
         zeros = jnp.zeros((8, LANES), jnp.float32)
-
         for scratch in (w, w_next, h, h_next):
             scratch[...] = jnp.zeros_like(scratch)
 
-        def coefficients(wave_sq, s_re, s_im, sigma):
-            diag = 5.0 - wave_sq
-            scale = (0.5 * OMEGA) / (diag * diag + sigma * sigma)
-            er = diag * scale
-            ei = -sigma * scale
-            return er, ei, 2.0 * (er * s_re - ei * s_im), 2.0 * (er * s_im + ei * s_re)
-
-        def sigma_z(tile):
-            if tile == 0:
-                return zeros
-            z = (rows + 8 * (tile - 1)).astype(jnp.float32)
-            ramp = jnp.maximum(z - (CZ - PML) + 1.0, 0.0) / PML
-            return SIGMA * ramp * ramp * flag_z
-
         for tile in range(4):
-            along_z = sigma_z(tile)
+            along_z = sigma_z(tile, keep[3])
             kept_rows = rows < 5
+            at, inner = pl.ds(8 * tile, 8), pl.ds(8 + 8 * tile, 8)
             for plane in range(EXT):
-                values = [tile_of(fields, x_band, low, f, plane, tile, keep_x) for f in range(5)]
-                w_re, w_im, s_re, s_im, wave_sq = values
-                at = pl.ds(8 * tile, 8)
-                w[0, plane + 1, pl.ds(8 + 8 * tile, 8), :] = w_re
-                w[1, plane + 1, pl.ds(8 + 8 * tile, 8), :] = w_im
-                if plane == 0:
-                    er, ei, fr, fi = zeros, zeros, OMEGA * w_re, OMEGA * w_im
-                else:
-                    ramp = max(plane - BAND - (CX - PML) + 1.0, 0.0) / PML
-                    sigma = along_z + SIGMA * ramp * ramp * flag_x
-                    er, ei, fr, fi = coefficients(wave_sq, s_re, s_im, sigma)
-                    if tile == 0:
-                        er = jnp.where(kept_rows, 0.0, er)
-                        ei = jnp.where(kept_rows, 0.0, ei)
-                        fr = jnp.where(kept_rows, OMEGA * w_re, fr)
-                        fi = jnp.where(kept_rows, OMEGA * w_im, fi)
-                e_re[plane, at, :] = er
-                e_im[plane, at, :] = ei
-                f_re[plane, at, :] = fr
-                f_im[plane, at, :] = fi
-
+                for part in range(2):
+                    w[part, plane + 1, inner, :] = tile_of(
+                        fields, x_band, low, part, plane, tile, keep_x
+                    )
             for start in range(STRIDE):
-                at = pl.ds(8 * tile, 8)
                 w_re, w_im, s_re, s_im, wave_sq = [halo[f, start, at, :] for f in range(5)]
-                h[0, start, pl.ds(8 + 8 * tile, 8), :] = w_re
-                h[1, start, pl.ds(8 + 8 * tile, 8), :] = w_im
+                h[0, start, inner, :] = w_re
+                h[1, start, inner, :] = w_im
                 x = (STRIDE * group + start - BAND).astype(jnp.float32)
                 ramp = jnp.maximum(x - (CX - PML) + 1.0, 0.0) / PML
-                sigma = along_z + SIGMA * ramp * ramp * flag_x
+                sigma = along_z + SIGMA * ramp * ramp * keep[2]
                 er, ei, fr, fi = coefficients(wave_sq, s_re, s_im, sigma)
                 kept = (place < least) | (place >= least + HALO) | (group == PER)
                 if start == 0:
@@ -237,9 +262,6 @@
         first_lane = lanes == 0
         last_lane = lanes == LANES - 1
         turns = [GROUP * (j + half) for j in range(PER)]
-        joined = place == (GROUP - 1) * half
-        to_edge = jnp.where(half == 0, LANES - 1, 1)
-        back_turns = [lax.rem(LANES - turn + to_edge, LANES) for turn in turns]
         taken = [
             lanes == lax.rem(turn + jnp.where(half == 0, LANES - 1, 0), LANES) for turn in turns
         ]
@@ -275,8 +297,18 @@
                             both[s + 1][1], both[s][1] + both[s + 2][1],
                         )
                         hq[part, s, at, :] = q
-                        hs[part, s, at, :] = jnp.where(joined, q, 0.0)
+                        hs[pl.ds(32 * (STRIDE * part + s) + 8 * tile, 8), :] = q
                         hr[part, s, at, :] = near
+
+            value = hs[...]
+            head = value.astype(jnp.bfloat16)
+            tail = (value - head.astype(jnp.float32)).astype(jnp.bfloat16)
+            both = jnp.concatenate([head, tail], 1)
+            for m in range(MOVERS):
+                moved = jnp.dot(both, movers[m], preferred_element_type=jnp.float32)
+                sides[2 * m] = moved[:, :LANES]
+                if 2 * m + 1 < PER:
+                    sides[2 * m + 1] = moved[:, LANES:]
 
             for tile in range(4):
                 at = pl.ds(8 * tile, 8)
@@ -304,7 +336,7 @@
                     down = [[roll(value, 1) for value in pair] for pair in q]
                     side = [
                         [
-                            pltpu.roll(hs[part, s, at, :], back_turns[j], 1)
+                            sides[j, pl.ds(32 * (STRIDE * part + s) + 8 * tile, 8), :]
                             for part in range(2)
                         ]
                         for s in range(STRIDE)
@@ -361,12 +393,10 @@
             for s in range(STRIDE):
                 beside[part, s] = h[part, s, pl.ds(8, 32), :]
 
-    out[...] = own[...]
     for part in range(2):
-        x_first[part, 0] = own[part, 0]
-        x_first[part, 1] = beside[part, 0, pl.ds(8, CZ), :]
-        x_last[part, 0] = own[part, CX - 1]
-        x_last[part, 1] = beside[part, (CX - 1) % STRIDE, pl.ds(8, CZ), :]
+        for face, side in ((x_a, 1 - odd), (x_b, odd)):
+            face[part, 0] = own[part, (CX - 1) * side]
+            face[part, 1] = beside[part, (STRIDE - 1) * side, pl.ds(8, CZ), :]
         for face, z in ((z_first, 0), (z_last, CZ - 1)):
             face[part, pl.ds(24, 8), :] = jnp.zeros((8, LANES), jnp.float32)
             for x in range(CX):
@@ -375,33 +405,48 @@
                 face[part, pl.ds(SIDE_ROW + s, 1), :] = beside[part, s, pl.ds(8 + z, 1), :]
 
 
-def face_kernel(keep, z_first, z_last, x_low, x_high, first_out, last_out):
+def face_kernel(info, keep, z_first, z_last, x_a, x_b, a_out, b_out, first, last):
+    odd_x = info[2] == 1
+    odd_z = info[3] == 1
     group = lax.broadcasted_iota(jnp.int32, (1, LANES), 1) // GROUP
-    for face, out, z in ((z_first, first_out, 0), (z_last, last_out, CZ - 1)):
+    for face, out, z in ((z_first, first, 0), (z_last, last, CZ - 1)):
         out[...] = face[...]
         for part in range(2):
-            row = pl.ds(z, 1)
-            out[part, pl.ds(0, 1), :] = x_low[part, 0, row, :] * keep[0]
-            out[part, pl.ds(CX + 1, 1), :] = x_high[part, 0, row, :] * keep[1]
-            for s, ref, scale in ((STRIDE - 1, x_low, keep[0]), (0, x_high, keep[1])):
+            a, b = [[ref[part, n, pl.ds(z, 1), :] for n in range(2)] for ref in (x_a, x_b)]
+            low = [jnp.where(odd_x, a[n], b[n]) * keep[0] for n in range(2)]
+            high = [jnp.where(odd_x, b[n], a[n]) * keep[1] for n in range(2)]
+            out[part, pl.ds(0, 1), :] = low[0]
+            out[part, pl.ds(CX + 1, 1), :] = high[0]
+            for s, value, to, turn in (
+                (STRIDE - 1, low[1], 0, -6 * GROUP), (0, high[1], 7, 6 * GROUP)
+            ):
                 at = pl.ds(SIDE_ROW + s, 1)
-                to, turn = (0, -6 * GROUP) if s else (7, 6 * GROUP)
-                out[part, at, :] = jnp.where(
-                    group == to, roll(ref[part, 1, row, :] * scale, turn), face[part, at, :]
-                )
+                out[part, at, :] = jnp.where(group == to, roll(value, turn), face[part, at, :])
+    a_out[...] = jnp.where(odd_z, first[...], last[...])
+    b_out[...] = jnp.where(odd_z, last[...], first[...])
 
 
 def residual_kernel(
-    info, keep, field, source, wave, beside, x_low, x_high, z_low, z_high,
-    out, total, box, sides, mq, mr, hs,
+    info, keep, field, source, wave, beside, x_a, x_b, z_a, z_b,
+    out, total, box, sides, mq, mr, hs, z_low, z_high,
 ):
     half = info[0]
+    odd_x = info[2] == 1
+    odd_z = info[3] == 1
+    z_low[...] = jnp.where(odd_z, z_a[...], z_b[...])
+    z_high[...] = jnp.where(odd_z, z_b[...], z_a[...])
+
+    def x_sides(part, n, rows):
+        a, b = x_a[part, n, rows, :], x_b[part, n, rows, :]
+        return jnp.where(odd_x, a, b) * keep[0], jnp.where(odd_x, b, a) * keep[1]
+
     lanes = lane_ids()
     group = lanes // GROUP
     zeros = jnp.zeros((8, LANES), jnp.float32)
     for part in range(2):
-        box[part, 0, pl.ds(8, CZ), :] = x_low[part, 0] * keep[0]
-        box[part, CX + 1, pl.ds(8, CZ), :] = x_high[part, 0] * keep[1]
+        low, high = x_sides(part, 0, pl.ds(0, CZ))
+        box[part, 0, pl.ds(8, CZ), :] = low
+        box[part, CX + 1, pl.ds(8, CZ), :] = high
         for x in range(CX):
             box[part, x + 1, pl.ds(8, CZ), :] = field[part, x]
         for x in range(CX + 2):
@@ -413,15 +458,11 @@
             sides[part, s, pl.ds(8 + CZ, 1), :] = z_high[part, row, :] * keep[3]
             for tile in range(3):
                 value = beside[part, s, pl.ds(8 + 8 * tile, 8), :]
-                rows = pl.ds(8 * tile, 8)
+                low, high = x_sides(part, 1, pl.ds(8 * tile, 8))
                 if s == STRIDE - 1:
-                    value = jnp.where(
-                        group == 0, roll(x_low[part, 1, rows, :] * keep[0], -6 * GROUP), value
-                    )
+                    value = jnp.where(group == 0, roll(low, -6 * GROUP), value)
                 if s == 0:
-                    value = jnp.where(
-                        group == 7, roll(x_high[part, 1, rows, :] * keep[1], 6 * GROUP), value
-                    )
+                    value = jnp.where(group == 7, roll(high, 6 * GROUP), value)
                 sides[part, s, pl.ds(8 + 8 * tile, 8), :] = value
 
     def centre_and_z(ref, part, plane, tile):
@@ -495,6 +536,15 @@
     return lax.ppermute(value, axis, [(i, (i + by) % size) for i in range(size)])
 
 
+def pairs(value, axis, first):
+    size = lax.axis_size(axis)
+    moves = []
+    for i in range(first, size, 2):
+        j = (i + 1) % size
+        moves += [(i, j), (j, i)]
+    return lax.ppermute(value, axis, moves)
+
+
 def diagonal(value, by_x, by_z):
     size_x, size_z = lax.axis_size("gx"), lax.axis_size("gz")
     pairs = [
@@ -513,7 +563,7 @@
     size_x, size_z, size_y = lax.axis_size("gx"), lax.axis_size("gz"), lax.axis_size("gy")
     at_x, at_z, half = lax.axis_index("gx"), lax.axis_index("gz"), lax.axis_index("gy")
     active = (jnp.mod(at_x + at_z - front[0], size_z) == 0).astype(jnp.int32)
-    info = jnp.stack([half.astype(jnp.int32), active])
+    info = jnp.stack([half, active, at_x % 2, at_z % 2]).astype(jnp.int32)
     flag_bits = pml_flags[0, 0]
     as_float = lambda test: test.astype(jnp.float32)
     band_keep = jnp.stack(
@@ -533,7 +583,7 @@
         ]
     )
 
-    def call(kernel, outs, ins, name, scratch=(), place=VMEM, sems=0, limit=20 * MIB):
+    def call(kernel, outs, ins, name, scratch=(), place=VMEM, sems=0):
         scalars = sum(value.ndim == 1 for value in ins)
         return pl.pallas_call(
             kernel,
@@ -542,19 +592,18 @@
             out_specs=jax.tree.map(lambda _: VMEM, outs),
             scratch_shapes=[pltpu.VMEM(shape, jnp.float32) for shape in scratch]
             + [pltpu.SemaphoreType.DMA((sems,))] * (sems > 0),
-            compiler_params=pltpu.CompilerParams(vmem_limit_bytes=limit),
+            compiler_params=pltpu.CompilerParams(vmem_limit_bytes=20 * MIB),
             name=name,
         )(*ins)
 
     x_band, z_band, corner = call(
         bands_kernel,
         (f32(LAYERS, CZ, LANES), f32(LAYERS * CX, LANES), f32(72, LANES)),
-        (iterate, source, wave_sq),
+        [pltpu.with_memory_space_constraint(v, pltpu.HBM) for v in (iterate, source, wave_sq)],
         "bands",
         [(5, BAND, CZ, LANES), (5, CX, 8, LANES)],
         place=HBM,
         sems=15,
-        limit=60 * MIB,
     )
     corner = diagonal(corner, 1, 1)
     x_band = ring(x_band, "gx", 1)
@@ -570,34 +619,47 @@
     halo = swap(halo)
     planes, packs = (EXT, 32, LANES), (STRIDE, 32, LANES)
     own = (2, CX, CZ, LANES)
+    in_vmem = pltpu.VMEM(own, jnp.float32)
     box_like, pack_like = (2, EXT + 2, 48, LANES), (2, STRIDE, 48, LANES)
     x_face, z_face = f32(2, 2, CZ, LANES), f32(2, 32, LANES)
-    new, field, beside, x_first, x_last, z_first, z_last = call(
+    weights = call(
+        weights_kernel,
+        (f32(*planes),) * 4
+        + (jax.ShapeDtypeStruct((MOVERS, 2 * LANES, 2 * LANES), jnp.bfloat16),),
+        (info, band_keep, iterate, source, wave_sq, x_band, z_band, corner),
+        "weights",
+        [low_tiles],
+    )
+    new, beside, x_a, x_b, z_first, z_last = call(
         relax_kernel,
-        (f32(*own), f32(*own), f32(2, STRIDE, 32, LANES), x_face, x_face, z_face, z_face),
-        (info, band_keep, iterate, source, wave_sq, x_band, z_band, corner, halo),
+        (in_vmem, f32(2, STRIDE, 32, LANES), x_face, x_face, z_face, z_face),
+        (info, band_keep, iterate, x_band, z_band, corner, *weights, halo),
         "relax",
-        [low_tiles, box_like, box_like]
-        + [planes] * 4
+        [(2,) + low_tiles[1:], box_like, box_like]
         + [pack_like] * 2
         + [packs] * 4
-        + [(2,) + packs] * 3
-        + [(2,) + planes] * 2,
-    )
-    x_low = ring(x_last, "gx", 1)
-    x_high = ring(x_first, "gx", -1)
-    z_first, z_last = call(
-        face_kernel, (z_face, z_face), (box_keep, z_first, z_last, x_low, x_high), "faces"
-    )
-    z_low = ring(z_last, "gz", 1)
-    z_high = ring(z_first, "gz", -1)
+        + [(2,) + packs] * 2
+        + [(2 * STRIDE * 32, LANES)]
+        + [(2,) + planes] * 2
+        + [(PER, 2 * STRIDE * 32, LANES)],
+    )
+    x_a, x_b = pairs(x_a, "gx", 0), pairs(x_b, "gx", 1)
+    z_a, z_b = call(
+        face_kernel,
+        (z_face, z_face),
+        (info, box_keep, z_first, z_last, x_a, x_b),
+        "faces",
+        [z_face.shape] * 2,
+    )
+    z_a, z_b = pairs(z_a, "gz", 0), pairs(z_b, "gz", 1)
     count = size_x * size_z * size_y
     residual, total = call(
         residual_kernel,
-        (f32(*own), f32(count, LANES)),
-        (info, box_keep, field, source, wave_sq, beside, x_low, x_high, z_low, z_high),
+        (in_vmem, f32(count, LANES)),
+        (info, box_keep, new, source, wave_sq, beside, x_a, x_b, z_a, z_b),
         "residual",
-        [(2, CX + 2, 48, LANES), (2, STRIDE, 48, LANES), own, own, (2, STRIDE, CZ, LANES)],
+        [(2, CX + 2, 48, LANES), (2, STRIDE, 48, LANES), own, own, (2, STRIDE, CZ, LANES)]
+        + [z_face.shape] * 2,
     )
     parts = lax.all_to_all(total, ("gx", "gz", "gy"), 0, 0, tiled=True)
     cells = 2 * CX * CZ * LANES * count

time: 76.9 us -> 70.8 us (0.921); the launches traced: 77.6 us -> 70.3 us
  blocking collectives: 33.3 us -> 0 us
  starting transfers between devices: 16.9 us -> 31.2 us
  waiting for transfers between devices: 16.1 us -> 26.6 us
  local copies, waits for them, and re-layouts: 0.01 us -> 1.64 us
    all_to_all x1 -> x0, blocking collectives: 33.3 us -> none  [on_device(): parts = lax.all_to_all(total, ('gx', 'gz', 'gy'), 0, 0, tiled=True)]
    ppermute x0 -> x4, starting transfers between devices: none -> 11.8 us  [pairs(): return lax.ppermute(value, axis, moves)]
    all_to_all x0 -> x1, waiting for transfers between devices: none -> 11.3 us  [on_device(): parts = lax.all_to_all(total, ('gx', 'gz', 'gy'), 0, 0, tiled=True)]
    all_to_all x0 -> x1, starting transfers between devices: none -> 10.6 us  [on_device(): parts = lax.all_to_all(total, ('gx', 'gz', 'gy'), 0, 0, tiled=True)]
    ppermute x0 -> x4, waiting for transfers between devices: none -> 10.2 us  [pairs(): return lax.ppermute(value, axis, moves)]
    ppermute x6 -> x2, waiting for transfers between devices: 10 us -> 0.41 us  [ring(): lax.ppermute(value, axis, [(i, (i + by) % size) for i in range(size)])]
    ppermute x6 -> x2, starting transfers between devices: 11 us -> 2.93 us  [ring(): lax.ppermute(value, axis, [(i, (i + by) % size) for i in range(size)])]
    unnamed x6 -> x8, local copies, waits for them, and re-layouts: 0.01 us -> 1.64 us
  transfers between devices with their start and end apart: 8 -> 9, of which waited for: 6 -> 8; matrix products, arithmetic and copies ran while one was open for 0% -> 3% of each run, Pallas kernels for 0% -> 2%
where the time goes in v2:
time: 70.8 us; the launch traced here: 70.3 us
  starting transfers between devices  31.2 us (44%)
  waiting for transfers between devices  26.6 us (38%)
  Pallas kernels  6.96 us (10%)
  between operations  3.3 us (5%)
  local copies, waits for them, and re-layouts  1.64 us (2%)
    ppermute x4, starting transfers between devices, pairs(): return lax.ppermute(value, axis, moves)  11.8 us
    all_to_all x1, waiting for transfers between devices, on_device(): parts = lax.all_to_all(total, ('gx', 'gz', 'gy'), 0, 0, tiled=True)  11.3 us
    all_to_all x1, starting transfers between devices, on_device(): parts = lax.all_to_all(total, ('gx', 'gz', 'gy'), 0, 0, tiled=True)  10.6 us
    ppermute x4, waiting for transfers between devices, pairs(): return lax.ppermute(value, axis, moves)  10.2 us
    pallas_call x6, Pallas kernels, call(): pl.pallas_call(kernel, out_shape=outs, in_specs=[SMEM] * scalars + [place...  6.96 us
    ppermute x1, waiting for transfers between devices, diagonal(): return lax.ppermute(value, ('gx', 'gz'), pairs)  4.56 us
    ppermute x1, starting transfers between devices, diagonal(): return lax.ppermute(value, ('gx', 'gz'), pairs)  3.56 us
    ppermute x2, starting transfers between devices, ring(): lax.ppermute(value, axis, [(i, (i + by) % size) for i in range(size)])  2.93 us
  transfers between devices with their start and end apart: 9, of which 8 were waited for; matrix products, arithmetic and copies ran while one was open for 3% of the time, Pallas kernels for 2%

profile of v2, /device:TPU:1, one launch (start us, length us, event | category | flops | bytes accessed | tf_op | source)
XLA Modules:
  0.0 70.3 jit_solution(6212028551603628132)
XLA Ops:
  0.7 1.4 %bands.1 = (f32[17,24,128]{2,1,0:T(8,128)S(1)}, f32[408,128]{1,0:T(8,128)S(1)}, f32[72,128]{1,0:T(8,128)S(1)}) custom-call(f32[2,24,24,128]{3,2,1,0:T(8,128)} %iterate.7, f32[2,24,24,128]{3,2,1,0:T(8,128)} %source.7, f32[24,24,128]{2,1,0:T(8,128)} %wave.7), custom_call_target="tpu_custom_call" | custom-call | tf_op jit(solution)/shard_map/bands/pallas_call | solution.py:588
  2.1 3.6 %collective-permute-start.2 = (f32[72,128]{1,0:T(8,128)S(1)}, f32[72,128]{1,0:T(8,128)S(1)}, u32[]{:S(2)}, u32[]{:S(2)}) collective-permute-start(f32[72,128]{1,0:T(8,128)S(1)} %get-tuple-element.23), channel_id=1, source_target_pairs={{0,18},{2,20},{4,22},{6,24},{8,26},{10,28},{12,30},{14,16},{16,34}... | collective-permute-start | bytes 110600 | tf_op jit(solution)/shard_map/ppermute | solution.py:555
  5.6 1.3 %collective-permute-start = (f32[17,24,128]{2,1,0:T(8,128)S(1)}, f32[17,24,128]{2,1,0:T(8,128)S(1)}, u32[]{:S(2)}, u32[]{:S(2)}) collective-permute-start(f32[17,24,128]{2,1,0:T(8,128)S(1)} %get-tuple-element.21), channel_id=1, source_target_pairs={{0,16},{16,32},{32,48},{48,64},{64,80},{80,96},{96,112},{112,128},... | collective-permute-start | bytes 626696 | tf_op jit(solution)/shard_map/ppermute | solution.py:536
  6.9 1.6 %collective-permute-start.1 = (f32[408,128]{1,0:T(8,128)S(1)}, f32[408,128]{1,0:T(8,128)S(1)}, u32[]{:S(2)}, u32[]{:S(2)}) collective-permute-start(f32[408,128]{1,0:T(8,128)S(1)} %get-tuple-element.22), channel_id=1, source_target_pairs={{0,2},{2,4},{4,6},{6,8},{8,10},{10,12},{12,14},{14,0},{1,3},{3,5},... | collective-permute-start | bytes 626696 | tf_op jit(solution)/shard_map/ppermute | solution.py:536
  10.1 4.6 %collective-permute-done.2.corner = f32[72,128]{1,0:T(8,128)S(1)} collective-permute-done((f32[72,128]{1,0:T(8,128)S(1)}, f32[72,128]{1,0:T(8,128)S(1)}, u32[]{:S(2)}, u32[]{:S(2)}) %collective-permute-start.2) | collective-permute-done | bytes 36896 | tf_op jit(solution)/shard_map/ppermute | solution.py:555
  14.7 0.4 collective-permute-done.x_band
  15.1 1.2 %pack_halo.1 = f32[5,4,32,128]{3,2,1,0:T(8,128)S(1)} custom-call(s32[4]{0:T(128)S(1)} %pad_add_fusion.info, f32[4]{0:T(128)S(1)} %pad_maximum_fusion.keep, f32[2,24,24,128]{3,2,1,0:T(8,128)S(1)} %copy-done, f32[2,24,24,128]{3,2,1,0:T(8,128)S(1)} %copy-done.1, f32[24,24,128]{2,1,0:T(8,128)S(1)} %copy-done.2, f32[17,24,128]{2,1,0:T(8,128)S(1)} %collective-permute-done.x_band, ...), custom_call_target="tpu_custom_call" | custom-call | tf_op jit(solution)/shard_map/pack_halo/pallas_call | solution.py:588
  16.3 2.3 %collective-permute-start.3 = (f32[5,4,32,128]{3,2,1,0:T(8,128)S(1)}, f32[5,4,32,128]{3,2,1,0:T(8,128)S(1)}, u32[]{:S(2)}, u32[]{:S(2)}) collective-permute-start(f32[5,4,32,128]{3,2,1,0:T(8,128)S(1)} %pack_halo.1), channel_id=1, source_target_pairs={{0,1},{1,0},{2,3},{3,2},{4,5},{5,4},{6,7},{7,6},{8,9},{9,8},{10,11... | collective-permute-start | bytes 983048 | tf_op jit(solution)/shard_map/ppermute | solution.py:559
  18.7 1.1 %weights.1 = (f32[28,32,128]{2,1,0:T(8,128)S(1)}, f32[28,32,128]{2,1,0:T(8,128)S(1)}, f32[28,32,128]{2,1,0:T(8,128)S(1)}, f32[28,32,128]{2,1,0:T(8,128)S(1)}, bf16[4,256,256]{2,1,0:T(8,128)(2,1)S(1)}) custom-call(s32[4]{0:T(128)S(1)} %pad_add_fusion.info, f32[4]{0:T(128)S(1)} %pad_maximum_fusion.keep, f32[2,24,24,128]{3,2,1,0:T(8,128)S(1)} %copy-done, ...), custom_call_target="tpu_custom_call" | custom-call | tf_op jit(solution)/shard_map/weights/pallas_call | solution.py:588
  19.8 0.2 collective-permute-done.3.halo
  19.9 0.6 relax.1
  20.6 10.8 %collective-permute-start.4 = (f32[2,2,24,128]{3,2,1,0:T(8,128)S(1)}, f32[2,2,24,128]{3,2,1,0:T(8,128)S(1)}, u32[]{:S(2)}, u32[]{:S(2)}) collective-permute-start(f32[2,2,24,128]{3,2,1,0:T(8,128)S(1)} %get-tuple-element.31), channel_id=1, source_target_pairs={{0,16},{16,0},{32,48},{48,32},{64,80},{80,64},{96,112},{112,96},{1... | collective-permute-start | bytes 147464 | tf_op jit(solution)/shard_map/ppermute | solution.py:545
  31.4 1.4 %collective-permute-done.4.x_a = f32[2,2,24,128]{3,2,1,0:T(8,128)S(1)} collective-permute-done((f32[2,2,24,128]{3,2,1,0:T(8,128)S(1)}, f32[2,2,24,128]{3,2,1,0:T(8,128)S(1)}, u32[]{:S(2)}, u32[]{:S(2)}) %collective-permute-start.4) | collective-permute-done | bytes 49184 | tf_op jit(solution)/shard_map/ppermute | solution.py:545
  32.8 4.8 %collective-permute-done.5.x_b = f32[2,2,24,128]{3,2,1,0:T(8,128)S(1)} collective-permute-done((f32[2,2,24,128]{3,2,1,0:T(8,128)S(1)}, f32[2,2,24,128]{3,2,1,0:T(8,128)S(1)}, u32[]{:S(2)}, u32[]{:S(2)}) %collective-permute-start.5) | collective-permute-done | bytes 49184 | tf_op jit(solution)/shard_map/ppermute | solution.py:545
  37.6 0.6 faces.1
  38.3 1.0 %collective-permute-start.6 = (f32[2,32,128]{2,1,0:T(8,128)S(1)}, f32[2,32,128]{2,1,0:T(8,128)S(1)}, u32[]{:S(2)}, u32[]{:S(2)}) collective-permute-start(f32[2,32,128]{2,1,0:T(8,128)S(1)} %get-tuple-element.35), channel_id=1, source_target_pairs={{0,2},{2,0},{4,6},{6,4},{8,10},{10,8},{12,14},{14,12},{1,3},{3,1},... | collective-permute-start | bytes 98312 | tf_op jit(solution)/shard_map/ppermute | solution.py:545
  39.3 1.8 %collective-permute-done.6.z_a = f32[2,32,128]{2,1,0:T(8,128)S(1)} collective-permute-done((f32[2,32,128]{2,1,0:T(8,128)S(1)}, f32[2,32,128]{2,1,0:T(8,128)S(1)}, u32[]{:S(2)}, u32[]{:S(2)}) %collective-permute-start.6) | collective-permute-done | bytes 32800 | tf_op jit(solution)/shard_map/ppermute | solution.py:545
  41.1 2.1 %collective-permute-done.7.z_b = f32[2,32,128]{2,1,0:T(8,128)S(1)} collective-permute-done((f32[2,32,128]{2,1,0:T(8,128)S(1)}, f32[2,32,128]{2,1,0:T(8,128)S(1)}, u32[]{:S(2)}, u32[]{:S(2)}) %collective-permute-start.7) | collective-permute-done | bytes 32800 | tf_op jit(solution)/shard_map/ppermute | solution.py:545
  43.2 2.0 %residual.1 = (f32[2,24,24,128]{3,2,1,0:T(8,128)S(1)}, f32[256,128]{1,0:T(8,128)}) custom-call(s32[4]{0:T(128)S(1)} %pad_add_fusion.info, f32[4]{0:T(128)S(1)} %pad_maximum_fusion.1.keep, f32[2,24,24,128]{3,2,1,0:T(8,128)S(1)} %get-tuple-element.39.field, f32[2,24,24,128]{3,2,1,0:T(8,128)S(1)} %copy-done.1, f32[24,24,128]{2,1,0:T(8,128)S(1)} %copy-done.2, ...), custom_call_target="tpu_custom_call" | custom-call | tf_op jit(solution)/shard_map/residual/pallas_call | solution.py:588
  45.2 10.6 %all-to-all-start = ((f32[256,1,128]{2,1,0:T(1,128)}), f32[256,1,128]{2,1,0:T(1,128)S(1)}, u32[]{:S(2)}, u32[]{:S(2)}) async-start(f32[256,1,128]{2,1,0:T(1,128)} %bitcast.13), calls=%async_computation | async-start | bytes 262144 | tf_op jit(solution)/shard_map/all_to_all | solution.py:664
  55.8 0.8 %copy.9 = f32[2,24,24,128]{3,2,1,0:T(8,128)} copy(f32[2,24,24,128]{3,2,1,0:T(8,128)S(1)} %get-tuple-element.39.field) | data formatting | bytes 1179648
  56.7 0.8 %copy.10 = f32[2,24,24,128]{3,2,1,0:T(8,128)} copy(f32[2,24,24,128]{3,2,1,0:T(8,128)S(1)} %get-tuple-element.40) | data formatting | bytes 1179648
  57.5 11.3 %all-to-all-done = f32[256,1,128]{2,1,0:T(1,128)S(1)} async-done(((f32[256,1,128]{2,1,0:T(1,128)}), f32[256,1,128]{2,1,0:T(1,128)S(1)}, u32[]{:S(2)}, u32[]{:S(2)}) %all-to-all-start) | async-done | bytes 131104 | tf_op jit(solution)/shard_map/all_to_all | solution.py:664
  68.8 0.3 reduce_sum.9
  (12 shorter events, 0.3 us)
Async XLA Ops:
  0.6 14.4 %copy-start = (f32[2,24,24,128]{3,2,1,0:T(8,128)S(1)}, f32[2,24,24,128]{3,2,1,0:T(8,128)}, u32[]{:S(2)}) copy-start(f32[2,24,24,128]{3,2,1,0:T(8,128)} %iterate.7) | copy-start | bytes 1769476
  0.6 14.4 %copy-start.1 = (f32[2,24,24,128]{3,2,1,0:T(8,128)S(1)}, f32[2,24,24,128]{3,2,1,0:T(8,128)}, u32[]{:S(2)}) copy-start(f32[2,24,24,128]{3,2,1,0:T(8,128)} %source.7) | copy-start | bytes 1769476
  0.7 14.4 %copy-start.2 = (f32[24,24,128]{2,1,0:T(8,128)S(1)}, f32[24,24,128]{2,1,0:T(8,128)}, u32[]{:S(2)}) copy-start(f32[24,24,128]{2,1,0:T(8,128)} %wave.7) | copy-start | bytes 884740
  2.1 12.6 %collective-permute-start.2 = (f32[72,128]{1,0:T(8,128)S(1)}, f32[72,128]{1,0:T(8,128)S(1)}, u32[]{:S(2)}, u32[]{:S(2)}) collective-permute-start(f32[72,128]{1,0:T(8,128)S(1)} %get-tuple-element.23), channel_id=1, source_target_pairs={{0,18},{2,20},{4,22},{6,24},{8,26},{10,28},{12,30},{14,16},{16,34}... | collective-permute-start | bytes 110600 | tf_op jit(solution)/shard_map/ppermute | solution.py:555
  5.6 9.4 %collective-permute-start = (f32[17,24,128]{2,1,0:T(8,128)S(1)}, f32[17,24,128]{2,1,0:T(8,128)S(1)}, u32[]{:S(2)}, u32[]{:S(2)}) collective-permute-start(f32[17,24,128]{2,1,0:T(8,128)S(1)} %get-tuple-element.21), channel_id=1, source_target_pairs={{0,16},{16,32},{32,48},{48,64},{64,80},{80,96},{96,112},{112,128},... | collective-permute-start | bytes 626696 | tf_op jit(solution)/shard_map/ppermute | solution.py:536
  6.9 8.1 %collective-permute-start.1 = (f32[408,128]{1,0:T(8,128)S(1)}, f32[408,128]{1,0:T(8,128)S(1)}, u32[]{:S(2)}, u32[]{:S(2)}) collective-permute-start(f32[408,128]{1,0:T(8,128)S(1)} %get-tuple-element.22), channel_id=1, source_target_pairs={{0,2},{2,4},{4,6},{6,8},{8,10},{10,12},{12,14},{14,0},{1,3},{3,5},... | collective-permute-start | bytes 626696 | tf_op jit(solution)/shard_map/ppermute | solution.py:536
  16.3 3.6 %collective-permute-start.3 = (f32[5,4,32,128]{3,2,1,0:T(8,128)S(1)}, f32[5,4,32,128]{3,2,1,0:T(8,128)S(1)}, u32[]{:S(2)}, u32[]{:S(2)}) collective-permute-start(f32[5,4,32,128]{3,2,1,0:T(8,128)S(1)} %pack_halo.1), channel_id=1, source_target_pairs={{0,1},{1,0},{2,3},{3,2},{4,5},{5,4},{6,7},{7,6},{8,9},{9,8},{10,11... | collective-permute-start | bytes 983048 | tf_op jit(solution)/shard_map/ppermute | solution.py:559
  20.6 12.2 %collective-permute-start.4 = (f32[2,2,24,128]{3,2,1,0:T(8,128)S(1)}, f32[2,2,24,128]{3,2,1,0:T(8,128)S(1)}, u32[]{:S(2)}, u32[]{:S(2)}) collective-permute-start(f32[2,2,24,128]{3,2,1,0:T(8,128)S(1)} %get-tuple-element.31), channel_id=1, source_target_pairs={{0,16},{16,0},{32,48},{48,32},{64,80},{80,64},{96,112},{112,96},{1... | collective-permute-start | bytes 147464 | tf_op jit(solution)/shard_map/ppermute | solution.py:545
  31.4 6.3 %collective-permute-start.5 = (f32[2,2,24,128]{3,2,1,0:T(8,128)S(1)}, f32[2,2,24,128]{3,2,1,0:T(8,128)S(1)}, u32[]{:S(2)}, u32[]{:S(2)}) collective-permute-start(f32[2,2,24,128]{3,2,1,0:T(8,128)S(1)} %get-tuple-element.32), channel_id=1, source_target_pairs={{16,32},{32,16},{48,64},{64,48},{80,96},{96,80},{112,128},{128,112... | collective-permute-start | bytes 147464 | tf_op jit(solution)/shard_map/ppermute | solution.py:545
  38.3 2.9 %collective-permute-start.6 = (f32[2,32,128]{2,1,0:T(8,128)S(1)}, f32[2,32,128]{2,1,0:T(8,128)S(1)}, u32[]{:S(2)}, u32[]{:S(2)}) collective-permute-start(f32[2,32,128]{2,1,0:T(8,128)S(1)} %get-tuple-element.35), channel_id=1, source_target_pairs={{0,2},{2,0},{4,6},{6,4},{8,10},{10,8},{12,14},{14,12},{1,3},{3,1},... | collective-permute-start | bytes 98312 | tf_op jit(solution)/shard_map/ppermute | solution.py:545
  39.3 4.0 %collective-permute-start.7 = (f32[2,32,128]{2,1,0:T(8,128)S(1)}, f32[2,32,128]{2,1,0:T(8,128)S(1)}, u32[]{:S(2)}, u32[]{:S(2)}) collective-permute-start(f32[2,32,128]{2,1,0:T(8,128)S(1)} %get-tuple-element.36), channel_id=1, source_target_pairs={{2,4},{4,2},{6,8},{8,6},{10,12},{12,10},{14,0},{0,14},{3,5},{5,3},... | collective-permute-start | bytes 98312 | tf_op jit(solution)/shard_map/ppermute | solution.py:545
  45.2 23.6 %all-to-all-start = ((f32[256,1,128]{2,1,0:T(1,128)}), f32[256,1,128]{2,1,0:T(1,128)S(1)}, u32[]{:S(2)}, u32[]{:S(2)}) async-start(f32[256,1,128]{2,1,0:T(1,128)} %bitcast.13), calls=%async_computation | async-start | bytes 262144 | tf_op jit(solution)/shard_map/all_to_all | solution.py:664

commit v3 on v2

--- a/solution.py
+++ b/solution.py
@@ -17,11 +17,13 @@
 EXT = CX + BAND
 GROUP = 16
 HALO = 11
+OVER = GROUP - HALO
 STRIDE = 4
 MOVERS = (EXT // STRIDE + 1) // 2
 LAYERS = 2 * BAND + 3 * (BAND - 1)
 PER = EXT // STRIDE
 
+HALO_ROW = 2 * CZ
 SIDE_ROW = 26
 
 MIB = 1024 * 1024
@@ -126,25 +128,63 @@
                 low[field, plane, to, :] = corner[rows, :] * keep_both
 
 
-def halo_kernel(info, keep, iterate, source, wave, x_band, z_band, corner, out, low):
-    half = info[0]
-    keep_x = keep[0]
-    fill_low_tiles(low, z_band, corner, keep_x, keep[1])
-    fields = [(iterate, 0), (iterate, 1), (source, 0), (source, 1), (wave, None)]
+def own_layout(half):
+    return OVER + (HALO - OVER) * half, HALO * half, OVER
+
+
+def other_layout(half):
+    return HALO - (HALO - OVER) * half, OVER * half, HALO
+
+
+def join_lane(half):
+    return OVER + (GROUP - 1 - 2 * OVER) * half
+
+
+def pack(packed, values, layout):
+    turn, least, count = layout
     lanes = lane_ids()
     place = lanes % GROUP
-    least = (GROUP - HALO) * (1 - half)
-    wanted = (place >= least) & (place < least + HALO)
-    masks = [wanted & (lanes // GROUP == j) for j in range(PER)]
+    wanted = (place >= least) & (place < least + count)
+    turned = [(j, pltpu.roll(v, lax.rem(GROUP * j + turn, LANES), 1)) for j, v in values]
+    for j, value in turned:
+        packed = jnp.where(wanted & (lanes // GROUP == j), value, packed)
+    return packed
+
+
+def inner_halo_kernel(info, iterate, source, wave, theirs, mine):
+    half = info[0]
+    fields = [(iterate, 0), (iterate, 1), (source, 0), (source, 1), (wave, None)]
+    zeros = jnp.zeros((8, LANES), jnp.float32)
     for field in range(5):
         for start in range(STRIDE):
-            for tile in range(4):
-                packed = jnp.zeros((8, LANES), jnp.float32)
-                for j in range(PER):
-                    value = tile_of(fields, x_band, low, field, STRIDE * j + start, tile, keep_x)
-                    turned = pltpu.roll(value, GROUP * (j + 1 - half), 1)
-                    packed = jnp.where(masks[j], turned, packed)
-                out[field, start, pl.ds(8 * tile, 8), :] = packed
+            for tile in range(1, 4):
+                values = [
+                    (j, tile_of(fields, None, None, field, STRIDE * j + start, tile, None))
+                    for j in range(1, PER)
+                ]
+                at = pl.ds(8 * tile, 8)
+                theirs[field, start, at, :] = pack(zeros, values, other_layout(half))
+                mine[field, start, at, :] = pack(zeros, values, own_layout(half))
+
+
+def pack_bands(inner, out, low, x_band, keep_x, layout):
+    for field in range(5):
+        for start in range(STRIDE):
+            values = [(j, low[field, STRIDE * j + start]) for j in range(PER)]
+            zeros = jnp.zeros((8, LANES), jnp.float32)
+            out[field, start, pl.ds(0, 8), :] = pack(zeros, values, layout)
+            for tile in range(1, 4):
+                at = pl.ds(8 * tile, 8)
+                packed = inner[field, start, at, :]
+                if start >= layers(field):
+                    value = x_band[layer_row(field, start), pl.ds(8 * (tile - 1), 8), :] * keep_x
+                    packed = pack(packed, [(0, value)], layout)
+                out[field, start, at, :] = packed
+
+
+def halo_kernel(info, keep, inner, x_band, z_band, corner, out, low):
+    fill_low_tiles(low, z_band, corner, keep[0], keep[1])
+    pack_bands(inner, out, low, x_band, keep[0], other_layout(info[0]))
 
 
 def coefficients(wave_sq, s_re, s_im, sigma):
@@ -164,8 +204,8 @@
 
 
 def weights_kernel(
-    info, keep, iterate, source, wave, x_band, z_band, corner,
-    e_re, e_im, f_re, f_im, movers, low,
+    info, keep, iterate, source, wave, inner, x_band, z_band, corner,
+    e_re, e_im, f_re, f_im, movers, mine, low,
 ):
     half = info[0]
     keep_x = keep[0]
@@ -173,11 +213,12 @@
     row = lax.broadcasted_iota(jnp.int32, (16, 2 * LANES), 0)
     ends = lane % LANES == (LANES - 1) * (1 - half)
     for m in range(MOVERS):
-        start = GROUP * (2 * m + lane // LANES) + (GROUP - 1) * half
+        start = GROUP * (2 * m + lane // LANES) + join_lane(half)
         for first in range(0, 2 * LANES, 16):
             hit = ends & ((row + first) % LANES == start)
             movers[m, pl.ds(first, 16), :] = hit.astype(jnp.float32).astype(jnp.bfloat16)
     fill_low_tiles(low, z_band, corner, keep_x, keep[1])
+    pack_bands(inner, mine, low, x_band, keep_x, own_layout(half))
     fields = [(iterate, 0), (iterate, 1), (source, 0), (source, 1), (wave, None)]
     zeros = jnp.zeros((8, LANES), jnp.float32)
     kept_rows = row_ids() < 5
@@ -205,9 +246,9 @@
 
 
 def relax_kernel(
-    info, keep, iterate, x_band, z_band, corner, e_re, e_im, f_re, f_im, movers, halo,
+    info, keep, iterate, x_band, z_band, corner, e_re, e_im, f_re, f_im, movers, mine, halo,
     own, beside, x_a, x_b, z_first, z_last,
-    low, w, w_next, h, h_next, he_re, he_im, hf_re, hf_im, hq, hr, hs, mq, mr, sides,
+    low, w, h, he_re, he_im, hf_re, hf_im, hq, hr, hs, mq, mr, sides,
 ):
     half = info[0]
     active = info[1]
@@ -227,9 +268,10 @@
         rows = row_ids()
         place = lanes % GROUP
         group = lanes // GROUP
-        least = (GROUP - HALO) * half
+        turn, least, count = own_layout(half)
+        repeated = (place >= least) & (place < least + count)
         zeros = jnp.zeros((8, LANES), jnp.float32)
-        for scratch in (w, w_next, h, h_next):
+        for scratch in (w, h):
             scratch[...] = jnp.zeros_like(scratch)
 
         for tile in range(4):
@@ -238,18 +280,20 @@
             at, inner = pl.ds(8 * tile, 8), pl.ds(8 + 8 * tile, 8)
             for plane in range(EXT):
                 for part in range(2):
-                    w[part, plane + 1, inner, :] = tile_of(
-                        fields, x_band, low, part, plane, tile, keep_x
-                    )
+                    value = tile_of(fields, x_band, low, part, plane, tile, keep_x)
+                    w[part, plane + 1, inner, :] = value
             for start in range(STRIDE):
-                w_re, w_im, s_re, s_im, wave_sq = [halo[f, start, at, :] for f in range(5)]
+                w_re, w_im, s_re, s_im, wave_sq = [
+                    jnp.where(repeated, mine[f, start, at, :], halo[f, start, at, :])
+                    for f in range(5)
+                ]
                 h[0, start, inner, :] = w_re
                 h[1, start, inner, :] = w_im
                 x = (STRIDE * group + start - BAND).astype(jnp.float32)
                 ramp = jnp.maximum(x - (CX - PML) + 1.0, 0.0) / PML
                 sigma = along_z + SIGMA * ramp * ramp * keep[2]
                 er, ei, fr, fi = coefficients(wave_sq, s_re, s_im, sigma)
-                kept = (place < least) | (place >= least + HALO) | (group == PER)
+                kept = group == PER
                 if start == 0:
                     kept = kept | (group == 0)
                 if tile == 0:
@@ -261,11 +305,6 @@
 
         first_lane = lanes == 0
         last_lane = lanes == LANES - 1
-        turns = [GROUP * (j + half) for j in range(PER)]
-        taken = [
-            lanes == lax.rem(turn + jnp.where(half == 0, LANES - 1, 0), LANES) for turn in turns
-        ]
-
         def undamped(plane, tile):
             return plane < BAND + CX - PML and tile < 3
 
@@ -276,7 +315,8 @@
                 return new_re + er * t_re, new_im + er * t_im
             return new_re + (er * t_re - ei * t_im), new_im + (er * t_im + ei * t_re)
 
-        def sweep(w, h, w_out, h_out):
+        def sweep():
+            first = 1
             def centre_and_z(ref, part, plane, tile):
                 base = 8 + 8 * tile
                 return ref[part, plane, pl.ds(base, 8), :], (
@@ -313,8 +353,9 @@
             for tile in range(4):
                 at = pl.ds(8 * tile, 8)
                 for part in range(2):
-                    before, here = (zeros, zeros), centre_and_z(w, part, 1, tile)
-                    for plane in range(EXT):
+                    before = centre_and_z(w, part, first, tile)
+                    here = centre_and_z(w, part, first + 1, tile)
+                    for plane in range(first, EXT):
                         after = (zeros, zeros)
                         if plane + 1 < EXT:
                             after = centre_and_z(w, part, plane + 2, tile)
@@ -328,20 +369,18 @@
             for tile in range(4):
                 at = pl.ds(8 * tile, 8)
                 base = 8 + 8 * tile
-                joint = [[hq[part, s, at, :] for s in range(STRIDE)] for part in range(2)]
                 for j in range(PER):
-                    planes = range(STRIDE * j, STRIDE * (j + 1))
+                    planes = range(max(STRIDE * j, first), STRIDE * (j + 1))
                     q = [[mq[part, plane, at, :] for part in range(2)] for plane in planes]
                     up = [[roll(value, -1) for value in pair] for pair in q]
                     down = [[roll(value, 1) for value in pair] for pair in q]
                     side = [
                         [
-                            sides[j, pl.ds(32 * (STRIDE * part + s) + 8 * tile, 8), :]
+                            sides[j, pl.ds(32 * (STRIDE * part + plane % STRIDE) + 8 * tile, 8), :]
                             for part in range(2)
                         ]
-                        for s in range(STRIDE)
+                        for plane in planes
                     ]
-                    turned = [[pltpu.roll(value, turns[j], 1) for value in pair] for pair in q]
                     for n, plane in enumerate(planes):
                         total = [
                             jnp.where(last_lane, side[n][part], up[n][part])
@@ -349,20 +388,14 @@
                             + mr[part, plane, at, :]
                             for part in range(2)
                         ]
-                        for part in range(2):
-                            joint[part][n] = jnp.where(taken[j], turned[n][part], joint[part][n])
                         new_re, new_im = updated(
                             w[0, plane + 1, pl.ds(base, 8), :], w[1, plane + 1, pl.ds(base, 8), :],
                             total[0], total[1],
                             e_re[plane, at, :], None if undamped(plane, tile) else e_im[plane, at, :],
                             f_re[plane, at, :], f_im[plane, at, :],
                         )
-                        w_out[0, plane + 1, pl.ds(base, 8), :] = new_re
-                        w_out[1, plane + 1, pl.ds(base, 8), :] = new_im
-
-                for part in range(2):
-                    for s in range(STRIDE):
-                        hq[part, s, at, :] = joint[part][s]
+                        w[0, plane + 1, pl.ds(base, 8), :] = new_re
+                        w[1, plane + 1, pl.ds(base, 8), :] = new_im
 
             for tile in range(4):
                 at = pl.ds(8 * tile, 8)
@@ -378,25 +411,51 @@
                         he_re[s, at, :], he_im[s, at, :],
                         hf_re[s, at, :], hf_im[s, at, :],
                     )
-                    h_out[0, s, pl.ds(base, 8), :] = new_re
-                    h_out[1, s, pl.ds(base, 8), :] = new_im
-
-        def two_sweeps(turn, carry):
-            sweep(w, h, w_next, h_next)
-            sweep(w_next, h_next, w, h)
+                    h[0, s, pl.ds(base, 8), :] = new_re
+                    h[1, s, pl.ds(base, 8), :] = new_im
+
+        def renew():
+            for tile in range(4):
+                at = pl.ds(8 + 8 * tile, 8)
+                for part in range(2):
+                    for s in range(STRIDE):
+                        values = [(j, w[part, STRIDE * j + s + 1, at, :]) for j in range(PER)]
+                        h[part, s, at, :] = pack(h[part, s, at, :], values, own_layout(half))
+
+        def one_sweep(turn, carry):
+            sweep()
+
+            @pl.when(turn == SWEEPS // 2 - 1)
+            def _():
+                renew()
+
             return carry
 
-        lax.fori_loop(0, SWEEPS // 2, two_sweeps, 0)
+        lax.fori_loop(0, SWEEPS, one_sweep, 0)
         for part in range(2):
             for x in range(CX):
                 own[part, x] = w[part, x + BAND + 1, pl.ds(16, CZ), :]
             for s in range(STRIDE):
                 beside[part, s] = h[part, s, pl.ds(8, 32), :]
 
+    place_in = lane_ids() // GROUP
+    for face, side in ((x_a, 1 - odd), (x_b, odd)):
+        turned = [
+            pltpu.roll(
+                beside[n // 3, (STRIDE - 1) * side, pl.ds(8 + 8 * (n % 3), 8), :],
+                lax.rem(LANES + GROUP * (n - 1 - (PER - 2) * side), LANES),
+                1,
+            )
+            for n in range(6)
+        ]
+        packed = turned[0]
+        for n in range(1, 6):
+            packed = jnp.where(place_in == n, turned[n], packed)
+        face[pl.ds(HALO_ROW, 8), :] = packed
+
     for part in range(2):
         for face, side in ((x_a, 1 - odd), (x_b, odd)):
-            face[part, 0] = own[part, (CX - 1) * side]
-            face[part, 1] = beside[part, (STRIDE - 1) * side, pl.ds(8, CZ), :]
+            face[pl.ds(CZ * part, CZ), :] = own[part, (CX - 1) * side]
         for face, z in ((z_first, 0), (z_last, CZ - 1)):
             face[part, pl.ds(24, 8), :] = jnp.zeros((8, LANES), jnp.float32)
             for x in range(CX):
@@ -412,13 +471,15 @@
     for face, out, z in ((z_first, first, 0), (z_last, last, CZ - 1)):
         out[...] = face[...]
         for part in range(2):
-            a, b = [[ref[part, n, pl.ds(z, 1), :] for n in range(2)] for ref in (x_a, x_b)]
+            rows = [pl.ds(CZ * part + z, 1), pl.ds(HALO_ROW + z % 8, 1)]
+            a, b = [[ref[row, :] for row in rows] for ref in (x_a, x_b)]
+            piece = 3 * part + z // 8
             low = [jnp.where(odd_x, a[n], b[n]) * keep[0] for n in range(2)]
             high = [jnp.where(odd_x, b[n], a[n]) * keep[1] for n in range(2)]
             out[part, pl.ds(0, 1), :] = low[0]
             out[part, pl.ds(CX + 1, 1), :] = high[0]
             for s, value, to, turn in (
-                (STRIDE - 1, low[1], 0, -6 * GROUP), (0, high[1], 7, 6 * GROUP)
+                (STRIDE - 1, low[1], 0, -GROUP * piece), (0, high[1], 7, GROUP * (7 - piece))
             ):
                 at = pl.ds(SIDE_ROW + s, 1)
                 out[part, at, :] = jnp.where(group == to, roll(value, turn), face[part, at, :])
@@ -436,15 +497,16 @@
     z_low[...] = jnp.where(odd_z, z_a[...], z_b[...])
     z_high[...] = jnp.where(odd_z, z_b[...], z_a[...])
 
-    def x_sides(part, n, rows):
-        a, b = x_a[part, n, rows, :], x_b[part, n, rows, :]
+    def x_sides(rows):
+        a, b = x_a[rows, :], x_b[rows, :]
         return jnp.where(odd_x, a, b) * keep[0], jnp.where(odd_x, b, a) * keep[1]
 
     lanes = lane_ids()
     group = lanes // GROUP
     zeros = jnp.zeros((8, LANES), jnp.float32)
+    low_halo, high_halo = x_sides(pl.ds(HALO_ROW, 8))
     for part in range(2):
-        low, high = x_sides(part, 0, pl.ds(0, CZ))
+        low, high = x_sides(pl.ds(CZ * part, CZ))
         box[part, 0, pl.ds(8, CZ), :] = low
         box[part, CX + 1, pl.ds(8, CZ), :] = high
         for x in range(CX):
@@ -458,11 +520,11 @@
             sides[part, s, pl.ds(8 + CZ, 1), :] = z_high[part, row, :] * keep[3]
             for tile in range(3):
                 value = beside[part, s, pl.ds(8 + 8 * tile, 8), :]
-                low, high = x_sides(part, 1, pl.ds(8 * tile, 8))
+                piece = 3 * part + tile
                 if s == STRIDE - 1:
-                    value = jnp.where(group == 0, roll(low, -6 * GROUP), value)
+                    value = jnp.where(group == 0, roll(low_halo, -GROUP * piece), value)
                 if s == 0:
-                    value = jnp.where(group == 7, roll(high, 6 * GROUP), value)
+                    value = jnp.where(group == 7, roll(high_halo, GROUP * (7 - piece)), value)
                 sides[part, s, pl.ds(8 + 8 * tile, 8), :] = value
 
     def centre_and_z(ref, part, plane, tile):
@@ -471,7 +533,7 @@
             ref[part, plane, pl.ds(base - 1, 8), :] + ref[part, plane, pl.ds(base + 1, 8), :]
         )
 
-    joined = lanes % GROUP == (GROUP - 1) * half
+    joined = lanes % GROUP == join_lane(half)
     for part in range(2):
         for tile in range(3):
             at = pl.ds(8 * tile, 8)
@@ -501,13 +563,13 @@
 
     first_lane = lanes == 0
     last_lane = lanes == LANES - 1
-    to_edge = jnp.where(half == 0, LANES - 1, 1)
+    to_edge = (LANES - 1) * (1 - half) - join_lane(half)
     squares = [zeros] * 4
     for part in range(2):
         for tile in range(3):
             at = pl.ds(8 * tile, 8)
             for j in range(1, PER):
-                turn = lax.rem(LANES - GROUP * (j + half) + to_edge, LANES)
+                turn = lax.rem(2 * LANES - GROUP * j + to_edge, LANES)
                 planes = range(STRIDE * (j - 1), STRIDE * j)
                 q = [mq[part, x, at, :] for x in planes]
                 up = [roll(value, -1) for value in q]
@@ -609,10 +671,14 @@
     x_band = ring(x_band, "gx", 1)
     z_band = ring(z_band, "gz", 1)
     low_tiles = (5, EXT, 8, LANES)
+    packed = f32(5, STRIDE, 32, LANES)
+    theirs, mine = call(
+        inner_halo_kernel, (packed, packed), (info, iterate, source, wave_sq), "pack_inner"
+    )
     halo = call(
         halo_kernel,
-        f32(5, STRIDE, 32, LANES),
-        (info, band_keep, iterate, source, wave_sq, x_band, z_band, corner),
+        packed,
+        (info, band_keep, theirs, x_band, z_band, corner),
         "pack_halo",
         [low_tiles],
     )
@@ -621,12 +687,12 @@
     own = (2, CX, CZ, LANES)
     in_vmem = pltpu.VMEM(own, jnp.float32)
     box_like, pack_like = (2, EXT + 2, 48, LANES), (2, STRIDE, 48, LANES)
-    x_face, z_face = f32(2, 2, CZ, LANES), f32(2, 32, LANES)
+    x_face, z_face = f32(HALO_ROW + 8, LANES), f32(2, 32, LANES)
     weights = call(
         weights_kernel,
         (f32(*planes),) * 4
-        + (jax.ShapeDtypeStruct((MOVERS, 2 * LANES, 2 * LANES), jnp.bfloat16),),
-        (info, band_keep, iterate, source, wave_sq, x_band, z_band, corner),
+        + (jax.ShapeDtypeStruct((MOVERS, 2 * LANES, 2 * LANES), jnp.bfloat16), packed),
+        (info, band_keep, iterate, source, wave_sq, mine, x_band, z_band, corner),
         "weights",
         [low_tiles],
     )
@@ -635,8 +701,7 @@
         (in_vmem, f32(2, STRIDE, 32, LANES), x_face, x_face, z_face, z_face),
         (info, band_keep, iterate, x_band, z_band, corner, *weights, halo),
         "relax",
-        [(2,) + low_tiles[1:], box_like, box_like]
-        + [pack_like] * 2
+        [(2,) + low_tiles[1:], box_like, pack_like]
         + [packs] * 4
         + [(2,) + packs] * 2
         + [(2 * STRIDE * 32, LANES)]
@@ -655,7 +720,7 @@
     count = size_x * size_z * size_y
     residual, total = call(
         residual_kernel,
-        (in_vmem, f32(count, LANES)),
+        (in_vmem, pltpu.VMEM((count, LANES), jnp.float32)),
         (info, box_keep, new, source, wave_sq, beside, x_a, x_b, z_a, z_b),
         "residual",
         [(2, CX + 2, 48, LANES), (2, STRIDE, 48, LANES), own, own, (2, STRIDE, CZ, LANES)]

time: 70.8 us -> 70.1 us (level)
  waiting for transfers between devices: 26.6 us -> 18.2 us
  starting transfers between devices: 31.2 us -> 38.1 us
  Pallas kernels: 6.96 us -> 8.21 us
    all_to_all x1, starting transfers between devices: 10.6 us -> 20 us  [on_device(): parts = lax.all_to_all(total, ('gx', 'gz', 'gy'), 0, 0, tiled=True)]
    ppermute x4, waiting for transfers between devices: 10.2 us -> 3.37 us  [pairs(): return lax.ppermute(value, axis, moves)]
    ppermute x4, starting transfers between devices: 11.8 us -> 9.17 us  [pairs(): return lax.ppermute(value, axis, moves)]
    ppermute x1, waiting for transfers between devices: 4.56 us -> 3.16 us  [diagonal(): return lax.ppermute(value, ('gx', 'gz'), pairs)]
    pallas_call x6 -> x7, Pallas kernels: 6.96 us -> 8.21 us  [call(): pl.pallas_call(kernel, out_shape=outs, in_specs=[SMEM] * scalars + [place...]
  transfers between devices with their start and end apart: 9 -> 9, of which waited for: 8 -> 5; matrix products, arithmetic and copies ran while one was open for 3% -> 3% of each run, Pallas kernels for 2% -> 4%
where the time goes in v3:
time: 70.1 us; the launch traced here: 70 us
  starting transfers between devices  38.1 us (54%)
  waiting for transfers between devices  18.2 us (26%)
  Pallas kernels  8.21 us (12%)
  between operations  3.29 us (5%)
  local copies, waits for them, and re-layouts  1.64 us (2%)
    all_to_all x1, starting transfers between devices, on_device(): parts = lax.all_to_all(total, ('gx', 'gz', 'gy'), 0, 0, tiled=True)  20 us
    all_to_all x1, waiting for transfers between devices, on_device(): parts = lax.all_to_all(total, ('gx', 'gz', 'gy'), 0, 0, tiled=True)  11.3 us
    ppermute x4, starting transfers between devices, pairs(): return lax.ppermute(value, axis, moves)  9.17 us
    pallas_call x7, Pallas kernels, call(): pl.pallas_call(kernel, out_shape=outs, in_specs=[SMEM] * scalars + [place...  8.21 us
    ppermute x1, starting transfers between devices, diagonal(): return lax.ppermute(value, ('gx', 'gz'), pairs)  3.56 us
    ppermute x4, waiting for transfers between devices, pairs(): return lax.ppermute(value, axis, moves)  3.37 us
    ppermute x1, waiting for transfers between devices, diagonal(): return lax.ppermute(value, ('gx', 'gz'), pairs)  3.16 us
    ppermute x2, starting transfers between devices, ring(): lax.ppermute(value, axis, [(i, (i + by) % size) for i in range(size)])  2.93 us
  transfers between devices with their start and end apart: 9, of which 5 were waited for; matrix products, arithmetic and copies ran while one was open for 3% of the time, Pallas kernels for 4%

profile of v3, /device:TPU:1, one launch (start us, length us, event | category | flops | bytes accessed | tf_op | source)
XLA Modules:
  0.0 70.0 jit_solution(3646100850125208458)
XLA Ops:
  0.7 1.4 %bands.1 = (f32[17,24,128]{2,1,0:T(8,128)S(1)}, f32[408,128]{1,0:T(8,128)S(1)}, f32[72,128]{1,0:T(8,128)S(1)}) custom-call(f32[2,24,24,128]{3,2,1,0:T(8,128)} %iterate.7, f32[2,24,24,128]{3,2,1,0:T(8,128)} %source.7, f32[24,24,128]{2,1,0:T(8,128)} %wave.7), custom_call_target="tpu_custom_call" | custom-call | tf_op jit(solution)/shard_map/bands/pallas_call | solution.py:650
  2.1 3.6 %collective-permute-start.2 = (f32[72,128]{1,0:T(8,128)S(1)}, f32[72,128]{1,0:T(8,128)S(1)}, u32[]{:S(2)}, u32[]{:S(2)}) collective-permute-start(f32[72,128]{1,0:T(8,128)S(1)} %get-tuple-element.26), channel_id=1, source_target_pairs={{0,18},{2,20},{4,22},{6,24},{8,26},{10,28},{12,30},{14,16},{16,34}... | collective-permute-start | bytes 110600 | tf_op jit(solution)/shard_map/ppermute | solution.py:617
  5.6 1.3 %collective-permute-start = (f32[17,24,128]{2,1,0:T(8,128)S(1)}, f32[17,24,128]{2,1,0:T(8,128)S(1)}, u32[]{:S(2)}, u32[]{:S(2)}) collective-permute-start(f32[17,24,128]{2,1,0:T(8,128)S(1)} %get-tuple-element.24), channel_id=1, source_target_pairs={{0,16},{16,32},{32,48},{48,64},{64,80},{80,96},{96,112},{112,128},... | collective-permute-start | bytes 626696 | tf_op jit(solution)/shard_map/ppermute | solution.py:598
  6.9 1.6 %collective-permute-start.1 = (f32[408,128]{1,0:T(8,128)S(1)}, f32[408,128]{1,0:T(8,128)S(1)}, u32[]{:S(2)}, u32[]{:S(2)}) collective-permute-start(f32[408,128]{1,0:T(8,128)S(1)} %get-tuple-element.25), channel_id=1, source_target_pairs={{0,2},{2,4},{4,6},{6,8},{8,10},{10,12},{12,14},{14,0},{1,3},{3,5},... | collective-permute-start | bytes 626696 | tf_op jit(solution)/shard_map/ppermute | solution.py:598
  10.1 1.4 %pack_inner.1 = (f32[5,4,32,128]{3,2,1,0:T(8,128)S(1)}, f32[5,4,32,128]{3,2,1,0:T(8,128)S(1)}) custom-call(s32[4]{0:T(128)S(1)} %pad_add_fusion.info, f32[2,24,24,128]{3,2,1,0:T(8,128)S(1)} %copy-done.1, f32[2,24,24,128]{3,2,1,0:T(8,128)S(1)} %copy-done, f32[24,24,128]{2,1,0:T(8,128)S(1)} %copy-done.2), custom_call_target="tpu_custom_call" | custom-call | tf_op jit(solution)/shard_map/pack_inner/pallas_call | solution.py:650
  11.5 3.2 %collective-permute-done.2.corner = f32[72,128]{1,0:T(8,128)S(1)} collective-permute-done((f32[72,128]{1,0:T(8,128)S(1)}, f32[72,128]{1,0:T(8,128)S(1)}, u32[]{:S(2)}, u32[]{:S(2)}) %collective-permute-start.2) | collective-permute-done | bytes 36896 | tf_op jit(solution)/shard_map/ppermute | solution.py:617
  14.7 0.4 collective-permute-done.x_band
  15.1 0.9 %pack_halo.1 = f32[5,4,32,128]{3,2,1,0:T(8,128)S(1)} custom-call(s32[4]{0:T(128)S(1)} %pad_add_fusion.info, f32[4]{0:T(128)S(1)} %pad_maximum_fusion.keep, f32[5,4,32,128]{3,2,1,0:T(8,128)S(1)} %get-tuple-element.34.inner, f32[17,24,128]{2,1,0:T(8,128)S(1)} %collective-permute-done.x_band, f32[408,128]{1,0:T(8,128)S(1)} %collective-permute-done.1.z_band, ...), custom_call_target="tpu_custom_call" | custom-call | tf_op jit(solution)/shard_map/pack_halo/pallas_call | solution.py:650
  15.9 2.3 %collective-permute-start.3 = (f32[5,4,32,128]{3,2,1,0:T(8,128)S(1)}, f32[5,4,32,128]{3,2,1,0:T(8,128)S(1)}, u32[]{:S(2)}, u32[]{:S(2)}) collective-permute-start(f32[5,4,32,128]{3,2,1,0:T(8,128)S(1)} %pack_halo.1), channel_id=1, source_target_pairs={{0,1},{1,0},{2,3},{3,2},{4,5},{5,4},{6,7},{7,6},{8,9},{9,8},{10,11... | collective-permute-start | bytes 983048 | tf_op jit(solution)/shard_map/ppermute | solution.py:621
  18.3 1.2 %weights.1 = (f32[28,32,128]{2,1,0:T(8,128)S(1)}, f32[28,32,128]{2,1,0:T(8,128)S(1)}, f32[28,32,128]{2,1,0:T(8,128)S(1)}, f32[28,32,128]{2,1,0:T(8,128)S(1)}, bf...) custom-call(s32[4]{0:T(128)S(1)} %pad_add_fusion.info, f32[4]{0:T(128)S(1)} %pad_maximum_fusion.keep, ...), custom_call_target="tpu_custom_call" | custom-call | tf_op jit(solution)/shard_map/weights/pallas_call | solution.py:650
  19.5 0.7 %relax.1 = (f32[2,24,24,128]{3,2,1,0:T(8,128)S(1)}, f32[2,4,32,128]{3,2,1,0:T(8,128)S(1)}, f32[56,128]{1,0:T(8,128)S(1)}, f32[56,128]{1,0:T(8,128)S(1)}, f32[2,3...) custom-call(s32[4]{0:T(128)S(1)} %pad_add_fusion.info, f32[4]{0:T(128)S(1)} %pad_maximum_fusion.keep, ...), custom_call_target="tpu_custom_call" | custom-call | tf_op jit(solution)/shard_map/relax/pallas_call | solution.py:650
  20.3 0.1 collective-permute-start.4
  20.4 4.0 %collective-permute-start.5 = (f32[56,128]{1,0:T(8,128)S(1)}, f32[56,128]{1,0:T(8,128)S(1)}, u32[]{:S(2)}, u32[]{:S(2)}) collective-permute-start(f32[56,128]{1,0:T(8,128)S(1)} %get-tuple-element.38), channel_id=1, source_target_pairs={{16,32},{32,16},{48,64},{64,48},{80,96},{96,80},{112,128},{128,112... | collective-permute-start | bytes 86024 | tf_op jit(solution)/shard_map/ppermute | solution.py:607
  24.4 2.1 %collective-permute-done.5.x_b = f32[56,128]{1,0:T(8,128)S(1)} collective-permute-done((f32[56,128]{1,0:T(8,128)S(1)}, f32[56,128]{1,0:T(8,128)S(1)}, u32[]{:S(2)}, u32[]{:S(2)}) %collective-permute-start.5) | collective-permute-done | bytes 28704 | tf_op jit(solution)/shard_map/ppermute | solution.py:607
  26.5 0.6 faces.1
  27.1 0.9 %collective-permute-start.6 = (f32[2,32,128]{2,1,0:T(8,128)S(1)}, f32[2,32,128]{2,1,0:T(8,128)S(1)}, u32[]{:S(2)}, u32[]{:S(2)}) collective-permute-start(f32[2,32,128]{2,1,0:T(8,128)S(1)} %get-tuple-element.41), channel_id=1, source_target_pairs={{0,2},{2,0},{4,6},{6,4},{8,10},{10,8},{12,14},{14,12},{1,3},{3,1},... | collective-permute-start | bytes 98312 | tf_op jit(solution)/shard_map/ppermute | solution.py:607
  28.1 4.2 %collective-permute-start.7 = (f32[2,32,128]{2,1,0:T(8,128)S(1)}, f32[2,32,128]{2,1,0:T(8,128)S(1)}, u32[]{:S(2)}, u32[]{:S(2)}) collective-permute-start(f32[2,32,128]{2,1,0:T(8,128)S(1)} %get-tuple-element.42), channel_id=1, source_target_pairs={{2,4},{4,2},{6,8},{8,6},{10,12},{12,10},{14,0},{0,14},{3,5},{5,3},... | collective-permute-start | bytes 98312 | tf_op jit(solution)/shard_map/ppermute | solution.py:607
  32.2 1.3 %collective-permute-done.7.z_b = f32[2,32,128]{2,1,0:T(8,128)S(1)} collective-permute-done((f32[2,32,128]{2,1,0:T(8,128)S(1)}, f32[2,32,128]{2,1,0:T(8,128)S(1)}, u32[]{:S(2)}, u32[]{:S(2)}) %collective-permute-start.7) | collective-permute-done | bytes 32800 | tf_op jit(solution)/shard_map/ppermute | solution.py:607
  33.5 2.0 %residual.1 = (f32[2,24,24,128]{3,2,1,0:T(8,128)S(1)}, f32[256,128]{1,0:T(8,128)}) custom-call(s32[4]{0:T(128)S(1)} %pad_add_fusion.info, f32[4]{0:T(128)S(1)} %pad_maximum_fusion.1.keep, f32[2,24,24,128]{3,2,1,0:T(8,128)S(1)} %get-tuple-element.45.field, f32[2,24,24,128]{3,2,1,0:T(8,128)S(1)} %copy-done, f32[24,24,128]{2,1,0:T(8,128)S(1)} %copy-done.2, ...), custom_call_target="tpu_custom_call" | custom-call | tf_op jit(solution)/shard_map/residual/pallas_call | solution.py:650
  35.5 20.0 %all-to-all-start = ((f32[256,1,128]{2,1,0:T(1,128)}), f32[256,1,128]{2,1,0:T(1,128)S(1)}, u32[]{:S(2)}, u32[]{:S(2)}) async-start(f32[256,1,128]{2,1,0:T(1,128)} %bitcast.13), calls=%async_computation | async-start | bytes 262144 | tf_op jit(solution)/shard_map/all_to_all | solution.py:729
  55.5 0.8 %copy.9 = f32[2,24,24,128]{3,2,1,0:T(8,128)} copy(f32[2,24,24,128]{3,2,1,0:T(8,128)S(1)} %get-tuple-element.45.field) | data formatting | bytes 1179648
  56.4 0.8 %copy.10 = f32[2,24,24,128]{3,2,1,0:T(8,128)} copy(f32[2,24,24,128]{3,2,1,0:T(8,128)S(1)} %get-tuple-element.46) | data formatting | bytes 1179648
  57.2 11.3 %all-to-all-done = f32[256,1,128]{2,1,0:T(1,128)S(1)} async-done(((f32[256,1,128]{2,1,0:T(1,128)}), f32[256,1,128]{2,1,0:T(1,128)S(1)}, u32[]{:S(2)}, u32[]{:S(2)}) %all-to-all-start) | async-done | bytes 131104 | tf_op jit(solution)/shard_map/all_to_all | solution.py:729
  68.5 0.3 reduce_sum.9
  (13 shorter events, 0.3 us)
Async XLA Ops:
  0.6 9.5 %copy-start.1 = (f32[2,24,24,128]{3,2,1,0:T(8,128)S(1)}, f32[2,24,24,128]{3,2,1,0:T(8,128)}, u32[]{:S(2)}) copy-start(f32[2,24,24,128]{3,2,1,0:T(8,128)} %iterate.7) | copy-start | bytes 1769476
  0.6 9.5 %copy-start = (f32[2,24,24,128]{3,2,1,0:T(8,128)S(1)}, f32[2,24,24,128]{3,2,1,0:T(8,128)}, u32[]{:S(2)}) copy-start(f32[2,24,24,128]{3,2,1,0:T(8,128)} %source.7) | copy-start | bytes 1769476
  0.7 9.5 %copy-start.2 = (f32[24,24,128]{2,1,0:T(8,128)S(1)}, f32[24,24,128]{2,1,0:T(8,128)}, u32[]{:S(2)}) copy-start(f32[24,24,128]{2,1,0:T(8,128)} %wave.7) | copy-start | bytes 884740
  2.1 12.6 %collective-permute-start.2 = (f32[72,128]{1,0:T(8,128)S(1)}, f32[72,128]{1,0:T(8,128)S(1)}, u32[]{:S(2)}, u32[]{:S(2)}) collective-permute-start(f32[72,128]{1,0:T(8,128)S(1)} %get-tuple-element.26), channel_id=1, source_target_pairs={{0,18},{2,20},{4,22},{6,24},{8,26},{10,28},{12,30},{14,16},{16,34}... | collective-permute-start | bytes 110600 | tf_op jit(solution)/shard_map/ppermute | solution.py:617
  5.6 9.4 %collective-permute-start = (f32[17,24,128]{2,1,0:T(8,128)S(1)}, f32[17,24,128]{2,1,0:T(8,128)S(1)}, u32[]{:S(2)}, u32[]{:S(2)}) collective-permute-start(f32[17,24,128]{2,1,0:T(8,128)S(1)} %get-tuple-element.24), channel_id=1, source_target_pairs={{0,16},{16,32},{32,48},{48,64},{64,80},{80,96},{96,112},{112,128},... | collective-permute-start | bytes 626696 | tf_op jit(solution)/shard_map/ppermute | solution.py:598
  6.9 8.1 %collective-permute-start.1 = (f32[408,128]{1,0:T(8,128)S(1)}, f32[408,128]{1,0:T(8,128)S(1)}, u32[]{:S(2)}, u32[]{:S(2)}) collective-permute-start(f32[408,128]{1,0:T(8,128)S(1)} %get-tuple-element.25), channel_id=1, source_target_pairs={{0,2},{2,4},{4,6},{6,8},{8,10},{10,12},{12,14},{14,0},{1,3},{3,5},... | collective-permute-start | bytes 626696 | tf_op jit(solution)/shard_map/ppermute | solution.py:598
  15.9 3.6 %collective-permute-start.3 = (f32[5,4,32,128]{3,2,1,0:T(8,128)S(1)}, f32[5,4,32,128]{3,2,1,0:T(8,128)S(1)}, u32[]{:S(2)}, u32[]{:S(2)}) collective-permute-start(f32[5,4,32,128]{3,2,1,0:T(8,128)S(1)} %pack_halo.1), channel_id=1, source_target_pairs={{0,1},{1,0},{2,3},{3,2},{4,5},{5,4},{6,7},{7,6},{8,9},{9,8},{10,11... | collective-permute-start | bytes 983048 | tf_op jit(solution)/shard_map/ppermute | solution.py:621
  20.3 4.2 %collective-permute-start.4 = (f32[56,128]{1,0:T(8,128)S(1)}, f32[56,128]{1,0:T(8,128)S(1)}, u32[]{:S(2)}, u32[]{:S(2)}) collective-permute-start(f32[56,128]{1,0:T(8,128)S(1)} %get-tuple-element.37), channel_id=1, source_target_pairs={{0,16},{16,0},{32,48},{48,32},{64,80},{80,64},{96,112},{112,96},{1... | collective-permute-start | bytes 86024 | tf_op jit(solution)/shard_map/ppermute | solution.py:607
  20.4 6.1 %collective-permute-start.5 = (f32[56,128]{1,0:T(8,128)S(1)}, f32[56,128]{1,0:T(8,128)S(1)}, u32[]{:S(2)}, u32[]{:S(2)}) collective-permute-start(f32[56,128]{1,0:T(8,128)S(1)} %get-tuple-element.38), channel_id=1, source_target_pairs={{16,32},{32,16},{48,64},{64,48},{80,96},{96,80},{112,128},{128,112... | collective-permute-start | bytes 86024 | tf_op jit(solution)/shard_map/ppermute | solution.py:607
  27.1 5.1 %collective-permute-start.6 = (f32[2,32,128]{2,1,0:T(8,128)S(1)}, f32[2,32,128]{2,1,0:T(8,128)S(1)}, u32[]{:S(2)}, u32[]{:S(2)}) collective-permute-start(f32[2,32,128]{2,1,0:T(8,128)S(1)} %get-tuple-element.41), channel_id=1, source_target_pairs={{0,2},{2,0},{4,6},{6,4},{8,10},{10,8},{12,14},{14,12},{1,3},{3,1},... | collective-permute-start | bytes 98312 | tf_op jit(solution)/shard_map/ppermute | solution.py:607
  28.1 5.5 %collective-permute-start.7 = (f32[2,32,128]{2,1,0:T(8,128)S(1)}, f32[2,32,128]{2,1,0:T(8,128)S(1)}, u32[]{:S(2)}, u32[]{:S(2)}) collective-permute-start(f32[2,32,128]{2,1,0:T(8,128)S(1)} %get-tuple-element.42), channel_id=1, source_target_pairs={{2,4},{4,2},{6,8},{8,6},{10,12},{12,10},{14,0},{0,14},{3,5},{5,3},... | collective-permute-start | bytes 98312 | tf_op jit(solution)/shard_map/ppermute | solution.py:607
  35.5 33.0 %all-to-all-start = ((f32[256,1,128]{2,1,0:T(1,128)}), f32[256,1,128]{2,1,0:T(1,128)S(1)}, u32[]{:S(2)}, u32[]{:S(2)}) async-start(f32[256,1,128]{2,1,0:T(1,128)} %bitcast.13), calls=%async_computation | async-start | bytes 262144 | tf_op jit(solution)/shard_map/all_to_all | solution.py:729

commit v4 on v3

--- a/solution.py
+++ b/solution.py
@@ -39,6 +39,10 @@
 
 def row_ids():
     return lax.broadcasted_iota(jnp.int32, (8, LANES), 0)
+
+
+def flags(info, first):
+    return [info[first + n].astype(jnp.float32) for n in range(4)]
 
 
 def roll(value, shift):
@@ -182,7 +186,8 @@
                 out[field, start, at, :] = packed
 
 
-def halo_kernel(info, keep, inner, x_band, z_band, corner, out, low):
+def halo_kernel(info, inner, x_band, z_band, corner, out, low):
+    keep = flags(info, 4)
     fill_low_tiles(low, z_band, corner, keep[0], keep[1])
     pack_bands(inner, out, low, x_band, keep[0], other_layout(info[0]))
 
@@ -204,9 +209,10 @@
 
 
 def weights_kernel(
-    info, keep, iterate, source, wave, inner, x_band, z_band, corner,
+    info, iterate, source, wave, inner, x_band, z_band, corner,
     e_re, e_im, f_re, f_im, movers, mine, low,
 ):
+    keep = flags(info, 4)
     half = info[0]
     keep_x = keep[0]
     lane = lax.broadcasted_iota(jnp.int32, (16, 2 * LANES), 1)
@@ -246,10 +252,11 @@
 
 
 def relax_kernel(
-    info, keep, iterate, x_band, z_band, corner, e_re, e_im, f_re, f_im, movers, mine, halo,
+    info, iterate, x_band, z_band, corner, e_re, e_im, f_re, f_im, movers, mine, halo,
     own, beside, x_a, x_b, z_first, z_last,
     low, w, h, he_re, he_im, hf_re, hf_im, hq, hr, hs, mq, mr, sides,
 ):
+    keep = flags(info, 4)
     half = info[0]
     active = info[1]
     odd = info[2]
@@ -464,7 +471,8 @@
                 face[part, pl.ds(SIDE_ROW + s, 1), :] = beside[part, s, pl.ds(8 + z, 1), :]
 
 
-def face_kernel(info, keep, z_first, z_last, x_a, x_b, a_out, b_out, first, last):
+def face_kernel(info, z_first, z_last, x_a, x_b, a_out, b_out, first, last):
+    keep = flags(info, 8)
     odd_x = info[2] == 1
     odd_z = info[3] == 1
     group = lax.broadcasted_iota(jnp.int32, (1, LANES), 1) // GROUP
@@ -488,9 +496,10 @@
 
 
 def residual_kernel(
-    info, keep, field, source, wave, beside, x_a, x_b, z_a, z_b,
+    info, field, source, wave, beside, x_a, x_b, z_a, z_b,
     out, total, box, sides, mq, mr, hs, z_low, z_high,
 ):
+    keep = flags(info, 8)
     half = info[0]
     odd_x = info[2] == 1
     odd_z = info[3] == 1
@@ -625,25 +634,14 @@
     size_x, size_z, size_y = lax.axis_size("gx"), lax.axis_size("gz"), lax.axis_size("gy")
     at_x, at_z, half = lax.axis_index("gx"), lax.axis_index("gz"), lax.axis_index("gy")
     active = (jnp.mod(at_x + at_z - front[0], size_z) == 0).astype(jnp.int32)
-    info = jnp.stack([half, active, at_x % 2, at_z % 2]).astype(jnp.int32)
     flag_bits = pml_flags[0, 0]
-    as_float = lambda test: test.astype(jnp.float32)
-    band_keep = jnp.stack(
+    info = jnp.stack(
         [
-            as_float(at_x > 0),
-            as_float(at_z > 0),
-            as_float(flag_bits % 2),
-            as_float(flag_bits // 2 % 2),
+            half, active, at_x % 2, at_z % 2,
+            at_x > 0, at_z > 0, flag_bits % 2, flag_bits // 2 % 2,
+            at_x > 0, at_x < size_x - 1, at_z > 0, at_z < size_z - 1,
         ]
-    )
-    box_keep = jnp.stack(
-        [
-            as_float(at_x > 0),
-            as_float(at_x < size_x - 1),
-            as_float(at_z > 0),
-            as_float(at_z < size_z - 1),
-        ]
-    )
+    ).astype(jnp.int32)
 
     def call(kernel, outs, ins, name, scratch=(), place=VMEM, sems=0):
         scalars = sum(value.ndim == 1 for value in ins)
@@ -678,7 +676,7 @@
     halo = call(
         halo_kernel,
         packed,
-        (info, band_keep, theirs, x_band, z_band, corner),
+        (info, theirs, x_band, z_band, corner),
         "pack_halo",
         [low_tiles],
     )
@@ -692,14 +690,14 @@
         weights_kernel,
         (f32(*planes),) * 4
         + (jax.ShapeDtypeStruct((MOVERS, 2 * LANES, 2 * LANES), jnp.bfloat16), packed),
-        (info, band_keep, iterate, source, wave_sq, mine, x_band, z_band, corner),
+        (info, iterate, source, wave_sq, mine, x_band, z_band, corner),
         "weights",
         [low_tiles],
     )
     new, beside, x_a, x_b, z_first, z_last = call(
         relax_kernel,
         (in_vmem, f32(2, STRIDE, 32, LANES), x_face, x_face, z_face, z_face),
-        (info, band_keep, iterate, x_band, z_band, corner, *weights, halo),
+        (info, iterate, x_band, z_band, corner, *weights, halo),
         "relax",
         [(2,) + low_tiles[1:], box_like, pack_like]
         + [packs] * 4
@@ -712,7 +710,7 @@
     z_a, z_b = call(
         face_kernel,
         (z_face, z_face),
-        (info, box_keep, z_first, z_last, x_a, x_b),
+        (info, z_first, z_last, x_a, x_b),
         "faces",
         [z_face.shape] * 2,
     )
@@ -721,7 +719,7 @@
     residual, total = call(
         residual_kernel,
         (in_vmem, pltpu.VMEM((count, LANES), jnp.float32)),
-        (info, box_keep, new, source, wave_sq, beside, x_a, x_b, z_a, z_b),
+        (info, new, source, wave_sq, beside, x_a, x_b, z_a, z_b),
         "residual",
         [(2, CX + 2, 48, LANES), (2, STRIDE, 48, LANES), own, own, (2, STRIDE, CZ, LANES)]
         + [z_face.shape] * 2,

time: 70.1 us -> 68.8 us (0.981)
  starting transfers between devices: 38.1 us -> 31 us
  waiting for transfers between devices: 18.2 us -> 24.1 us
    all_to_all x1, starting transfers between devices: 20 us -> 13.3 us  [on_device(): parts = lax.all_to_all(total, ('gx', 'gz', 'gy'), 0, 0, tiled=True)]
    ppermute x1, waiting for transfers between devices: 3.16 us -> 7.18 us  [diagonal(): return lax.ppermute(value, ('gx', 'gz'), pairs)]
    ppermute x4, waiting for transfers between devices: 3.37 us -> 5.6 us  [pairs(): return lax.ppermute(value, axis, moves)]
    ppermute x1, starting transfers between devices: 3.56 us -> 2.65 us  [diagonal(): return lax.ppermute(value, ('gx', 'gz'), pairs)]
    ppermute x2, starting transfers between devices: 2.93 us -> 3.84 us  [ring(): lax.ppermute(value, axis, [(i, (i + by) % size) for i in range(size)])]
where the time goes in v4:
time: 68.8 us; the launch traced here: 68.6 us
  starting transfers between devices  31 us (45%)
  waiting for transfers between devices  24.1 us (35%)
  Pallas kernels  8.18 us (12%)
  between operations  3.31 us (5%)
  local copies, waits for them, and re-layouts  1.73 us (3%)
    all_to_all x1, starting transfers between devices, on_device(): parts = lax.all_to_all(total, ('gx', 'gz', 'gy'), 0, 0, tiled=True)  13.3 us
    all_to_all x1, waiting for transfers between devices, on_device(): parts = lax.all_to_all(total, ('gx', 'gz', 'gy'), 0, 0, tiled=True)  11.3 us
    ppermute x4, starting transfers between devices, pairs(): return lax.ppermute(value, axis, moves)  9.59 us
    pallas_call x7, Pallas kernels, call(): pl.pallas_call(kernel, out_shape=outs, in_specs=[SMEM] * scalars + [place...  8.18 us
    ppermute x1, waiting for transfers between devices, diagonal(): return lax.ppermute(value, ('gx', 'gz'), pairs)  7.18 us
    ppermute x4, waiting for transfers between devices, pairs(): return lax.ppermute(value, axis, moves)  5.6 us
    ppermute x2, starting transfers between devices, ring(): lax.ppermute(value, axis, [(i, (i + by) % size) for i in range(size)])  3.84 us
    ppermute x1, starting transfers between devices, diagonal(): return lax.ppermute(value, ('gx', 'gz'), pairs)  2.65 us
  transfers between devices with their start and end apart: 9, of which 5 were waited for; matrix products, arithmetic and copies ran while one was open for 3% of the time, Pallas kernels for 4%

profile of v4, /device:TPU:1, one launch (start us, length us, event | category | flops | bytes accessed | tf_op | source)
XLA Modules:
  0.0 68.6 jit_solution(7646242288008447297)
XLA Ops:
  0.7 1.4 %bands.1 = (f32[17,24,128]{2,1,0:T(8,128)S(1)}, f32[408,128]{1,0:T(8,128)S(1)}, f32[72,128]{1,0:T(8,128)S(1)}) custom-call(f32[2,24,24,128]{3,2,1,0:T(8,128)} %iterate.7, f32[2,24,24,128]{3,2,1,0:T(8,128)} %source.7, f32[24,24,128]{2,1,0:T(8,128)} %wave.7), custom_call_target="tpu_custom_call" | custom-call | tf_op jit(solution)/shard_map/bands/pallas_call | solution.py:648
  2.1 2.2 %collective-permute-start = (f32[17,24,128]{2,1,0:T(8,128)S(1)}, f32[17,24,128]{2,1,0:T(8,128)S(1)}, u32[]{:S(2)}, u32[]{:S(2)}) collective-permute-start(f32[17,24,128]{2,1,0:T(8,128)S(1)} %get-tuple-element.24), channel_id=1, source_target_pairs={{0,16},{16,32},{32,48},{48,64},{64,80},{80,96},{96,112},{112,128},... | collective-permute-start | bytes 626696 | tf_op jit(solution)/shard_map/ppermute | solution.py:607
  4.3 1.6 %collective-permute-start.1 = (f32[408,128]{1,0:T(8,128)S(1)}, f32[408,128]{1,0:T(8,128)S(1)}, u32[]{:S(2)}, u32[]{:S(2)}) collective-permute-start(f32[408,128]{1,0:T(8,128)S(1)} %get-tuple-element.25), channel_id=1, source_target_pairs={{0,2},{2,4},{4,6},{6,8},{8,10},{10,12},{12,14},{14,0},{1,3},{3,5},... | collective-permute-start | bytes 626696 | tf_op jit(solution)/shard_map/ppermute | solution.py:607
  5.9 2.6 %collective-permute-start.2 = (f32[72,128]{1,0:T(8,128)S(1)}, f32[72,128]{1,0:T(8,128)S(1)}, u32[]{:S(2)}, u32[]{:S(2)}) collective-permute-start(f32[72,128]{1,0:T(8,128)S(1)} %get-tuple-element.26), channel_id=1, source_target_pairs={{0,18},{2,20},{4,22},{6,24},{8,26},{10,28},{12,30},{14,16},{16,34}... | collective-permute-start | bytes 110600 | tf_op jit(solution)/shard_map/ppermute | solution.py:626
  10.1 1.4 %pack_inner.1 = (f32[5,4,32,128]{3,2,1,0:T(8,128)S(1)}, f32[5,4,32,128]{3,2,1,0:T(8,128)S(1)}) custom-call(s32[12]{0:T(128)S(1)} %stack.65.info, f32[2,24,24,128]{3,2,1,0:T(8,128)S(1)} %copy-done, f32[2,24,24,128]{3,2,1,0:T(8,128)S(1)} %copy-done.1, f32[24,24,128]{2,1,0:T(8,128)S(1)} %copy-done.2), custom_call_target="tpu_custom_call" | custom-call | tf_op jit(solution)/shard_map/pack_inner/pallas_call | solution.py:648
  11.4 7.2 %collective-permute-done.2.corner = f32[72,128]{1,0:T(8,128)S(1)} collective-permute-done((f32[72,128]{1,0:T(8,128)S(1)}, f32[72,128]{1,0:T(8,128)S(1)}, u32[]{:S(2)}, u32[]{:S(2)}) %collective-permute-start.2) | collective-permute-done | bytes 36896 | tf_op jit(solution)/shard_map/ppermute | solution.py:626
  18.6 0.9 %pack_halo.1 = f32[5,4,32,128]{3,2,1,0:T(8,128)S(1)} custom-call(s32[12]{0:T(128)S(1)} %stack.65.info, f32[5,4,32,128]{3,2,1,0:T(8,128)S(1)} %get-tuple-element.34.inner, f32[17,24,128]{2,1,0:T(8,128)S(1)} %collective-permute-done.x_band, f32[408,128]{1,0:T(8,128)S(1)} %collective-permute-done.1.z_band, f32[72,128]{1,0:T(8,128)S(1)} %collective-permute-done.2.corner), custom_call_target="tpu_custom_call" | custom-call | tf_op jit(solution)/shard_map/pack_halo/pallas_call | solution.py:648
  19.5 1.7 %collective-permute-start.3 = (f32[5,4,32,128]{3,2,1,0:T(8,128)S(1)}, f32[5,4,32,128]{3,2,1,0:T(8,128)S(1)}, u32[]{:S(2)}, u32[]{:S(2)}) collective-permute-start(f32[5,4,32,128]{3,2,1,0:T(8,128)S(1)} %pack_halo.1), channel_id=1, source_target_pairs={{0,1},{1,0},{2,3},{3,2},{4,5},{5,4},{6,7},{7,6},{8,9},{9,8},{10,11... | collective-permute-start | bytes 983048 | tf_op jit(solution)/shard_map/ppermute | solution.py:630
  21.2 1.2 %weights.1 = (f32[28,32,128]{2,1,0:T(8,128)S(1)}, f32[28,32,128]{2,1,0:T(8,128)S(1)}, f32[28,32,128]{2,1,0:T(8,128)S(1)}, f32[28,32,128]{2,1,0:T(8,128)S(1)}, bf...) custom-call(s32[12]{0:T(128)S(1)} %stack.65.info, f32[2,24,24,128]{3,2,1,0:T(8,128)S(1)} %copy-done, ...), custom_call_target="tpu_custom_call" | custom-call | tf_op jit(solution)/shard_map/weights/pallas_call | solution.py:648
  22.4 0.7 %relax.1 = (f32[2,24,24,128]{3,2,1,0:T(8,128)S(1)}, f32[2,4,32,128]{3,2,1,0:T(8,128)S(1)}, f32[56,128]{1,0:T(8,128)S(1)}, f32[56,128]{1,0:T(8,128)S(1)}, f32[2,3...) custom-call(s32[12]{0:T(128)S(1)} %stack.65.info, f32[2,24,24,128]{3,2,1,0:T(8,128)S(1)} %copy-done, ...), custom_call_target="tpu_custom_call" | custom-call | tf_op jit(solution)/shard_map/relax/pallas_call | solution.py:648
  23.1 0.1 collective-permute-start.4
  23.2 1.8 %collective-permute-start.5 = (f32[56,128]{1,0:T(8,128)S(1)}, f32[56,128]{1,0:T(8,128)S(1)}, u32[]{:S(2)}, u32[]{:S(2)}) collective-permute-start(f32[56,128]{1,0:T(8,128)S(1)} %get-tuple-element.38), channel_id=1, source_target_pairs={{16,32},{32,16},{48,64},{64,48},{80,96},{96,80},{112,128},{128,112... | collective-permute-start | bytes 86024 | tf_op jit(solution)/shard_map/ppermute | solution.py:616
  25.1 0.9 %collective-permute-done.4.x_a = f32[56,128]{1,0:T(8,128)S(1)} collective-permute-done((f32[56,128]{1,0:T(8,128)S(1)}, f32[56,128]{1,0:T(8,128)S(1)}, u32[]{:S(2)}, u32[]{:S(2)}) %collective-permute-start.4) | collective-permute-done | bytes 28704 | tf_op jit(solution)/shard_map/ppermute | solution.py:616
  25.9 3.4 %collective-permute-done.5.x_b = f32[56,128]{1,0:T(8,128)S(1)} collective-permute-done((f32[56,128]{1,0:T(8,128)S(1)}, f32[56,128]{1,0:T(8,128)S(1)}, u32[]{:S(2)}, u32[]{:S(2)}) %collective-permute-start.5) | collective-permute-done | bytes 28704 | tf_op jit(solution)/shard_map/ppermute | solution.py:616
  29.4 0.6 faces.1
  30.0 0.1 collective-permute-start.6
  30.1 7.6 %collective-permute-start.7 = (f32[2,32,128]{2,1,0:T(8,128)S(1)}, f32[2,32,128]{2,1,0:T(8,128)S(1)}, u32[]{:S(2)}, u32[]{:S(2)}) collective-permute-start(f32[2,32,128]{2,1,0:T(8,128)S(1)} %get-tuple-element.42), channel_id=1, source_target_pairs={{2,4},{4,2},{6,8},{8,6},{10,12},{12,10},{14,0},{0,14},{3,5},{5,3},... | collective-permute-start | bytes 98312 | tf_op jit(solution)/shard_map/ppermute | solution.py:616
  37.7 1.3 %collective-permute-done.7.z_b = f32[2,32,128]{2,1,0:T(8,128)S(1)} collective-permute-done((f32[2,32,128]{2,1,0:T(8,128)S(1)}, f32[2,32,128]{2,1,0:T(8,128)S(1)}, u32[]{:S(2)}, u32[]{:S(2)}) %collective-permute-start.7) | collective-permute-done | bytes 32800 | tf_op jit(solution)/shard_map/ppermute | solution.py:616
  39.0 2.0 %residual.1 = (f32[2,24,24,128]{3,2,1,0:T(8,128)S(1)}, f32[256,128]{1,0:T(8,128)}) custom-call(s32[12]{0:T(128)S(1)} %stack.65.info, f32[2,24,24,128]{3,2,1,0:T(8,128)S(1)} %get-tuple-element.45.field, f32[2,24,24,128]{3,2,1,0:T(8,128)S(1)} %copy-done.1, f32[24,24,128]{2,1,0:T(8,128)S(1)} %copy-done.2, f32[2,4,32,128]{3,2,1,0:T(8,128)S(1)} %get-tuple-element.36.beside, ...), custom_call_target="tpu_custom_call" | custom-call | tf_op jit(solution)/shard_map/residual/pallas_call | solution.py:648
  40.9 13.3 %all-to-all-start = ((f32[256,1,128]{2,1,0:T(1,128)}), f32[256,1,128]{2,1,0:T(1,128)S(1)}, u32[]{:S(2)}, u32[]{:S(2)}) async-start(f32[256,1,128]{2,1,0:T(1,128)} %bitcast.13), calls=%async_computation | async-start | bytes 262144 | tf_op jit(solution)/shard_map/all_to_all | solution.py:727
  54.2 0.8 %copy.9 = f32[2,24,24,128]{3,2,1,0:T(8,128)} copy(f32[2,24,24,128]{3,2,1,0:T(8,128)S(1)} %get-tuple-element.45.field) | data formatting | bytes 1179648
  55.0 0.8 %copy.10 = f32[2,24,24,128]{3,2,1,0:T(8,128)} copy(f32[2,24,24,128]{3,2,1,0:T(8,128)S(1)} %get-tuple-element.46) | data formatting | bytes 1179648
  55.8 11.3 %all-to-all-done = f32[256,1,128]{2,1,0:T(1,128)S(1)} async-done(((f32[256,1,128]{2,1,0:T(1,128)}), f32[256,1,128]{2,1,0:T(1,128)S(1)}, u32[]{:S(2)}, u32[]{:S(2)}) %all-to-all-start) | async-done | bytes 131104 | tf_op jit(solution)/shard_map/all_to_all | solution.py:727
  67.1 0.3 reduce_sum.9
  (11 shorter events, 0.1 us)
Async XLA Ops:
  0.6 9.4 %copy-start = (f32[2,24,24,128]{3,2,1,0:T(8,128)S(1)}, f32[2,24,24,128]{3,2,1,0:T(8,128)}, u32[]{:S(2)}) copy-start(f32[2,24,24,128]{3,2,1,0:T(8,128)} %iterate.7) | copy-start | bytes 1769476
  0.6 9.4 %copy-start.1 = (f32[2,24,24,128]{3,2,1,0:T(8,128)S(1)}, f32[2,24,24,128]{3,2,1,0:T(8,128)}, u32[]{:S(2)}) copy-start(f32[2,24,24,128]{3,2,1,0:T(8,128)} %source.7) | copy-start | bytes 1769476
  0.7 9.4 %copy-start.2 = (f32[24,24,128]{2,1,0:T(8,128)S(1)}, f32[24,24,128]{2,1,0:T(8,128)}, u32[]{:S(2)}) copy-start(f32[24,24,128]{2,1,0:T(8,128)} %wave.7) | copy-start | bytes 884740
  2.1 16.6 %collective-permute-start = (f32[17,24,128]{2,1,0:T(8,128)S(1)}, f32[17,24,128]{2,1,0:T(8,128)S(1)}, u32[]{:S(2)}, u32[]{:S(2)}) collective-permute-start(f32[17,24,128]{2,1,0:T(8,128)S(1)} %get-tuple-element.24), channel_id=1, source_target_pairs={{0,16},{16,32},{32,48},{48,64},{64,80},{80,96},{96,112},{112,128},... | collective-permute-start | bytes 626696 | tf_op jit(solution)/shard_map/ppermute | solution.py:607
  4.3 14.4 %collective-permute-start.1 = (f32[408,128]{1,0:T(8,128)S(1)}, f32[408,128]{1,0:T(8,128)S(1)}, u32[]{:S(2)}, u32[]{:S(2)}) collective-permute-start(f32[408,128]{1,0:T(8,128)S(1)} %get-tuple-element.25), channel_id=1, source_target_pairs={{0,2},{2,4},{4,6},{6,8},{8,10},{10,12},{12,14},{14,0},{1,3},{3,5},... | collective-permute-start | bytes 626696 | tf_op jit(solution)/shard_map/ppermute | solution.py:607
  5.9 12.7 %collective-permute-start.2 = (f32[72,128]{1,0:T(8,128)S(1)}, f32[72,128]{1,0:T(8,128)S(1)}, u32[]{:S(2)}, u32[]{:S(2)}) collective-permute-start(f32[72,128]{1,0:T(8,128)S(1)} %get-tuple-element.26), channel_id=1, source_target_pairs={{0,18},{2,20},{4,22},{6,24},{8,26},{10,28},{12,30},{14,16},{16,34}... | collective-permute-start | bytes 110600 | tf_op jit(solution)/shard_map/ppermute | solution.py:626
  19.5 2.9 %collective-permute-start.3 = (f32[5,4,32,128]{3,2,1,0:T(8,128)S(1)}, f32[5,4,32,128]{3,2,1,0:T(8,128)S(1)}, u32[]{:S(2)}, u32[]{:S(2)}) collective-permute-start(f32[5,4,32,128]{3,2,1,0:T(8,128)S(1)} %pack_halo.1), channel_id=1, source_target_pairs={{0,1},{1,0},{2,3},{3,2},{4,5},{5,4},{6,7},{7,6},{8,9},{9,8},{10,11... | collective-permute-start | bytes 983048 | tf_op jit(solution)/shard_map/ppermute | solution.py:630
  23.1 2.8 %collective-permute-start.4 = (f32[56,128]{1,0:T(8,128)S(1)}, f32[56,128]{1,0:T(8,128)S(1)}, u32[]{:S(2)}, u32[]{:S(2)}) collective-permute-start(f32[56,128]{1,0:T(8,128)S(1)} %get-tuple-element.37), channel_id=1, source_target_pairs={{0,16},{16,0},{32,48},{48,32},{64,80},{80,64},{96,112},{112,96},{1... | collective-permute-start | bytes 86024 | tf_op jit(solution)/shard_map/ppermute | solution.py:616
  23.2 6.1 %collective-permute-start.5 = (f32[56,128]{1,0:T(8,128)S(1)}, f32[56,128]{1,0:T(8,128)S(1)}, u32[]{:S(2)}, u32[]{:S(2)}) collective-permute-start(f32[56,128]{1,0:T(8,128)S(1)} %get-tuple-element.38), channel_id=1, source_target_pairs={{16,32},{32,16},{48,64},{64,48},{80,96},{96,80},{112,128},{128,112... | collective-permute-start | bytes 86024 | tf_op jit(solution)/shard_map/ppermute | solution.py:616
  30.0 7.7 %collective-permute-start.6 = (f32[2,32,128]{2,1,0:T(8,128)S(1)}, f32[2,32,128]{2,1,0:T(8,128)S(1)}, u32[]{:S(2)}, u32[]{:S(2)}) collective-permute-start(f32[2,32,128]{2,1,0:T(8,128)S(1)} %get-tuple-element.41), channel_id=1, source_target_pairs={{0,2},{2,0},{4,6},{6,4},{8,10},{10,8},{12,14},{14,12},{1,3},{3,1},... | collective-permute-start | bytes 98312 | tf_op jit(solution)/shard_map/ppermute | solution.py:616
  30.1 8.9 %collective-permute-start.7 = (f32[2,32,128]{2,1,0:T(8,128)S(1)}, f32[2,32,128]{2,1,0:T(8,128)S(1)}, u32[]{:S(2)}, u32[]{:S(2)}) collective-permute-start(f32[2,32,128]{2,1,0:T(8,128)S(1)} %get-tuple-element.42), channel_id=1, source_target_pairs={{2,4},{4,2},{6,8},{8,6},{10,12},{12,10},{14,0},{0,14},{3,5},{5,3},... | collective-permute-start | bytes 98312 | tf_op jit(solution)/shard_map/ppermute | solution.py:616
  40.9 26.2 %all-to-all-start = ((f32[256,1,128]{2,1,0:T(1,128)}), f32[256,1,128]{2,1,0:T(1,128)S(1)}, u32[]{:S(2)}, u32[]{:S(2)}) async-start(f32[256,1,128]{2,1,0:T(1,128)} %bitcast.13), calls=%async_computation | async-start | bytes 262144 | tf_op jit(solution)/shard_map/all_to_all | solution.py:727

commit v5 on v4

--- a/solution.py
+++ b/solution.py
@@ -155,8 +155,16 @@
     return packed
 
 
-def inner_halo_kernel(info, iterate, source, wave, theirs, mine):
+def inner_halo_kernel(info, iterate, source, wave, theirs, mine, movers):
     half = info[0]
+    lane = lax.broadcasted_iota(jnp.int32, (16, 2 * LANES), 1)
+    row = lax.broadcasted_iota(jnp.int32, (16, 2 * LANES), 0)
+    ends = lane % LANES == (LANES - 1) * (1 - half)
+    for m in range(MOVERS):
+        start = GROUP * (2 * m + lane // LANES) + join_lane(half)
+        for first in range(0, 2 * LANES, 16):
+            hit = ends & ((row + first) % LANES == start)
+            movers[m, pl.ds(first, 16), :] = hit.astype(jnp.float32).astype(jnp.bfloat16)
     fields = [(iterate, 0), (iterate, 1), (source, 0), (source, 1), (wave, None)]
     zeros = jnp.zeros((8, LANES), jnp.float32)
     for field in range(5):
@@ -210,19 +218,11 @@
 
 def weights_kernel(
     info, iterate, source, wave, inner, x_band, z_band, corner,
-    e_re, e_im, f_re, f_im, movers, mine, low,
+    e_re, e_im, f_re, f_im, mine, low,
 ):
     keep = flags(info, 4)
     half = info[0]
     keep_x = keep[0]
-    lane = lax.broadcasted_iota(jnp.int32, (16, 2 * LANES), 1)
-    row = lax.broadcasted_iota(jnp.int32, (16, 2 * LANES), 0)
-    ends = lane % LANES == (LANES - 1) * (1 - half)
-    for m in range(MOVERS):
-        start = GROUP * (2 * m + lane // LANES) + join_lane(half)
-        for first in range(0, 2 * LANES, 16):
-            hit = ends & ((row + first) % LANES == start)
-            movers[m, pl.ds(first, 16), :] = hit.astype(jnp.float32).astype(jnp.bfloat16)
     fill_low_tiles(low, z_band, corner, keep_x, keep[1])
     pack_bands(inner, mine, low, x_band, keep_x, own_layout(half))
     fields = [(iterate, 0), (iterate, 1), (source, 0), (source, 1), (wave, None)]
@@ -670,8 +670,9 @@
     z_band = ring(z_band, "gz", 1)
     low_tiles = (5, EXT, 8, LANES)
     packed = f32(5, STRIDE, 32, LANES)
-    theirs, mine = call(
-        inner_halo_kernel, (packed, packed), (info, iterate, source, wave_sq), "pack_inner"
+    moves = jax.ShapeDtypeStruct((MOVERS, 2 * LANES, 2 * LANES), jnp.bfloat16)
+    theirs, mine, movers = call(
+        inner_halo_kernel, (packed, packed, moves), (info, iterate, source, wave_sq), "pack_inner"
     )
     halo = call(
         halo_kernel,
@@ -686,10 +687,9 @@
     in_vmem = pltpu.VMEM(own, jnp.float32)
     box_like, pack_like = (2, EXT + 2, 48, LANES), (2, STRIDE, 48, LANES)
     x_face, z_face = f32(HALO_ROW + 8, LANES), f32(2, 32, LANES)
-    weights = call(
+    *weights, mine = call(
         weights_kernel,
-        (f32(*planes),) * 4
-        + (jax.ShapeDtypeStruct((MOVERS, 2 * LANES, 2 * LANES), jnp.bfloat16), packed),
+        (f32(*planes),) * 4 + (packed,),
         (info, iterate, source, wave_sq, mine, x_band, z_band, corner),
         "weights",
         [low_tiles],
@@ -697,7 +697,7 @@
     new, beside, x_a, x_b, z_first, z_last = call(
         relax_kernel,
         (in_vmem, f32(2, STRIDE, 32, LANES), x_face, x_face, z_face, z_face),
-        (info, iterate, x_band, z_band, corner, *weights, halo),
+        (info, iterate, x_band, z_band, corner, *weights, movers, mine, halo),
         "relax",
         [(2,) + low_tiles[1:], box_like, pack_like]
         + [packs] * 4

time: 68.8 us -> 68.8 us (level); the launches traced: 68.6 us -> 69.7 us
  waiting for transfers between devices: 24.1 us -> 26.9 us
  starting transfers between devices: 31 us -> 29.4 us
    ppermute x4, starting transfers between devices: 9.59 us -> 5.92 us  [pairs(): return lax.ppermute(value, axis, moves)]
    ppermute x4, waiting for transfers between devices: 5.6 us -> 8.27 us  [pairs(): return lax.ppermute(value, axis, moves)]
    all_to_all x1, starting transfers between devices: 13.3 us -> 15.3 us  [on_device(): parts = lax.all_to_all(total, ('gx', 'gz', 'gy'), 0, 0, tiled=True)]
  transfers between devices with their start and end apart: 9 -> 9, of which waited for: 5 -> 7; matrix products, arithmetic and copies ran while one was open for 3% -> 2% of each run, Pallas kernels for 4% -> 4%
where the time goes in v5:
time: 68.8 us; the launch traced here: 69.7 us
  starting transfers between devices  29.4 us (43%)
  waiting for transfers between devices  26.9 us (39%)
  Pallas kernels  8.02 us (12%)
  between operations  3.31 us (5%)
  local copies, waits for them, and re-layouts  1.73 us (3%)
    all_to_all x1, starting transfers between devices, on_device(): parts = lax.all_to_all(total, ('gx', 'gz', 'gy'), 0, 0, tiled=True)  15.3 us
    all_to_all x1, waiting for transfers between devices, on_device(): parts = lax.all_to_all(total, ('gx', 'gz', 'gy'), 0, 0, tiled=True)  11.3 us
    ppermute x4, waiting for transfers between devices, pairs(): return lax.ppermute(value, axis, moves)  8.27 us
    pallas_call x7, Pallas kernels, call(): pl.pallas_call(kernel, out_shape=outs, in_specs=[SMEM] * scalars + [place...  8.02 us
    ppermute x1, waiting for transfers between devices, diagonal(): return lax.ppermute(value, ('gx', 'gz'), pairs)  7.18 us
    ppermute x4, starting transfers between devices, pairs(): return lax.ppermute(value, axis, moves)  5.92 us
    ppermute x2, starting transfers between devices, ring(): lax.ppermute(value, axis, [(i, (i + by) % size) for i in range(size)])  3.84 us
    ppermute x1, starting transfers between devices, diagonal(): return lax.ppermute(value, ('gx', 'gz'), pairs)  2.65 us
  transfers between devices with their start and end apart: 9, of which 7 were waited for; matrix products, arithmetic and copies ran while one was open for 2% of the time, Pallas kernels for 4%

profile of v5, /device:TPU:1, one launch (start us, length us, event | category | flops | bytes accessed | tf_op | source)
XLA Modules:
  0.0 69.7 jit_solution(2192734223200021004)
XLA Ops:
  0.7 1.4 %bands.1 = (f32[17,24,128]{2,1,0:T(8,128)S(1)}, f32[408,128]{1,0:T(8,128)S(1)}, f32[72,128]{1,0:T(8,128)S(1)}) custom-call(f32[2,24,24,128]{3,2,1,0:T(8,128)} %iterate.7, f32[2,24,24,128]{3,2,1,0:T(8,128)} %source.7, f32[24,24,128]{2,1,0:T(8,128)} %wave.7), custom_call_target="tpu_custom_call" | custom-call | tf_op jit(solution)/shard_map/bands/pallas_call | solution.py:648
  2.1 2.2 %collective-permute-start = (f32[17,24,128]{2,1,0:T(8,128)S(1)}, f32[17,24,128]{2,1,0:T(8,128)S(1)}, u32[]{:S(2)}, u32[]{:S(2)}) collective-permute-start(f32[17,24,128]{2,1,0:T(8,128)S(1)} %get-tuple-element.24), channel_id=1, source_target_pairs={{0,16},{16,32},{32,48},{48,64},{64,80},{80,96},{96,112},{112,128},... | collective-permute-start | bytes 626696 | tf_op jit(solution)/shard_map/ppermute | solution.py:607
  4.3 1.6 %collective-permute-start.1 = (f32[408,128]{1,0:T(8,128)S(1)}, f32[408,128]{1,0:T(8,128)S(1)}, u32[]{:S(2)}, u32[]{:S(2)}) collective-permute-start(f32[408,128]{1,0:T(8,128)S(1)} %get-tuple-element.25), channel_id=1, source_target_pairs={{0,2},{2,4},{4,6},{6,8},{8,10},{10,12},{12,14},{14,0},{1,3},{3,5},... | collective-permute-start | bytes 626696 | tf_op jit(solution)/shard_map/ppermute | solution.py:607
  5.9 2.6 %collective-permute-start.2 = (f32[72,128]{1,0:T(8,128)S(1)}, f32[72,128]{1,0:T(8,128)S(1)}, u32[]{:S(2)}, u32[]{:S(2)}) collective-permute-start(f32[72,128]{1,0:T(8,128)S(1)} %get-tuple-element.26), channel_id=1, source_target_pairs={{0,18},{2,20},{4,22},{6,24},{8,26},{10,28},{12,30},{14,16},{16,34}... | collective-permute-start | bytes 110600 | tf_op jit(solution)/shard_map/ppermute | solution.py:626
  10.1 1.4 %pack_inner.1 = (f32[5,4,32,128]{3,2,1,0:T(8,128)S(1)}, f32[5,4,32,128]{3,2,1,0:T(8,128)S(1)}, bf16[4,256,256]{2,1,0:T(8,128)(2,1)S(1)}) custom-call(s32[12]{0:T(128)S(1)} %stack.65.info, f32[2,24,24,128]{3,2,1,0:T(8,128)S(1)} %copy-done, f32[2,24,24,128]{3,2,1,0:T(8,128)S(1)} %copy-done.1, f32[24,24,128]{2,1,0:T(8,128)S(1)} %copy-done.2), custom_call_target="tpu_custom_call" | custom-call | tf_op jit(solution)/shard_map/pack_inner/pallas_call | solution.py:648
  11.4 7.2 %collective-permute-done.2.corner = f32[72,128]{1,0:T(8,128)S(1)} collective-permute-done((f32[72,128]{1,0:T(8,128)S(1)}, f32[72,128]{1,0:T(8,128)S(1)}, u32[]{:S(2)}, u32[]{:S(2)}) %collective-permute-start.2) | collective-permute-done | bytes 36896 | tf_op jit(solution)/shard_map/ppermute | solution.py:626
  18.6 0.9 %pack_halo.1 = f32[5,4,32,128]{3,2,1,0:T(8,128)S(1)} custom-call(s32[12]{0:T(128)S(1)} %stack.65.info, f32[5,4,32,128]{3,2,1,0:T(8,128)S(1)} %get-tuple-element.34.inner, f32[17,24,128]{2,1,0:T(8,128)S(1)} %collective-permute-done.x_band, f32[408,128]{1,0:T(8,128)S(1)} %collective-permute-done.1.z_band, f32[72,128]{1,0:T(8,128)S(1)} %collective-permute-done.2.corner), custom_call_target="tpu_custom_call" | custom-call | tf_op jit(solution)/shard_map/pack_halo/pallas_call | solution.py:648
  19.5 1.7 %collective-permute-start.3 = (f32[5,4,32,128]{3,2,1,0:T(8,128)S(1)}, f32[5,4,32,128]{3,2,1,0:T(8,128)S(1)}, u32[]{:S(2)}, u32[]{:S(2)}) collective-permute-start(f32[5,4,32,128]{3,2,1,0:T(8,128)S(1)} %pack_halo.1), channel_id=1, source_target_pairs={{0,1},{1,0},{2,3},{3,2},{4,5},{5,4},{6,7},{7,6},{8,9},{9,8},{10,11... | collective-permute-start | bytes 983048 | tf_op jit(solution)/shard_map/ppermute | solution.py:630
  21.2 1.1 %weights.1 = (f32[28,32,128]{2,1,0:T(8,128)S(1)}, f32[28,32,128]{2,1,0:T(8,128)S(1)}, f32[28,32,128]{2,1,0:T(8,128)S(1)}, f32[28,32,128]{2,1,0:T(8,128)S(1)}, f32[5,4,32,128]{3,2,1,0:T(8,128)S(1)}) custom-call(s32[12]{0:T(128)S(1)} %stack.65.info, f32[2,24,24,128]{3,2,1,0:T(8,128)S(1)} %copy-done, f32[2,24,24,128]{3,2,1,0:T(8,128)S(1)} %copy-done.1, ...), custom_call_target="tpu_custom_call" | custom-call | tf_op jit(solution)/shard_map/weights/pallas_call | solution.py:648
  22.2 0.2 collective-permute-done.3.halo
  22.4 0.7 %relax.1 = (f32[2,24,24,128]{3,2,1,0:T(8,128)S(1)}, f32[2,4,32,128]{3,2,1,0:T(8,128)S(1)}, f32[56,128]{1,0:T(8,128)S(1)}, f32[56,128]{1,0:T(8,128)S(1)}, f32[2,3...) custom-call(s32[12]{0:T(128)S(1)} %stack.65.info, f32[2,24,24,128]{3,2,1,0:T(8,128)S(1)} %copy-done, ...), custom_call_target="tpu_custom_call" | custom-call | tf_op jit(solution)/shard_map/relax/pallas_call | solution.py:648
  23.2 1.8 %collective-permute-start.5 = (f32[56,128]{1,0:T(8,128)S(1)}, f32[56,128]{1,0:T(8,128)S(1)}, u32[]{:S(2)}, u32[]{:S(2)}) collective-permute-start(f32[56,128]{1,0:T(8,128)S(1)} %get-tuple-element.38), channel_id=1, source_target_pairs={{16,32},{32,16},{48,64},{64,48},{80,96},{96,80},{112,128},{128,112... | collective-permute-start | bytes 86024 | tf_op jit(solution)/shard_map/ppermute | solution.py:616
  25.1 0.9 %collective-permute-done.4.x_a = f32[56,128]{1,0:T(8,128)S(1)} collective-permute-done((f32[56,128]{1,0:T(8,128)S(1)}, f32[56,128]{1,0:T(8,128)S(1)}, u32[]{:S(2)}, u32[]{:S(2)}) %collective-permute-start.4) | collective-permute-done | bytes 28704 | tf_op jit(solution)/shard_map/ppermute | solution.py:616
  25.9 3.4 %collective-permute-done.5.x_b = f32[56,128]{1,0:T(8,128)S(1)} collective-permute-done((f32[56,128]{1,0:T(8,128)S(1)}, f32[56,128]{1,0:T(8,128)S(1)}, u32[]{:S(2)}, u32[]{:S(2)}) %collective-permute-start.5) | collective-permute-done | bytes 28704 | tf_op jit(solution)/shard_map/ppermute | solution.py:616
  29.4 0.6 faces.1
  30.0 4.0 %collective-permute-start.6 = (f32[2,32,128]{2,1,0:T(8,128)S(1)}, f32[2,32,128]{2,1,0:T(8,128)S(1)}, u32[]{:S(2)}, u32[]{:S(2)}) collective-permute-start(f32[2,32,128]{2,1,0:T(8,128)S(1)} %get-tuple-element.41), channel_id=1, source_target_pairs={{0,2},{2,0},{4,6},{6,4},{8,10},{10,8},{12,14},{14,12},{1,3},{3,1},... | collective-permute-start | bytes 98312 | tf_op jit(solution)/shard_map/ppermute | solution.py:616
  34.0 1.3 %collective-permute-done.6.z_a = f32[2,32,128]{2,1,0:T(8,128)S(1)} collective-permute-done((f32[2,32,128]{2,1,0:T(8,128)S(1)}, f32[2,32,128]{2,1,0:T(8,128)S(1)}, u32[]{:S(2)}, u32[]{:S(2)}) %collective-permute-start.6) | collective-permute-done | bytes 32800 | tf_op jit(solution)/shard_map/ppermute | solution.py:616
  35.3 2.7 %collective-permute-done.7.z_b = f32[2,32,128]{2,1,0:T(8,128)S(1)} collective-permute-done((f32[2,32,128]{2,1,0:T(8,128)S(1)}, f32[2,32,128]{2,1,0:T(8,128)S(1)}, u32[]{:S(2)}, u32[]{:S(2)}) %collective-permute-start.7) | collective-permute-done | bytes 32800 | tf_op jit(solution)/shard_map/ppermute | solution.py:616
  38.0 2.0 %residual.1 = (f32[2,24,24,128]{3,2,1,0:T(8,128)S(1)}, f32[256,128]{1,0:T(8,128)}) custom-call(s32[12]{0:T(128)S(1)} %stack.65.info, f32[2,24,24,128]{3,2,1,0:T(8,128)S(1)} %get-tuple-element.45.field, f32[2,24,24,128]{3,2,1,0:T(8,128)S(1)} %copy-done.1, f32[24,24,128]{2,1,0:T(8,128)S(1)} %copy-done.2, f32[2,4,32,128]{3,2,1,0:T(8,128)S(1)} %get-tuple-element.36.beside, ...), custom_call_target="tpu_custom_call" | custom-call | tf_op jit(solution)/shard_map/residual/pallas_call | solution.py:648
  39.9 15.3 %all-to-all-start = ((f32[256,1,128]{2,1,0:T(1,128)}), f32[256,1,128]{2,1,0:T(1,128)S(1)}, u32[]{:S(2)}, u32[]{:S(2)}) async-start(f32[256,1,128]{2,1,0:T(1,128)} %bitcast.13), calls=%async_computation | async-start | bytes 262144 | tf_op jit(solution)/shard_map/all_to_all | solution.py:727
  55.3 0.8 %copy.9 = f32[2,24,24,128]{3,2,1,0:T(8,128)} copy(f32[2,24,24,128]{3,2,1,0:T(8,128)S(1)} %get-tuple-element.45.field) | data formatting | bytes 1179648
  56.1 0.8 %copy.10 = f32[2,24,24,128]{3,2,1,0:T(8,128)} copy(f32[2,24,24,128]{3,2,1,0:T(8,128)S(1)} %get-tuple-element.46) | data formatting | bytes 1179648
  56.9 11.3 %all-to-all-done = f32[256,1,128]{2,1,0:T(1,128)S(1)} async-done(((f32[256,1,128]{2,1,0:T(1,128)}), f32[256,1,128]{2,1,0:T(1,128)S(1)}, u32[]{:S(2)}, u32[]{:S(2)}) %all-to-all-start) | async-done | bytes 131104 | tf_op jit(solution)/shard_map/all_to_all | solution.py:727
  68.2 0.3 reduce_sum.9
  (11 shorter events, 0.2 us)
Async XLA Ops:
  0.6 9.4 %copy-start = (f32[2,24,24,128]{3,2,1,0:T(8,128)S(1)}, f32[2,24,24,128]{3,2,1,0:T(8,128)}, u32[]{:S(2)}) copy-start(f32[2,24,24,128]{3,2,1,0:T(8,128)} %iterate.7) | copy-start | bytes 1769476
  0.6 9.4 %copy-start.1 = (f32[2,24,24,128]{3,2,1,0:T(8,128)S(1)}, f32[2,24,24,128]{3,2,1,0:T(8,128)}, u32[]{:S(2)}) copy-start(f32[2,24,24,128]{3,2,1,0:T(8,128)} %source.7) | copy-start | bytes 1769476
  0.7 9.4 %copy-start.2 = (f32[24,24,128]{2,1,0:T(8,128)S(1)}, f32[24,24,128]{2,1,0:T(8,128)}, u32[]{:S(2)}) copy-start(f32[24,24,128]{2,1,0:T(8,128)} %wave.7) | copy-start | bytes 884740
  2.1 16.6 %collective-permute-start = (f32[17,24,128]{2,1,0:T(8,128)S(1)}, f32[17,24,128]{2,1,0:T(8,128)S(1)}, u32[]{:S(2)}, u32[]{:S(2)}) collective-permute-start(f32[17,24,128]{2,1,0:T(8,128)S(1)} %get-tuple-element.24), channel_id=1, source_target_pairs={{0,16},{16,32},{32,48},{48,64},{64,80},{80,96},{96,112},{112,128},... | collective-permute-start | bytes 626696 | tf_op jit(solution)/shard_map/ppermute | solution.py:607
  4.3 14.4 %collective-permute-start.1 = (f32[408,128]{1,0:T(8,128)S(1)}, f32[408,128]{1,0:T(8,128)S(1)}, u32[]{:S(2)}, u32[]{:S(2)}) collective-permute-start(f32[408,128]{1,0:T(8,128)S(1)} %get-tuple-element.25), channel_id=1, source_target_pairs={{0,2},{2,4},{4,6},{6,8},{8,10},{10,12},{12,14},{14,0},{1,3},{3,5},... | collective-permute-start | bytes 626696 | tf_op jit(solution)/shard_map/ppermute | solution.py:607
  5.9 12.7 %collective-permute-start.2 = (f32[72,128]{1,0:T(8,128)S(1)}, f32[72,128]{1,0:T(8,128)S(1)}, u32[]{:S(2)}, u32[]{:S(2)}) collective-permute-start(f32[72,128]{1,0:T(8,128)S(1)} %get-tuple-element.26), channel_id=1, source_target_pairs={{0,18},{2,20},{4,22},{6,24},{8,26},{10,28},{12,30},{14,16},{16,34}... | collective-permute-start | bytes 110600 | tf_op jit(solution)/shard_map/ppermute | solution.py:626
  19.5 2.9 %collective-permute-start.3 = (f32[5,4,32,128]{3,2,1,0:T(8,128)S(1)}, f32[5,4,32,128]{3,2,1,0:T(8,128)S(1)}, u32[]{:S(2)}, u32[]{:S(2)}) collective-permute-start(f32[5,4,32,128]{3,2,1,0:T(8,128)S(1)} %pack_halo.1), channel_id=1, source_target_pairs={{0,1},{1,0},{2,3},{3,2},{4,5},{5,4},{6,7},{7,6},{8,9},{9,8},{10,11... | collective-permute-start | bytes 983048 | tf_op jit(solution)/shard_map/ppermute | solution.py:630
  23.1 2.8 %collective-permute-start.4 = (f32[56,128]{1,0:T(8,128)S(1)}, f32[56,128]{1,0:T(8,128)S(1)}, u32[]{:S(2)}, u32[]{:S(2)}) collective-permute-start(f32[56,128]{1,0:T(8,128)S(1)} %get-tuple-element.37), channel_id=1, source_target_pairs={{0,16},{16,0},{32,48},{48,32},{64,80},{80,64},{96,112},{112,96},{1... | collective-permute-start | bytes 86024 | tf_op jit(solution)/shard_map/ppermute | solution.py:616
  23.2 6.1 %collective-permute-start.5 = (f32[56,128]{1,0:T(8,128)S(1)}, f32[56,128]{1,0:T(8,128)S(1)}, u32[]{:S(2)}, u32[]{:S(2)}) collective-permute-start(f32[56,128]{1,0:T(8,128)S(1)} %get-tuple-element.38), channel_id=1, source_target_pairs={{16,32},{32,16},{48,64},{64,48},{80,96},{96,80},{112,128},{128,112... | collective-permute-start | bytes 86024 | tf_op jit(solution)/shard_map/ppermute | solution.py:616
  30.0 5.3 %collective-permute-start.6 = (f32[2,32,128]{2,1,0:T(8,128)S(1)}, f32[2,32,128]{2,1,0:T(8,128)S(1)}, u32[]{:S(2)}, u32[]{:S(2)}) collective-permute-start(f32[2,32,128]{2,1,0:T(8,128)S(1)} %get-tuple-element.41), channel_id=1, source_target_pairs={{0,2},{2,0},{4,6},{6,4},{8,10},{10,8},{12,14},{14,12},{1,3},{3,1},... | collective-permute-start | bytes 98312 | tf_op jit(solution)/shard_map/ppermute | solution.py:616
  34.0 4.0 %collective-permute-start.7 = (f32[2,32,128]{2,1,0:T(8,128)S(1)}, f32[2,32,128]{2,1,0:T(8,128)S(1)}, u32[]{:S(2)}, u32[]{:S(2)}) collective-permute-start(f32[2,32,128]{2,1,0:T(8,128)S(1)} %get-tuple-element.42), channel_id=1, source_target_pairs={{2,4},{4,2},{6,8},{8,6},{10,12},{12,10},{14,0},{0,14},{3,5},{5,3},... | collective-permute-start | bytes 98312 | tf_op jit(solution)/shard_map/ppermute | solution.py:616
  39.9 28.3 %all-to-all-start = ((f32[256,1,128]{2,1,0:T(1,128)}), f32[256,1,128]{2,1,0:T(1,128)S(1)}, u32[]{:S(2)}, u32[]{:S(2)}) async-start(f32[256,1,128]{2,1,0:T(1,128)} %bitcast.13), calls=%async_computation | async-start | bytes 262144 | tf_op jit(solution)/shard_map/all_to_all | solution.py:727

commit v6 on v5

--- a/solution.py
+++ b/solution.py
@@ -496,11 +496,10 @@
 
 
 def residual_kernel(
-    info, field, source, wave, beside, x_a, x_b, z_a, z_b,
-    out, total, box, sides, mq, mr, hs, z_low, z_high,
+    info, field, source, wave, beside, movers, x_a, x_b, z_a, z_b,
+    out, total, box, sides, mq, mr, hs, moved_to, z_low, z_high,
 ):
     keep = flags(info, 8)
-    half = info[0]
     odd_x = info[2] == 1
     odd_z = info[3] == 1
     z_low[...] = jnp.where(odd_z, z_a[...], z_b[...])
@@ -542,7 +541,6 @@
             ref[part, plane, pl.ds(base - 1, 8), :] + ref[part, plane, pl.ds(base + 1, 8), :]
         )
 
-    joined = lanes % GROUP == join_lane(half)
     for part in range(2):
         for tile in range(3):
             at = pl.ds(8 * tile, 8)
@@ -555,7 +553,17 @@
                     both[s + 1][0], both[s][0] + both[s + 2][0],
                     both[s + 1][1], both[s][1] + both[s + 2][1],
                 )
-                hs[part, s, at, :] = jnp.where(joined, q, 0.0)
+                hs[pl.ds(CZ * (STRIDE * part + s) + 8 * tile, 8), :] = q
+
+    value = hs[...]
+    head = value.astype(jnp.bfloat16)
+    tail = (value - head.astype(jnp.float32)).astype(jnp.bfloat16)
+    both = jnp.concatenate([head, tail], 1)
+    for m in range(MOVERS):
+        moved = jnp.dot(both, movers[m], preferred_element_type=jnp.float32)
+        moved_to[2 * m] = moved[:, :LANES]
+        if 2 * m + 1 < PER:
+            moved_to[2 * m + 1] = moved[:, LANES:]
 
     for part in range(2):
         for tile in range(3):
@@ -572,18 +580,19 @@
 
     first_lane = lanes == 0
     last_lane = lanes == LANES - 1
-    to_edge = (LANES - 1) * (1 - half) - join_lane(half)
     squares = [zeros] * 4
     for part in range(2):
         for tile in range(3):
             at = pl.ds(8 * tile, 8)
             for j in range(1, PER):
-                turn = lax.rem(2 * LANES - GROUP * j + to_edge, LANES)
                 planes = range(STRIDE * (j - 1), STRIDE * j)
                 q = [mq[part, x, at, :] for x in planes]
                 up = [roll(value, -1) for value in q]
                 down = [roll(value, 1) for value in q]
-                side = [pltpu.roll(hs[part, s, at, :], turn, 1) for s in range(STRIDE)]
+                side = [
+                    moved_to[j, pl.ds(CZ * (STRIDE * part + s) + 8 * tile, 8), :]
+                    for s in range(STRIDE)
+                ]
                 for n, x in enumerate(planes):
                     y = jnp.where(last_lane, side[n], up[n]) + jnp.where(
                         first_lane, side[n], down[n]
@@ -719,9 +728,10 @@
     residual, total = call(
         residual_kernel,
         (in_vmem, pltpu.VMEM((count, LANES), jnp.float32)),
-        (info, new, source, wave_sq, beside, x_a, x_b, z_a, z_b),
+        (info, new, source, wave_sq, beside, movers, x_a, x_b, z_a, z_b),
         "residual",
-        [(2, CX + 2, 48, LANES), (2, STRIDE, 48, LANES), own, own, (2, STRIDE, CZ, LANES)]
+        [(2, CX + 2, 48, LANES), (2, STRIDE, 48, LANES), own, own]
+        + [(2 * STRIDE * CZ, LANES), (PER, 2 * STRIDE * CZ, LANES)]
         + [z_face.shape] * 2,
     )
     parts = lax.all_to_all(total, ("gx", "gz", "gy"), 0, 0, tiled=True)

time: 68.8 us -> 67.7 us (0.984); the launches traced: 69.7 us -> 67.2 us
  starting transfers between devices: 29.4 us -> 25.2 us
  waiting for transfers between devices: 26.9 us -> 28.7 us
    all_to_all x1, starting transfers between devices: 15.3 us -> 10.4 us  [on_device(): parts = lax.all_to_all(total, ('gx', 'gz', 'gy'), 0, 0, tiled=True)]
    ppermute x4, waiting for transfers between devices: 8.27 us -> 10 us  [pairs(): return lax.ppermute(value, axis, moves)]
  transfers between devices with their start and end apart: 9 -> 9, of which waited for: 7 -> 7; matrix products, arithmetic and copies ran while one was open for 2% -> 3% of each run, Pallas kernels for 4% -> 4%
where the time goes in v6:
time: 67.7 us; the launch traced here: 67.2 us
  waiting for transfers between devices  28.7 us (42%)
  starting transfers between devices  25.2 us (37%)
  Pallas kernels  8.02 us (12%)
  between operations  3.32 us (5%)
  local copies, waits for them, and re-layouts  1.73 us (3%)
    all_to_all x1, waiting for transfers between devices, on_device(): parts = lax.all_to_all(total, ('gx', 'gz', 'gy'), 0, 0, tiled=True)  11.3 us
    all_to_all x1, starting transfers between devices, on_device(): parts = lax.all_to_all(total, ('gx', 'gz', 'gy'), 0, 0, tiled=True)  10.4 us
    ppermute x4, waiting for transfers between devices, pairs(): return lax.ppermute(value, axis, moves)  10 us
    pallas_call x7, Pallas kernels, call(): pl.pallas_call(kernel, out_shape=outs, in_specs=[SMEM] * scalars + [place...  8.02 us
    ppermute x1, waiting for transfers between devices, diagonal(): return lax.ppermute(value, ('gx', 'gz'), pairs)  7.18 us
    ppermute x4, starting transfers between devices, pairs(): return lax.ppermute(value, axis, moves)  6.6 us
    ppermute x2, starting transfers between devices, ring(): lax.ppermute(value, axis, [(i, (i + by) % size) for i in range(size)])  3.84 us
    ppermute x1, starting transfers between devices, diagonal(): return lax.ppermute(value, ('gx', 'gz'), pairs)  2.65 us
  transfers between devices with their start and end apart: 9, of which 7 were waited for; matrix products, arithmetic and copies ran while one was open for 3% of the time, Pallas kernels for 4%

profile of v6, /device:TPU:1, one launch (start us, length us, event | category | flops | bytes accessed | tf_op | source)
XLA Modules:
  0.0 67.2 jit_solution(2461024146405087741)
XLA Ops:
  0.7 1.4 %bands.1 = (f32[17,24,128]{2,1,0:T(8,128)S(1)}, f32[408,128]{1,0:T(8,128)S(1)}, f32[72,128]{1,0:T(8,128)S(1)}) custom-call(f32[2,24,24,128]{3,2,1,0:T(8,128)} %iterate.7, f32[2,24,24,128]{3,2,1,0:T(8,128)} %source.7, f32[24,24,128]{2,1,0:T(8,128)} %wave.7), custom_call_target="tpu_custom_call" | custom-call | tf_op jit(solution)/shard_map/bands/pallas_call | solution.py:657
  2.1 2.2 %collective-permute-start = (f32[17,24,128]{2,1,0:T(8,128)S(1)}, f32[17,24,128]{2,1,0:T(8,128)S(1)}, u32[]{:S(2)}, u32[]{:S(2)}) collective-permute-start(f32[17,24,128]{2,1,0:T(8,128)S(1)} %get-tuple-element.24), channel_id=1, source_target_pairs={{0,16},{16,32},{32,48},{48,64},{64,80},{80,96},{96,112},{112,128},... | collective-permute-start | bytes 626696 | tf_op jit(solution)/shard_map/ppermute | solution.py:616
  4.3 1.6 %collective-permute-start.1 = (f32[408,128]{1,0:T(8,128)S(1)}, f32[408,128]{1,0:T(8,128)S(1)}, u32[]{:S(2)}, u32[]{:S(2)}) collective-permute-start(f32[408,128]{1,0:T(8,128)S(1)} %get-tuple-element.25), channel_id=1, source_target_pairs={{0,2},{2,4},{4,6},{6,8},{8,10},{10,12},{12,14},{14,0},{1,3},{3,5},... | collective-permute-start | bytes 626696 | tf_op jit(solution)/shard_map/ppermute | solution.py:616
  5.9 2.6 %collective-permute-start.2 = (f32[72,128]{1,0:T(8,128)S(1)}, f32[72,128]{1,0:T(8,128)S(1)}, u32[]{:S(2)}, u32[]{:S(2)}) collective-permute-start(f32[72,128]{1,0:T(8,128)S(1)} %get-tuple-element.26), channel_id=1, source_target_pairs={{0,18},{2,20},{4,22},{6,24},{8,26},{10,28},{12,30},{14,16},{16,34}... | collective-permute-start | bytes 110600 | tf_op jit(solution)/shard_map/ppermute | solution.py:635
  10.1 1.4 %pack_inner.1 = (f32[5,4,32,128]{3,2,1,0:T(8,128)S(1)}, f32[5,4,32,128]{3,2,1,0:T(8,128)S(1)}, bf16[4,256,256]{2,1,0:T(8,128)(2,1)S(1)}) custom-call(s32[12]{0:T(128)S(1)} %stack.65.info, f32[2,24,24,128]{3,2,1,0:T(8,128)S(1)} %copy-done, f32[2,24,24,128]{3,2,1,0:T(8,128)S(1)} %copy-done.1, f32[24,24,128]{2,1,0:T(8,128)S(1)} %copy-done.2), custom_call_target="tpu_custom_call" | custom-call | tf_op jit(solution)/shard_map/pack_inner/pallas_call | solution.py:657
  11.4 7.2 %collective-permute-done.2.corner = f32[72,128]{1,0:T(8,128)S(1)} collective-permute-done((f32[72,128]{1,0:T(8,128)S(1)}, f32[72,128]{1,0:T(8,128)S(1)}, u32[]{:S(2)}, u32[]{:S(2)}) %collective-permute-start.2) | collective-permute-done | bytes 36896 | tf_op jit(solution)/shard_map/ppermute | solution.py:635
  18.6 0.9 %pack_halo.1 = f32[5,4,32,128]{3,2,1,0:T(8,128)S(1)} custom-call(s32[12]{0:T(128)S(1)} %stack.65.info, f32[5,4,32,128]{3,2,1,0:T(8,128)S(1)} %get-tuple-element.34.inner, f32[17,24,128]{2,1,0:T(8,128)S(1)} %collective-permute-done.x_band, f32[408,128]{1,0:T(8,128)S(1)} %collective-permute-done.1.z_band, f32[72,128]{1,0:T(8,128)S(1)} %collective-permute-done.2.corner), custom_call_target="tpu_custom_call" | custom-call | tf_op jit(solution)/shard_map/pack_halo/pallas_call | solution.py:657
  19.5 1.7 %collective-permute-start.3 = (f32[5,4,32,128]{3,2,1,0:T(8,128)S(1)}, f32[5,4,32,128]{3,2,1,0:T(8,128)S(1)}, u32[]{:S(2)}, u32[]{:S(2)}) collective-permute-start(f32[5,4,32,128]{3,2,1,0:T(8,128)S(1)} %pack_halo.1), channel_id=1, source_target_pairs={{0,1},{1,0},{2,3},{3,2},{4,5},{5,4},{6,7},{7,6},{8,9},{9,8},{10,11... | collective-permute-start | bytes 983048 | tf_op jit(solution)/shard_map/ppermute | solution.py:639
  21.2 1.1 %weights.1 = (f32[28,32,128]{2,1,0:T(8,128)S(1)}, f32[28,32,128]{2,1,0:T(8,128)S(1)}, f32[28,32,128]{2,1,0:T(8,128)S(1)}, f32[28,32,128]{2,1,0:T(8,128)S(1)}, f32[5,4,32,128]{3,2,1,0:T(8,128)S(1)}) custom-call(s32[12]{0:T(128)S(1)} %stack.65.info, f32[2,24,24,128]{3,2,1,0:T(8,128)S(1)} %copy-done, f32[2,24,24,128]{3,2,1,0:T(8,128)S(1)} %copy-done.1, ...), custom_call_target="tpu_custom_call" | custom-call | tf_op jit(solution)/shard_map/weights/pallas_call | solution.py:657
  22.2 0.2 collective-permute-done.3.halo
  22.4 0.7 %relax.1 = (f32[2,24,24,128]{3,2,1,0:T(8,128)S(1)}, f32[2,4,32,128]{3,2,1,0:T(8,128)S(1)}, f32[56,128]{1,0:T(8,128)S(1)}, f32[56,128]{1,0:T(8,128)S(1)}, f32[2,3...) custom-call(s32[12]{0:T(128)S(1)} %stack.65.info, f32[2,24,24,128]{3,2,1,0:T(8,128)S(1)} %copy-done, ...), custom_call_target="tpu_custom_call" | custom-call | tf_op jit(solution)/shard_map/relax/pallas_call | solution.py:657
  23.1 6.4 %collective-permute-start.4 = (f32[56,128]{1,0:T(8,128)S(1)}, f32[56,128]{1,0:T(8,128)S(1)}, u32[]{:S(2)}, u32[]{:S(2)}) collective-permute-start(f32[56,128]{1,0:T(8,128)S(1)} %get-tuple-element.37), channel_id=1, source_target_pairs={{0,16},{16,0},{32,48},{48,32},{64,80},{80,64},{96,112},{112,96},{1... | collective-permute-start | bytes 86024 | tf_op jit(solution)/shard_map/ppermute | solution.py:625
  29.5 1.3 %collective-permute-done.4.x_a = f32[56,128]{1,0:T(8,128)S(1)} collective-permute-done((f32[56,128]{1,0:T(8,128)S(1)}, f32[56,128]{1,0:T(8,128)S(1)}, u32[]{:S(2)}, u32[]{:S(2)}) %collective-permute-start.4) | collective-permute-done | bytes 28704 | tf_op jit(solution)/shard_map/ppermute | solution.py:625
  30.8 4.8 %collective-permute-done.5.x_b = f32[56,128]{1,0:T(8,128)S(1)} collective-permute-done((f32[56,128]{1,0:T(8,128)S(1)}, f32[56,128]{1,0:T(8,128)S(1)}, u32[]{:S(2)}, u32[]{:S(2)}) %collective-permute-start.5) | collective-permute-done | bytes 28704 | tf_op jit(solution)/shard_map/ppermute | solution.py:625
  35.6 0.6 faces.1
  36.3 0.1 collective-permute-start.7
  36.4 2.7 %collective-permute-done.6.z_a = f32[2,32,128]{2,1,0:T(8,128)S(1)} collective-permute-done((f32[2,32,128]{2,1,0:T(8,128)S(1)}, f32[2,32,128]{2,1,0:T(8,128)S(1)}, u32[]{:S(2)}, u32[]{:S(2)}) %collective-permute-start.6) | collective-permute-done | bytes 32800 | tf_op jit(solution)/shard_map/ppermute | solution.py:625
  39.1 1.3 %collective-permute-done.7.z_b = f32[2,32,128]{2,1,0:T(8,128)S(1)} collective-permute-done((f32[2,32,128]{2,1,0:T(8,128)S(1)}, f32[2,32,128]{2,1,0:T(8,128)S(1)}, u32[]{:S(2)}, u32[]{:S(2)}) %collective-permute-start.7) | collective-permute-done | bytes 32800 | tf_op jit(solution)/shard_map/ppermute | solution.py:625
  40.4 2.0 %residual.1 = (f32[2,24,24,128]{3,2,1,0:T(8,128)S(1)}, f32[256,128]{1,0:T(8,128)}) custom-call(s32[12]{0:T(128)S(1)} %stack.65.info, f32[2,24,24,128]{3,2,1,0:T(8,128)S(1)} %get-tuple-element.45.field, f32[2,24,24,128]{3,2,1,0:T(8,128)S(1)} %copy-done.1, f32[24,24,128]{2,1,0:T(8,128)S(1)} %copy-done.2, f32[2,4,32,128]{3,2,1,0:T(8,128)S(1)} %get-tuple-element.36.beside, ...), custom_call_target="tpu_custom_call" | custom-call | tf_op jit(solution)/shard_map/residual/pallas_call | solution.py:657
  42.3 10.4 %all-to-all-start = ((f32[256,1,128]{2,1,0:T(1,128)}), f32[256,1,128]{2,1,0:T(1,128)S(1)}, u32[]{:S(2)}, u32[]{:S(2)}) async-start(f32[256,1,128]{2,1,0:T(1,128)} %bitcast.13), calls=%async_computation | async-start | bytes 262144 | tf_op jit(solution)/shard_map/all_to_all | solution.py:737
  52.8 0.8 %copy.9 = f32[2,24,24,128]{3,2,1,0:T(8,128)} copy(f32[2,24,24,128]{3,2,1,0:T(8,128)S(1)} %get-tuple-element.45.field) | data formatting | bytes 1179648
  53.6 0.8 %copy.10 = f32[2,24,24,128]{3,2,1,0:T(8,128)} copy(f32[2,24,24,128]{3,2,1,0:T(8,128)S(1)} %get-tuple-element.46) | data formatting | bytes 1179648
  54.4 11.3 %all-to-all-done = f32[256,1,128]{2,1,0:T(1,128)S(1)} async-done(((f32[256,1,128]{2,1,0:T(1,128)}), f32[256,1,128]{2,1,0:T(1,128)S(1)}, u32[]{:S(2)}, u32[]{:S(2)}) %all-to-all-start) | async-done | bytes 131104 | tf_op jit(solution)/shard_map/all_to_all | solution.py:737
  65.7 0.3 reduce_sum.9
  (11 shorter events, 0.2 us)
Async XLA Ops:
  0.6 9.4 %copy-start = (f32[2,24,24,128]{3,2,1,0:T(8,128)S(1)}, f32[2,24,24,128]{3,2,1,0:T(8,128)}, u32[]{:S(2)}) copy-start(f32[2,24,24,128]{3,2,1,0:T(8,128)} %iterate.7) | copy-start | bytes 1769476
  0.6 9.4 %copy-start.1 = (f32[2,24,24,128]{3,2,1,0:T(8,128)S(1)}, f32[2,24,24,128]{3,2,1,0:T(8,128)}, u32[]{:S(2)}) copy-start(f32[2,24,24,128]{3,2,1,0:T(8,128)} %source.7) | copy-start | bytes 1769476
  0.7 9.4 %copy-start.2 = (f32[24,24,128]{2,1,0:T(8,128)S(1)}, f32[24,24,128]{2,1,0:T(8,128)}, u32[]{:S(2)}) copy-start(f32[24,24,128]{2,1,0:T(8,128)} %wave.7) | copy-start | bytes 884740
  2.1 16.6 %collective-permute-start = (f32[17,24,128]{2,1,0:T(8,128)S(1)}, f32[17,24,128]{2,1,0:T(8,128)S(1)}, u32[]{:S(2)}, u32[]{:S(2)}) collective-permute-start(f32[17,24,128]{2,1,0:T(8,128)S(1)} %get-tuple-element.24), channel_id=1, source_target_pairs={{0,16},{16,32},{32,48},{48,64},{64,80},{80,96},{96,112},{112,128},... | collective-permute-start | bytes 626696 | tf_op jit(solution)/shard_map/ppermute | solution.py:616
  4.3 14.4 %collective-permute-start.1 = (f32[408,128]{1,0:T(8,128)S(1)}, f32[408,128]{1,0:T(8,128)S(1)}, u32[]{:S(2)}, u32[]{:S(2)}) collective-permute-start(f32[408,128]{1,0:T(8,128)S(1)} %get-tuple-element.25), channel_id=1, source_target_pairs={{0,2},{2,4},{4,6},{6,8},{8,10},{10,12},{12,14},{14,0},{1,3},{3,5},... | collective-permute-start | bytes 626696 | tf_op jit(solution)/shard_map/ppermute | solution.py:616
  5.9 12.7 %collective-permute-start.2 = (f32[72,128]{1,0:T(8,128)S(1)}, f32[72,128]{1,0:T(8,128)S(1)}, u32[]{:S(2)}, u32[]{:S(2)}) collective-permute-start(f32[72,128]{1,0:T(8,128)S(1)} %get-tuple-element.26), channel_id=1, source_target_pairs={{0,18},{2,20},{4,22},{6,24},{8,26},{10,28},{12,30},{14,16},{16,34}... | collective-permute-start | bytes 110600 | tf_op jit(solution)/shard_map/ppermute | solution.py:635
  19.5 2.9 %collective-permute-start.3 = (f32[5,4,32,128]{3,2,1,0:T(8,128)S(1)}, f32[5,4,32,128]{3,2,1,0:T(8,128)S(1)}, u32[]{:S(2)}, u32[]{:S(2)}) collective-permute-start(f32[5,4,32,128]{3,2,1,0:T(8,128)S(1)} %pack_halo.1), channel_id=1, source_target_pairs={{0,1},{1,0},{2,3},{3,2},{4,5},{5,4},{6,7},{7,6},{8,9},{9,8},{10,11... | collective-permute-start | bytes 983048 | tf_op jit(solution)/shard_map/ppermute | solution.py:639
  23.1 7.7 %collective-permute-start.4 = (f32[56,128]{1,0:T(8,128)S(1)}, f32[56,128]{1,0:T(8,128)S(1)}, u32[]{:S(2)}, u32[]{:S(2)}) collective-permute-start(f32[56,128]{1,0:T(8,128)S(1)} %get-tuple-element.37), channel_id=1, source_target_pairs={{0,16},{16,0},{32,48},{48,32},{64,80},{80,64},{96,112},{112,96},{1... | collective-permute-start | bytes 86024 | tf_op jit(solution)/shard_map/ppermute | solution.py:625
  29.5 6.0 %collective-permute-start.5 = (f32[56,128]{1,0:T(8,128)S(1)}, f32[56,128]{1,0:T(8,128)S(1)}, u32[]{:S(2)}, u32[]{:S(2)}) collective-permute-start(f32[56,128]{1,0:T(8,128)S(1)} %get-tuple-element.38), channel_id=1, source_target_pairs={{16,32},{32,16},{48,64},{64,48},{80,96},{96,80},{112,128},{128,112... | collective-permute-start | bytes 86024 | tf_op jit(solution)/shard_map/ppermute | solution.py:625
  36.2 2.8 %collective-permute-start.6 = (f32[2,32,128]{2,1,0:T(8,128)S(1)}, f32[2,32,128]{2,1,0:T(8,128)S(1)}, u32[]{:S(2)}, u32[]{:S(2)}) collective-permute-start(f32[2,32,128]{2,1,0:T(8,128)S(1)} %get-tuple-element.41), channel_id=1, source_target_pairs={{0,2},{2,0},{4,6},{6,4},{8,10},{10,8},{12,14},{14,12},{1,3},{3,1},... | collective-permute-start | bytes 98312 | tf_op jit(solution)/shard_map/ppermute | solution.py:625
  36.3 4.1 %collective-permute-start.7 = (f32[2,32,128]{2,1,0:T(8,128)S(1)}, f32[2,32,128]{2,1,0:T(8,128)S(1)}, u32[]{:S(2)}, u32[]{:S(2)}) collective-permute-start(f32[2,32,128]{2,1,0:T(8,128)S(1)} %get-tuple-element.42), channel_id=1, source_target_pairs={{2,4},{4,2},{6,8},{8,6},{10,12},{12,10},{14,0},{0,14},{3,5},{5,3},... | collective-permute-start | bytes 98312 | tf_op jit(solution)/shard_map/ppermute | solution.py:625
  42.3 23.4 %all-to-all-start = ((f32[256,1,128]{2,1,0:T(1,128)}), f32[256,1,128]{2,1,0:T(1,128)S(1)}, u32[]{:S(2)}, u32[]{:S(2)}) async-start(f32[256,1,128]{2,1,0:T(1,128)} %bitcast.13), calls=%async_computation | async-start | bytes 262144 | tf_op jit(solution)/shard_map/all_to_all | solution.py:737
